TPU v7x, 256 devices: a whole 4x4x8 slice. The times are simulated.
256 devices in a mesh: blk: 128 (over y, x_hi, z, core), rhs: 2 (over x_lo).
Axes of the slice: x: 4 (x_hi: 2, x_lo: 2; x = x_hi * 2 + x_lo), y: 4, z: 8, core: 2. Of those that a mesh axis runs over, the one named last changes fastest.
Arguments:
- directions: bfloat16 [262144, 256], P('blk', 'rhs'), may hold values from -6 to 6
- axial_pos: bfloat16 [262144], P('blk'), may hold values from 0 to 8
- azimuth: bfloat16 [262144], P('blk'), may hold values from -3.140625 to 3.140625
- panel_area: bfloat16 [262144], P('blk'), may hold values from 0.5 to 2
Outputs:
- product: float32 [262144, 256], P('blk', 'rhs')
- gram: float32 [256, 256], P(None, 'rhs')
All inputs are finite; a program needn't handle non-finite values.
Results may differ from a plain program's by a relative error of at most 0.0029.
Values may be sent and summed in bfloat16 or wider, within the bound.
No kernel may reach another device: no remote copies, remote signals or barrier semaphores. Data moves between devices by JAX's collectives and lax.ppermute only.
A program may use at most 64 MiB of HBM per device.

v0:
```python
import functools

import jax
import jax.numpy as jnp
from jax import lax
from jax.experimental import pallas as pl
from jax.experimental.pallas import tpu as pltpu
from jax.sharding import Mesh, PartitionSpec as P

LANES = 128
VMEM_BYTES = 12 * 2**20
ROW_STEP = 256
COL_STEP = 1024
PIECES = 4
BLK = ("y", "xh", "z", "core")


def split_parts(base):
    high = base.astype(jnp.bfloat16).astype(jnp.float32)
    rest = base - high
    mid = rest.astype(jnp.bfloat16).astype(jnp.float32)
    low = (rest - mid).astype(jnp.bfloat16).astype(jnp.float32)
    return high, mid, low


def point_values(axial, angle, area):
    axial = axial.astype(jnp.float32) - 4.0
    angle = angle.astype(jnp.float32)
    area = area.astype(jnp.float32)
    cos, sin = jnp.cos(angle), jnp.sin(angle)
    return axial, cos, sin, axial * axial + cos * cos + sin * sin, 1.0 / (area * area)


def lay_rows(base_ref, features):
    groups = features[0].shape[0]
    base_ref[...] = jnp.zeros_like(base_ref)
    for row, feature in enumerate(features):
        for group in range(groups):
            base_ref[row : row + 1, group * LANES : (group + 1) * LANES] = feature[group : group + 1, :]


def column_factors(geometry, base_ref, col_ref):
    axial, cos, sin, norm, scale = point_values(*geometry)
    lay_rows(base_ref, (scale, norm * scale, axial * scale, cos * scale, sin * scale))
    high, mid, low = split_parts(base_ref[...])
    col_ref[...] = jnp.concatenate([high, high, high, mid, mid, low], axis=0).astype(jnp.bfloat16)


def row_factors(geometry, base_ref, row_ref):
    axial, cos, sin, norm, scale = point_values(*geometry)
    count = base_ref.shape[1]
    scale = scale * count
    double = -2.0 * scale
    lay_rows(base_ref, ((norm + 0.01) * scale, scale, axial * double, cos * double, sin * double))
    high, mid, low = split_parts(base_ref[...])
    stacked = jnp.concatenate([high, mid, low, high, mid, high], axis=0)
    for group in range(count // LANES):
        part = stacked[:, group * LANES : (group + 1) * LANES]
        row_ref[group * LANES : (group + 1) * LANES, :] = part.T.astype(jnp.bfloat16)


def tile_product(row_ref, col_ref, message_ref, offset, out_ref):
    height, width = row_ref.shape[0], col_ref.shape[1]
    step_cols = min(COL_STEP, width)

    def step_fn(step, carried):
        start = pl.multiple_of(step * step_cols, step_cols)
        factor = col_ref[:, pl.ds(start, step_cols)]
        directions = message_ref[pl.ds(offset + start, step_cols), :]
        for low in range(0, height, ROW_STEP):
            rows = slice(low, low + ROW_STEP)
            inverse = jnp.dot(row_ref[rows, :], factor, preferred_element_type=jnp.float32)
            values = lax.rsqrt(inverse).astype(jnp.bfloat16)
            out_ref[rows, :] += jnp.dot(values, directions, preferred_element_type=jnp.float32)
        return carried

    lax.fori_loop(0, width // step_cols, step_fn, 0)


def message_geometry(message_ref, count, offset=0, width=None):
    groups = count // LANES
    part = slice(offset // LANES, (offset + (width or count)) // LANES)
    values = (message_ref[count + k * groups : count + (k + 1) * groups, :] for k in range(3))
    return tuple(value.astype(jnp.float32)[part] for value in values)


def home_body(message_ref, out_ref, row_ref, base_ref, col_ref):
    geometry = message_geometry(message_ref, row_ref.shape[0])
    row_factors(geometry, base_ref, row_ref)
    column_factors(geometry, base_ref, col_ref)
    out_ref[...] = jnp.zeros_like(out_ref)
    tile_product(row_ref, col_ref, message_ref, 0, out_ref)


def guest_body(offset, row_ref, message_ref, *refs):
    *total_refs, out_ref, base_ref, col_ref = refs
    column_factors(
        message_geometry(message_ref, row_ref.shape[0], offset, col_ref.shape[1]), base_ref, col_ref
    )
    if total_refs:
        if len(total_refs) > 1:
            out_ref[...] = total_refs[0][...] + total_refs[1][...]
    else:
        out_ref[...] = jnp.zeros_like(out_ref)
    tile_product(row_ref, col_ref, message_ref, offset, out_ref)


def tile_scratch(width):
    return [pltpu.VMEM((8, width), jnp.float32), pltpu.VMEM((48, width), jnp.bfloat16)]


def tile_cost(count):
    return pl.CostEstimate(flops=count * count * 128, bytes_accessed=0, transcendentals=0)


def near(value):
    return pltpu.with_memory_space_constraint(value, pltpu.VMEM)


def home_tile(message, count):
    vmem = pl.BlockSpec(memory_space=pltpu.VMEM)
    return pl.pallas_call(
        home_body,
        out_shape=[pltpu.VMEM((count, LANES), jnp.float32), pltpu.VMEM((count, 48), jnp.bfloat16)],
        in_specs=[vmem],
        out_specs=[vmem, vmem],
        scratch_shapes=tile_scratch(count),
        cost_estimate=tile_cost(count),
        compiler_params=pltpu.CompilerParams(vmem_limit_bytes=VMEM_BYTES),
        name="home_tile",
    )(near(message))


def guest_tile(rows, message, totals, piece=0, pieces=1):
    count = rows.shape[0]
    width = count // pieces
    vmem = pl.BlockSpec(memory_space=pltpu.VMEM)
    operands = [near(value) for value in (rows, message, *totals)]
    return pl.pallas_call(
        functools.partial(guest_body, piece * width),
        out_shape=pltpu.VMEM((count, LANES), jnp.float32),
        in_specs=[vmem] * len(operands),
        out_specs=vmem,
        input_output_aliases={2: 0} if totals else {},
        scratch_shapes=tile_scratch(width),
        cost_estimate=tile_cost(count),
        compiler_params=pltpu.CompilerParams(vmem_limit_bytes=VMEM_BYTES),
        name="guest_tile",
    )(*operands)


def half_gram_body(own_ref, pair_ref, first_ref, second_ref, out_ref):
    value = 0.5 * first_ref[...] + second_ref[...]
    high = value.astype(jnp.bfloat16)
    low = (value - high.astype(jnp.float32)).astype(jnp.bfloat16)
    both = jnp.concatenate([high, low], axis=1)
    for k, ref in enumerate((own_ref, pair_ref)):
        part = lax.dot_general(
            ref[: value.shape[0], :], both, (((0,), (0,)), ((), ())), preferred_element_type=jnp.float32
        )
        out_ref[k] = part[:, :LANES] + part[:, LANES:]


def half_gram(own, pair, first, second):
    vmem = pl.BlockSpec(memory_space=pltpu.VMEM)
    return pl.pallas_call(
        half_gram_body,
        out_shape=jax.ShapeDtypeStruct((2, LANES, LANES), jnp.float32),
        in_specs=[vmem] * 4,
        out_specs=vmem,
        cost_estimate=pl.CostEstimate(flops=2 * 2048 * 256 * 256, bytes_accessed=3 * 2**20, transcendentals=0),
        compiler_params=pltpu.CompilerParams(vmem_limit_bytes=VMEM_BYTES),
        name="half_gram",
    )(near(own), near(pair), near(first), near(second))


def along_blk(value, sizes, target):
    ny, nx, nz, nc = sizes

    def index(y, x, z, c):
        return ((y % ny * nx + x % nx) * nz + z % nz) * nc + c % nc

    pairs = []
    for y in range(ny):
        for x in range(nx):
            for z in range(nz):
                for c in range(nc):
                    pairs.append((index(y, x, z, c), index(*target(y, x, z, c))))
    return lax.ppermute(value, BLK, pairs)


def from_neighbour(value, parity):
    count = lax.axis_size(BLK)
    pairs = []
    for block in range(count):
        chip, core = divmod(block, 2)
        first = chip % 2 == parity
        other = 2 * (chip + 1) + 1 - core if first else 2 * (chip - 1) + core
        pairs.append((block, other % count))
    return lax.ppermute(value, BLK, pairs)


def from_far(value):
    count = lax.axis_size(BLK)
    return lax.ppermute(
        value, BLK, [(b, (b - 3 if b % 2 == 0 else b + 3) % count) for b in range(count)]
    )


def core_swap(value):
    return lax.ppermute(value, "core", [(0, 1), (1, 0)])


def shards(sizes, directions, axial_pos, azimuth, panel_area):
    count = axial_pos.shape[0]
    geometry = [part.reshape(count // LANES, LANES) for part in (axial_pos, azimuth, panel_area)]
    message = jnp.concatenate([directions] + geometry, axis=0)
    other = core_swap(message)
    even = from_neighbour(message, 0)
    odd = from_neighbour(message, 1)

    first, rows = home_tile(message, count)
    first, late = lax.optimization_barrier((first, message))
    far = from_far(late)
    first = guest_tile(rows, other, (first,))
    first, even, later = lax.optimization_barrier((first, even, directions))
    pair = lax.ppermute(later, "rhs", [(0, 1), (1, 0)])
    even_other = core_swap(even)
    second = guest_tile(rows, even, ())
    second, odd = lax.optimization_barrier((second, odd))
    odd_other = core_swap(odd)
    second = guest_tile(rows, odd, (second,))
    second, far = lax.optimization_barrier((second, far))
    first = guest_tile(rows, far, (first,))
    half = half_gram(message, pair, first, second)

    core = lax.axis_index("core")
    keep = lax.dynamic_index_in_dim(half, core, 0, keepdims=False)
    value = keep + core_swap(lax.dynamic_index_in_dim(half, 1 - core, 0, keepdims=False))

    value, first, second = lax.optimization_barrier((value, first, second))
    crossed = lax.ppermute(value, ("core", "rhs"), [(2, 3), (3, 2)])
    product = guest_tile(rows, even_other, (first, second), 0, PIECES)
    value, crossed, product = lax.optimization_barrier((value, crossed, product))
    value = value + jnp.where(core == 0, value, crossed).T

    work = [(even_other, piece) for piece in range(1, PIECES)] + [(odd_other, piece) for piece in range(PIECES)]
    stages = (
        ((0, 0, 4), 2), ((0, 0, 2), 1), ((0, 0, 1), 1), ((2, 0, 0), 1), ((1, 0, 0), 1), ((0, 1, 0), 1),
    )
    for move, pieces in stages:
        value, product = lax.optimization_barrier((value, product))
        moved = along_blk(
            value, sizes, lambda y, x, z, c, d=move: (y + d[0], x + d[1], z + d[2], c)
        )
        for _ in range(pieces):
            guest, piece = work.pop(0)
            product = guest_tile(rows, guest, (product,), piece, PIECES)
        value, product, moved = lax.optimization_barrier((value, product, moved))
        value = value + moved
    value = value / (count * lax.axis_size(BLK))
    swapped = core_swap(value)
    upper = core == lax.axis_index("rhs")
    gram = jnp.concatenate([jnp.where(upper, value, swapped), jnp.where(upper, swapped, value)], axis=0)
    return product, gram


def solution(mesh):
    sizes = (4, 2, 8, 2)
    fine = Mesh(mesh.devices.reshape(sizes + (2,)), BLK + ("rhs",))
    in_specs = (P(BLK, "rhs"), P(BLK), P(BLK), P(BLK))
    out_specs = (P(BLK, "rhs"), P(None, "rhs"))
    return jax.shard_map(
        functools.partial(shards, sizes), mesh=fine, in_specs=in_specs, out_specs=out_specs, check_vma=False
    )
```

profile of v0, /device:TPU:1, one launch (start us, length us, event | category | flops | bytes accessed | tf_op | source)
XLA Modules:
  0.0 96.0 jit_solution(10678097342129705139)
XLA Ops:
  0.6 1.9 %pad_maximum_fusion.message_ref.own_ref = bf16[2096,128]{1,0:T(8,128)(2,1)} fusion(bf16[16,128]{1,0:T(8,128)(2,1)} %bitcast.9, bf16[16,128]{1,0:T(8,128)(2,1)} %bitcast.10, bf16[16,128]{1,0:T(8,128)(2,1)} %bitcast.11, bf16[2048,128]{1,0:T(8,128)(2,1)} %param.4), kind=kLoop, calls=%fused_computation | loop fusion | flops 2146304 | bytes 1073152 | tf_op jit(solution)/shard_map/concatenate | solution.py:217
  2.6 3.2 %collective-permute-start = (bf16[2096,128]{1,0:T(8,128)(2,1)}, bf16[2096,128]{1,0:T(8,128)(2,1)S(1)}, u32[]{:S(2)}, u32[]{:S(2)}) collective-permute-start(bf16[2096,128]{1,0:T(8,128)(2,1)} %pad_maximum_fusion.message_ref.own_ref), channel_id=1, source_target_pairs={{0,2},{2,0},{1,3},{3,1},{4,6},{6,4},{5,7},{7,5},{8,10},{10,8},{9,1... | collective-permute-start | bytes 1609736 | tf_op jit(solution)/shard_map/ppermute | solution.py:211
  5.8 9.5 %collective-permute-start.3 = (bf16[2096,128]{1,0:T(8,128)(2,1)}, bf16[2096,128]{1,0:T(8,128)(2,1)}, u32[]{:S(2)}, u32[]{:S(2)}) collective-permute-start(bf16[2096,128]{1,0:T(8,128)(2,1)} %pad_maximum_fusion.message_ref.own_ref), channel_id=1, source_target_pairs={{0,252},{2,254},{4,10},{6,8},{8,4},{10,6},{12,18},{14,16},{16,12},... | collective-permute-start | bytes 1609736 | tf_op jit(solution)/shard_map/ppermute | solution.py:200
  15.3 6.1 %home_tile.1 = (f32[2048,128]{1,0:T(8,128)S(1)}, bf16[2048,48]{1,0:T(8,128)(2,1)S(1)}) custom-call(bf16[2096,128]{1,0:T(8,128)(2,1)} %pad_maximum_fusion.message_ref.own_ref), custom_call_target="tpu_custom_call" | custom-call | flops 536870912 | tf_op jit(solution)/shard_map/home_tile/pallas_call | solution.py:122
  21.4 4.7 %guest_tile.12.refs_0_ = f32[2048,128]{1,0:T(8,128)S(1)} custom-call(bf16[2048,48]{1,0:T(8,128)(2,1)S(1)} %get-tuple-element.49.row_ref, bf16[2096,128]{1,0:T(8,128)(2,1)S(1)} %collective-permute-done.message_ref, f32[2048,128]{1,0:T(8,128)S(1)} %get-tuple-element.51.refs_0_), custom_call_target="tpu_custom_call", output_to_operand_aliasing={{}: (2, {})} | custom-call | flops 536870912 | tf_op jit(solution)/shard_map/guest_tile/pallas_call | solution.py:139
  26.6 1.8 %collective-permute-start.7 = (bf16[2096,128]{1,0:T(8,128)(2,1)}, bf16[2096,128]{1,0:T(8,128)(2,1)S(1)}, u32[]{:S(2)}, u32[]{:S(2)}) collective-permute-start(bf16[2096,128]{1,0:T(8,128)(2,1)} %collective-permute-done.1.message_ref), channel_id=1, source_target_pairs={{0,2},{2,0},{1,3},{3,1},{4,6},{6,4},{5,7},{7,5},{8,10},{10,8},{9,1... | collective-permute-start | bytes 1609736 | tf_op jit(solution)/shard_map/ppermute | solution.py:211
  28.4 5.8 %guest_tile.13.refs_0_ = f32[2048,128]{1,0:T(8,128)S(1)} custom-call(bf16[2048,48]{1,0:T(8,128)(2,1)S(1)} %get-tuple-element.49.row_ref, bf16[2096,128]{1,0:T(8,128)(2,1)} %collective-permute-done.1.message_ref), custom_call_target="tpu_custom_call" | custom-call | flops 536870912 | tf_op jit(solution)/shard_map/guest_tile/pallas_call | solution.py:139
  34.3 5.8 %guest_tile.14.second_ref.refs_1_ = f32[2048,128]{1,0:T(8,128)S(1)} custom-call(bf16[2048,48]{1,0:T(8,128)(2,1)S(1)} %get-tuple-element.49.row_ref, bf16[2096,128]{1,0:T(8,128)(2,1)} %collective-permute-done.3.message_ref, f32[2048,128]{1,0:T(8,128)S(1)} %guest_tile.13.refs_0_), custom_call_target="tpu_custom_call", output_to_operand_aliasing={{}: (2, {})} | custom-call | flops 536870912 | tf_op jit(solution)/shard_map/guest_tile/pallas_call | solution.py:139
  40.0 5.8 %guest_tile.15.first_ref.refs_0_ = f32[2048,128]{1,0:T(8,128)S(1)} custom-call(bf16[2048,48]{1,0:T(8,128)(2,1)S(1)} %get-tuple-element.49.row_ref, bf16[2096,128]{1,0:T(8,128)(2,1)} %collective-permute-done.4.message_ref, f32[2048,128]{1,0:T(8,128)S(1)} %guest_tile.12.refs_0_), custom_call_target="tpu_custom_call", output_to_operand_aliasing={{}: (2, {})} | custom-call | flops 536870912 | tf_op jit(solution)/shard_map/guest_tile/pallas_call | solution.py:139
  45.8 1.7 %half_gram.1 = f32[2,128,128]{2,1,0:T(8,128)S(1)} custom-call(bf16[2096,128]{1,0:T(8,128)(2,1)} %pad_maximum_fusion.message_ref.own_ref, bf16[2048,128]{1,0:T(8,128)(2,1)} %collective-permute-done.2.pair_ref, f32[2048,128]{1,0:T(8,128)S(1)} %guest_tile.15.first_ref.refs_0_, f32[2048,128]{1,0:T(8,128)S(1)} %guest_tile.14.second_ref.refs_1_), custom_call_target="tpu_custom_call" | custom-call | flops 268435456 | bytes 3145728 | tf_op jit(solution)/shard_map/half_gram/pallas_call | solution.py:166
  47.5 3.6 %collective-permute-start.5 = (f32[128,128]{1,0:T(8,128)S(1)}, f32[128,128]{1,0:T(8,128)S(1)}, u32[]{:S(2)}, u32[]{:S(2)}) collective-permute-start(f32[128,128]{1,0:T(8,128)S(1)} %dynamic-slice_bitcast_fusion), channel_id=1, source_target_pairs={{0,2},{2,0},{1,3},{3,1},{4,6},{6,4},{5,7},{7,5},{8,10},{10,8},{9,1... | collective-permute-start | bytes 196616 | tf_op jit(solution)/shard_map/ppermute | solution.py:211
  52.2 2.2 %collective-permute-start.6 = (f32[128,128]{0,1:T(8,128)S(1)}, f32[128,128]{0,1:T(8,128)S(1)}, u32[]{:S(2)}, u32[]{:S(2)}) collective-permute-start(f32[128,128]{0,1:T(8,128)S(1)} %copy.18), channel_id=1, source_target_pairs={{2,3},{3,2},{6,7},{7,6},{10,11},{11,10},{14,15},{15,14},{18,19},{1... | collective-permute-start | bytes 196616 | tf_op jit(solution)/shard_map/ppermute | solution.py:242
  54.4 2.0 %guest_tile.16.refs_0_ = f32[2048,128]{1,0:T(8,128)S(1)} custom-call(bf16[2048,48]{1,0:T(8,128)(2,1)S(1)} %get-tuple-element.49.row_ref, bf16[2096,128]{1,0:T(8,128)(2,1)S(1)} %collective-permute-done.7.message_ref, f32[2048,128]{1,0:T(8,128)S(1)} %guest_tile.15.first_ref.refs_0_, ...), custom_call_target="tpu_custom_call", output_to_operand_aliasing={{}: (2, {})} | custom-call | flops 536870912 | tf_op jit(solution)/shard_map/guest_tile/pallas_call | solution.py:139
  57.6 1.9 %guest_tile.17.refs_0_ = f32[2048,128]{1,0:T(8,128)S(1)} custom-call(bf16[2048,48]{1,0:T(8,128)(2,1)S(1)} %get-tuple-element.49.row_ref, bf16[2096,128]{1,0:T(8,128)(2,1)S(1)} %collective-permute-done.7.message_ref, f32[2048,128]{1,0:T(8,128)S(1)} %guest_tile.16.refs_0_), custom_call_target="tpu_custom_call", output_to_operand_aliasing={{}: (2, {})} | custom-call | flops 536870912 | tf_op jit(solution)/shard_map/guest_tile/pallas_call | solution.py:139
  59.6 1.9 %guest_tile.18.refs_0_ = f32[2048,128]{1,0:T(8,128)S(1)} custom-call(bf16[2048,48]{1,0:T(8,128)(2,1)S(1)} %get-tuple-element.49.row_ref, bf16[2096,128]{1,0:T(8,128)(2,1)S(1)} %collective-permute-done.7.message_ref, f32[2048,128]{1,0:T(8,128)S(1)} %guest_tile.17.refs_0_), custom_call_target="tpu_custom_call", output_to_operand_aliasing={{}: (2, {})} | custom-call | flops 536870912 | tf_op jit(solution)/shard_map/guest_tile/pallas_call | solution.py:139
  61.5 3.1 %collective-permute-done.8 = f32[128,128]{1,0:T(8,128)S(1)} collective-permute-done((f32[128,128]{1,0:T(8,128)S(1)}, f32[128,128]{1,0:T(8,128)S(1)}, u32[]{:S(2)}, u32[]{:S(2)}) %collective-permute-start.8) | collective-permute-done | bytes 65568 | tf_op jit(solution)/shard_map/ppermute | solution.py:189
  64.7 1.9 %guest_tile.19.refs_0_ = f32[2048,128]{1,0:T(8,128)S(1)} custom-call(bf16[2048,48]{1,0:T(8,128)(2,1)S(1)} %get-tuple-element.49.row_ref, bf16[2096,128]{1,0:T(8,128)(2,1)S(1)} %collective-permute-done.7.message_ref, f32[2048,128]{1,0:T(8,128)S(1)} %guest_tile.18.refs_0_), custom_call_target="tpu_custom_call", output_to_operand_aliasing={{}: (2, {})} | custom-call | flops 536870912 | tf_op jit(solution)/shard_map/guest_tile/pallas_call | solution.py:139
  66.7 4.3 %collective-permute-done.9 = f32[128,128]{1,0:T(8,128)S(1)} collective-permute-done((f32[128,128]{1,0:T(8,128)S(1)}, f32[128,128]{1,0:T(8,128)S(1)}, u32[]{:S(2)}, u32[]{:S(2)}) %collective-permute-start.9) | collective-permute-done | bytes 65568 | tf_op jit(solution)/shard_map/ppermute | solution.py:189
  71.1 3.0 %guest_tile.20.refs_0_ = f32[2048,128]{1,0:T(8,128)S(1)} custom-call(bf16[2048,48]{1,0:T(8,128)(2,1)S(1)} %get-tuple-element.49.row_ref, bf16[2096,128]{1,0:T(8,128)(2,1)} %collective-permute-done.10.message_ref, f32[2048,128]{1,0:T(8,128)S(1)} %guest_tile.19.refs_0_), custom_call_target="tpu_custom_call", output_to_operand_aliasing={{}: (2, {})} | custom-call | flops 536870912 | tf_op jit(solution)/shard_map/guest_tile/pallas_call | solution.py:139
  75.5 3.0 %guest_tile.21.refs_0_ = f32[2048,128]{1,0:T(8,128)S(1)} custom-call(bf16[2048,48]{1,0:T(8,128)(2,1)S(1)} %get-tuple-element.49.row_ref, bf16[2096,128]{1,0:T(8,128)(2,1)} %collective-permute-done.10.message_ref, f32[2048,128]{1,0:T(8,128)S(1)} %guest_tile.20.refs_0_), custom_call_target="tpu_custom_call", output_to_operand_aliasing={{}: (2, {})} | custom-call | flops 536870912 | tf_op jit(solution)/shard_map/guest_tile/pallas_call | solution.py:139
  80.2 3.0 %guest_tile.22.refs_0_ = f32[2048,128]{1,0:T(8,128)S(1)} custom-call(bf16[2048,48]{1,0:T(8,128)(2,1)S(1)} %get-tuple-element.49.row_ref, bf16[2096,128]{1,0:T(8,128)(2,1)} %collective-permute-done.10.message_ref, f32[2048,128]{1,0:T(8,128)S(1)} %guest_tile.21.refs_0_), custom_call_target="tpu_custom_call", output_to_operand_aliasing={{}: (2, {})} | custom-call | flops 536870912 | tf_op jit(solution)/shard_map/guest_tile/pallas_call | solution.py:139
  84.6 3.0 %guest_tile.23 = f32[2048,128]{1,0:T(8,128)S(1)} custom-call(bf16[2048,48]{1,0:T(8,128)(2,1)S(1)} %get-tuple-element.49.row_ref, bf16[2096,128]{1,0:T(8,128)(2,1)} %collective-permute-done.10.message_ref, f32[2048,128]{1,0:T(8,128)S(1)} %guest_tile.22.refs_0_), custom_call_target="tpu_custom_call", output_to_operand_aliasing={{}: (2, {})} | custom-call | flops 536870912 | tf_op jit(solution)/shard_map/guest_tile/pallas_call | solution.py:139
  87.6 1.6 %collective-permute-done.14 = f32[128,128]{1,0:T(8,128)S(1)} collective-permute-done((f32[128,128]{1,0:T(8,128)S(1)}, f32[128,128]{1,0:T(8,128)S(1)}, u32[]{:S(2)}, u32[]{:S(2)}) %collective-permute-start.14) | collective-permute-done | bytes 65568 | tf_op jit(solution)/shard_map/ppermute | solution.py:189
  89.3 5.1 %collective-permute-start.15 = (f32[128,128]{1,0:T(8,128)S(1)}, f32[128,128]{1,0:T(8,128)S(1)}, u32[]{:S(2)}, u32[]{:S(2)}) collective-permute-start(f32[128,128]{1,0:T(8,128)S(1)} %add_multiply_fusion), channel_id=1, source_target_pairs={{0,2},{2,0},{1,3},{3,1},{4,6},{6,4},{5,7},{7,5},{8,10},{10,8},{9,1... | collective-permute-start | bytes 196616 | tf_op jit(solution)/shard_map/ppermute | solution.py:211
  (37 shorter events, 9.1 us)
Async XLA Ops:
  2.6 18.9 %collective-permute-start = (bf16[2096,128]{1,0:T(8,128)(2,1)}, bf16[2096,128]{1,0:T(8,128)(2,1)S(1)}, u32[]{:S(2)}, u32[]{:S(2)}) collective-permute-start(bf16[2096,128]{1,0:T(8,128)(2,1)} %pad_maximum_fusion.message_ref.own_ref), channel_id=1, source_target_pairs={{0,2},{2,0},{1,3},{3,1},{4,6},{6,4},{5,7},{7,5},{8,10},{10,8},{9,1... | collective-permute-start | bytes 1609736 | tf_op jit(solution)/shard_map/ppermute | solution.py:211
  5.8 20.4 %collective-permute-start.1 = (bf16[2096,128]{1,0:T(8,128)(2,1)}, bf16[2096,128]{1,0:T(8,128)(2,1)}, u32[]{:S(2)}, u32[]{:S(2)}) collective-permute-start(bf16[2096,128]{1,0:T(8,128)(2,1)} %pad_maximum_fusion.message_ref.own_ref), channel_id=1, source_target_pairs={{0,6},{2,4},{4,0},{6,2},{8,14},{10,12},{12,8},{14,10},{16,22},{18,... | collective-permute-start | bytes 1609736 | tf_op jit(solution)/shard_map/ppermute | solution.py:200
  5.8 28.5 %collective-permute-start.3 = (bf16[2096,128]{1,0:T(8,128)(2,1)}, bf16[2096,128]{1,0:T(8,128)(2,1)}, u32[]{:S(2)}, u32[]{:S(2)}) collective-permute-start(bf16[2096,128]{1,0:T(8,128)(2,1)} %pad_maximum_fusion.message_ref.own_ref), channel_id=1, source_target_pairs={{0,252},{2,254},{4,10},{6,8},{8,4},{10,6},{12,18},{14,16},{16,12},... | collective-permute-start | bytes 1609736 | tf_op jit(solution)/shard_map/ppermute | solution.py:200
  21.3 18.7 %collective-permute-start.4 = (bf16[2096,128]{1,0:T(8,128)(2,1)}, bf16[2096,128]{1,0:T(8,128)(2,1)}, u32[]{:S(2)}, u32[]{:S(2)}) collective-permute-start(bf16[2096,128]{1,0:T(8,128)(2,1)} %pad_maximum_fusion.message_ref.own_ref), channel_id=1, source_target_pairs={{0,250},{2,8},{4,254},{6,12},{8,2},{10,16},{12,6},{14,20},{16,10},... | collective-permute-start | bytes 1609736 | tf_op jit(solution)/shard_map/ppermute | solution.py:205
  26.2 19.6 %collective-permute-start.2 = (bf16[2048,128]{1,0:T(8,128)(2,1)}, bf16[2048,128]{1,0:T(8,128)(2,1)}, u32[]{:S(2)}, u32[]{:S(2)}) collective-permute-start(bf16[2048,128]{1,0:T(8,128)(2,1)} %param.4), channel_id=1, source_target_pairs={{0,1},{1,0},{2,3},{3,2},{4,5},{5,4},{6,7},{7,6},{8,9},{9,8},{10,11... | collective-permute-start | bytes 1572872 | tf_op jit(solution)/shard_map/ppermute | solution.py:227
  26.6 27.8 %collective-permute-start.7 = (bf16[2096,128]{1,0:T(8,128)(2,1)}, bf16[2096,128]{1,0:T(8,128)(2,1)S(1)}, u32[]{:S(2)}, u32[]{:S(2)}) collective-permute-start(bf16[2096,128]{1,0:T(8,128)(2,1)} %collective-permute-done.1.message_ref), channel_id=1, source_target_pairs={{0,2},{2,0},{1,3},{3,1},{4,6},{6,4},{5,7},{7,5},{8,10},{10,8},{9,1... | collective-permute-start | bytes 1609736 | tf_op jit(solution)/shard_map/ppermute | solution.py:211
  47.5 4.5 %collective-permute-start.5 = (f32[128,128]{1,0:T(8,128)S(1)}, f32[128,128]{1,0:T(8,128)S(1)}, u32[]{:S(2)}, u32[]{:S(2)}) collective-permute-start(f32[128,128]{1,0:T(8,128)S(1)} %dynamic-slice_bitcast_fusion), channel_id=1, source_target_pairs={{0,2},{2,0},{1,3},{3,1},{4,6},{6,4},{5,7},{7,5},{8,10},{10,8},{9,1... | collective-permute-start | bytes 196616 | tf_op jit(solution)/shard_map/ppermute | solution.py:211
  51.2 19.9 %collective-permute-start.10 = (bf16[2096,128]{1,0:T(8,128)(2,1)}, bf16[2096,128]{1,0:T(8,128)(2,1)}, u32[]{:S(2)}, u32[]{:S(2)}) collective-permute-start(bf16[2096,128]{1,0:T(8,128)(2,1)} %collective-permute-done.3.message_ref), channel_id=1, source_target_pairs={{0,2},{2,0},{1,3},{3,1},{4,6},{6,4},{5,7},{7,5},{8,10},{10,8},{9,1... | collective-permute-start | bytes 1609736 | tf_op jit(solution)/shard_map/ppermute | solution.py:211
  52.2 5.0 %collective-permute-start.6 = (f32[128,128]{0,1:T(8,128)S(1)}, f32[128,128]{0,1:T(8,128)S(1)}, u32[]{:S(2)}, u32[]{:S(2)}) collective-permute-start(f32[128,128]{0,1:T(8,128)S(1)} %copy.18), channel_id=1, source_target_pairs={{2,3},{3,2},{6,7},{7,6},{10,11},{11,10},{14,15},{15,14},{18,19},{1... | collective-permute-start | bytes 196616 | tf_op jit(solution)/shard_map/ppermute | solution.py:242
  57.3 7.3 %collective-permute-start.8 = (f32[128,128]{1,0:T(8,128)S(1)}, f32[128,128]{1,0:T(8,128)S(1)}, u32[]{:S(2)}, u32[]{:S(2)}) collective-permute-start(f32[128,128]{1,0:T(8,128)S(1)} %bitcast_add_fusion), channel_id=1, source_target_pairs={{0,16},{2,18},{4,20},{6,22},{8,24},{10,26},{12,28},{14,30},{16,0},... | collective-permute-start | bytes 196616 | tf_op jit(solution)/shard_map/ppermute | solution.py:189
  64.6 6.3 %collective-permute-start.9 = (f32[128,128]{1,0:T(8,128)S(1)}, f32[128,128]{1,0:T(8,128)S(1)}, u32[]{:S(2)}, u32[]{:S(2)}) collective-permute-start(f32[128,128]{1,0:T(8,128)S(1)} %add.36), channel_id=1, source_target_pairs={{0,8},{2,10},{4,12},{6,14},{8,16},{10,18},{12,20},{14,22},{16,24},... | collective-permute-start | bytes 196616 | tf_op jit(solution)/shard_map/ppermute | solution.py:189
  71.0 4.4 %collective-permute-start.11 = (f32[128,128]{1,0:T(8,128)S(1)}, f32[128,128]{1,0:T(8,128)S(1)}, u32[]{:S(2)}, u32[]{:S(2)}) collective-permute-start(f32[128,128]{1,0:T(8,128)S(1)} %add.37), channel_id=1, source_target_pairs={{0,4},{2,6},{4,8},{6,10},{8,12},{10,14},{12,16},{14,18},{16,20},{1... | collective-permute-start | bytes 196616 | tf_op jit(solution)/shard_map/ppermute | solution.py:189
  75.4 4.7 %collective-permute-start.12 = (f32[128,128]{1,0:T(8,128)S(1)}, f32[128,128]{1,0:T(8,128)S(1)}, u32[]{:S(2)}, u32[]{:S(2)}) collective-permute-start(f32[128,128]{1,0:T(8,128)S(1)} %add.38), channel_id=1, source_target_pairs={{0,128},{2,130},{4,132},{6,134},{8,136},{10,138},{12,140},{14,142}... | collective-permute-start | bytes 196616 | tf_op jit(solution)/shard_map/ppermute | solution.py:189
  80.1 4.4 %collective-permute-start.13 = (f32[128,128]{1,0:T(8,128)S(1)}, f32[128,128]{1,0:T(8,128)S(1)}, u32[]{:S(2)}, u32[]{:S(2)}) collective-permute-start(f32[128,128]{1,0:T(8,128)S(1)} %add.39), channel_id=1, source_target_pairs={{0,64},{2,66},{4,68},{6,70},{8,72},{10,74},{12,76},{14,78},{16,80}... | collective-permute-start | bytes 196616 | tf_op jit(solution)/shard_map/ppermute | solution.py:189
  84.5 4.7 %collective-permute-start.14 = (f32[128,128]{1,0:T(8,128)S(1)}, f32[128,128]{1,0:T(8,128)S(1)}, u32[]{:S(2)}, u32[]{:S(2)}) collective-permute-start(f32[128,128]{1,0:T(8,128)S(1)} %add.40), channel_id=1, source_target_pairs={{0,32},{2,34},{4,36},{6,38},{8,40},{10,42},{12,44},{14,46},{16,48}... | collective-permute-start | bytes 196616 | tf_op jit(solution)/shard_map/ppermute | solution.py:189
  89.3 6.1 %collective-permute-start.15 = (f32[128,128]{1,0:T(8,128)S(1)}, f32[128,128]{1,0:T(8,128)S(1)}, u32[]{:S(2)}, u32[]{:S(2)}) collective-permute-start(f32[128,128]{1,0:T(8,128)S(1)} %add_multiply_fusion), channel_id=1, source_target_pairs={{0,2},{2,0},{1,3},{3,1},{4,6},{6,4},{5,7},{7,5},{8,10},{10,8},{9,1... | collective-permute-start | bytes 196616 | tf_op jit(solution)/shard_map/ppermute | solution.py:211
where the time goes:
time: 96.5 us; the launch traced here: 96 us
  Pallas kernels  49.5 us (51%)
  starting transfers between devices  26.8 us (28%)
  waiting for transfers between devices  14.9 us (15%)
  other arithmetic  2.68 us (3%)
  local copies, waits for them, and re-layouts  1.16 us (1%)
    pallas_call x12, Pallas kernels, guest_tile(): pl.pallas_call(functools.partial(guest_body, piece * width), out_shape=pl...  41.8 us
    ppermute x5, starting transfers between devices, core_swap(): return lax.ppermute(value, 'core', [(0, 1), (1, 0)])  13.9 us
    ppermute x6, waiting for transfers between devices, along_blk(): return lax.ppermute(value, BLK, pairs)  13.4 us
    ppermute x2, starting transfers between devices, from_neighbour(): return lax.ppermute(value, BLK, pairs)  9.48 us
    pallas_call x1, Pallas kernels, home_tile(): pl.pallas_call(home_body, out_shape=[pltpu.VMEM((count, LANES), jnp.float...  6.05 us
    ppermute x1, starting transfers between devices, shards(): crossed = lax.ppermute(value, ('core', 'rhs'), [(2, 3), (3, 2)])  2.22 us
  transfers between devices with their start and end apart: 16, of which 8 were waited for; matrix products, arithmetic and copies ran while one was open for 1% of the time, Pallas kernels for 52%

commit v1 on v0

v1 whole, which is shorter than its diff:
```python
import functools

import jax
import jax.numpy as jnp
from jax import lax
from jax.experimental import pallas as pl
from jax.experimental.pallas import tpu as pltpu
from jax.sharding import Mesh, PartitionSpec as P

LANES = 128
VMEM_BYTES = 12 * 2**20
ROW_STEP = 256
COL_STEP = 1024
PIECES = 4
COPIES = 4
BLK = ("y", "xh", "z", "core")


def split_parts(base):
    high = base.astype(jnp.bfloat16).astype(jnp.float32)
    rest = base - high
    mid = rest.astype(jnp.bfloat16).astype(jnp.float32)
    low = (rest - mid).astype(jnp.bfloat16).astype(jnp.float32)
    return high, mid, low


def point_values(axial, angle, area):
    axial = axial.astype(jnp.float32) - 4.0
    angle = angle.astype(jnp.float32)
    area = area.astype(jnp.float32)
    cos, sin = jnp.cos(angle), jnp.sin(angle)
    return axial, cos, sin, axial * axial + cos * cos + sin * sin, 1.0 / (area * area)


def lay_rows(base_ref, features):
    groups = features[0].shape[0]
    base_ref[...] = jnp.zeros_like(base_ref)
    for row, feature in enumerate(features):
        for group in range(groups):
            base_ref[row : row + 1, group * LANES : (group + 1) * LANES] = feature[group : group + 1, :]


def column_factors(geometry, base_ref, col_ref):
    axial, cos, sin, norm, scale = point_values(*geometry)
    lay_rows(base_ref, (scale, norm * scale, axial * scale, cos * scale, sin * scale))
    high, mid, low = split_parts(base_ref[...])
    col_ref[...] = jnp.concatenate([high, high, high, mid, mid, low], axis=0).astype(jnp.bfloat16)


def row_factors(geometry, base_ref, row_ref):
    axial, cos, sin, norm, scale = point_values(*geometry)
    count = base_ref.shape[1]
    scale = scale * count
    double = -2.0 * scale
    lay_rows(base_ref, ((norm + 0.01) * scale, scale, axial * double, cos * double, sin * double))
    high, mid, low = split_parts(base_ref[...])
    stacked = jnp.concatenate([high, mid, low, high, mid, high], axis=0)
    for group in range(count // LANES):
        part = stacked[:, group * LANES : (group + 1) * LANES]
        row_ref[group * LANES : (group + 1) * LANES, :] = part.T.astype(jnp.bfloat16)


def tile_product(row_ref, col_ref, directions_ref, out_ref, offset=0, width=None, arrive=None):
    width = width or col_ref.shape[1]
    step_cols = min(COL_STEP, width)

    def step_fn(step, carried):
        start = pl.multiple_of(step * step_cols, step_cols)
        if arrive is not None:
            arrive(step)
        cols = pl.ds(offset + start, step_cols)
        factor, directions = col_ref[:, cols], directions_ref[cols, :]
        for low in range(0, row_ref.shape[0], ROW_STEP):
            rows = slice(low, low + ROW_STEP)
            inverse = jnp.dot(row_ref[rows, :], factor, preferred_element_type=jnp.float32)
            values = lax.rsqrt(inverse).astype(jnp.bfloat16)
            out_ref[rows, :] += jnp.dot(values, directions, preferred_element_type=jnp.float32)
        return carried

    lax.fori_loop(0, width // step_cols, step_fn, 0)


def geometry_of(ref):
    groups = ref.shape[0] // 3
    return tuple(ref[k * groups : (k + 1) * groups, :].astype(jnp.float32) for k in range(3))


def geometry_copy(message_ref, geometry_ref, sem):
    rows = geometry_ref.shape[0]
    return pltpu.make_async_copy(message_ref.at[pl.ds(message_ref.shape[0] - rows, rows)], geometry_ref, sem)


def pack_body(directions_ref, axial_ref, angle_ref, area_ref, out_ref, sems):
    count = directions_ref.shape[0]
    part = count // COPIES
    copies = [
        pltpu.make_async_copy(
            directions_ref.at[pl.ds(k * part, part)], out_ref.at[pl.ds(k * part, part)], sems.at[k]
        )
        for k in range(COPIES)
    ]
    for copy in copies:
        copy.start()
    groups = axial_ref.shape[0]
    for k, ref in enumerate((axial_ref, angle_ref, area_ref)):
        out_ref[count + k * groups : count + (k + 1) * groups, :] = ref[...]
    for copy in copies:
        copy.wait()


def home_body(message_ref, out_ref, row_ref, base_ref, col_ref):
    count = row_ref.shape[0]
    geometry = geometry_of(message_ref.at[pl.ds(count, message_ref.shape[0] - count)])
    row_factors(geometry, base_ref, row_ref)
    column_factors(geometry, base_ref, col_ref)
    out_ref[...] = jnp.zeros_like(out_ref)
    tile_product(row_ref, col_ref, message_ref, out_ref)


def guest_body(has_total, n_later, row_ref, message_ref, *refs):
    refs = list(refs)
    if has_total:
        refs.pop(0)
    later = [refs.pop(0) for _ in range(n_later)]
    out_ref = refs.pop(0)
    outs = [(refs.pop(0), refs.pop(0)) for _ in range(n_later)]
    base_ref, col_ref, directions_ref, geometry_ref, sems = refs
    part = min(COL_STEP, row_ref.shape[0])
    steps = row_ref.shape[0] // part

    def piece_copy(step):
        rows = pl.ds(pl.multiple_of(step * part, part), part)
        return pltpu.make_async_copy(message_ref.at[rows], directions_ref.at[rows], sems.at[step])

    first = geometry_copy(message_ref, geometry_ref.at[0], sems.at[steps])
    first.start()
    for step in range(steps):
        piece_copy(step).start()
    copies = []
    for k, (ref, (dirs, _)) in enumerate(zip(later, outs)):
        at = steps + 1 + 2 * k
        copies.append(geometry_copy(ref, geometry_ref.at[k + 1], sems.at[at]))
        copies.append(pltpu.make_async_copy(ref.at[pl.ds(0, dirs.shape[0])], dirs, sems.at[at + 1]))
    for copy in copies:
        copy.start()
    first.wait()
    column_factors(geometry_of(geometry_ref.at[0]), base_ref, col_ref)
    if not has_total:
        out_ref[...] = jnp.zeros_like(out_ref)
    tile_product(row_ref, col_ref, directions_ref, out_ref, arrive=lambda step: piece_copy(step).wait())
    for copy in copies:
        copy.wait()
    for k, (_, factors) in enumerate(outs):
        column_factors(geometry_of(geometry_ref.at[k + 1]), base_ref, factors)


def piece_body(offset, width, row_ref, col_ref, directions_ref, total_ref, out_ref):
    tile_product(row_ref, col_ref, directions_ref, out_ref, offset, width)


def half_gram_body(own_ref, pair_ref, first_ref, second_ref, out_ref, sum_ref, directions_ref, sem):
    copy = pltpu.make_async_copy(pair_ref, directions_ref, sem)
    copy.start()
    first, second = first_ref[...], second_ref[...]
    value = 0.5 * first + second
    high = value.astype(jnp.bfloat16)
    low = (value - high.astype(jnp.float32)).astype(jnp.bfloat16)
    both = jnp.concatenate([high, low], axis=1)
    for k, ref in enumerate((own_ref, directions_ref)):
        if k == 1:
            copy.wait()
        part = lax.dot_general(
            ref[: value.shape[0], :], both, (((0,), (0,)), ((), ())), preferred_element_type=jnp.float32
        )
        out_ref[k] = part[:, :LANES] + part[:, LANES:]
    sum_ref[...] = first + second


def tile_cost(count):
    return pl.CostEstimate(flops=count * count * 128, bytes_accessed=0, transcendentals=0)


def near(value):
    return pltpu.with_memory_space_constraint(value, pltpu.VMEM)


def kernel_call(body, name, operands, places, outs, scratch, cost, aliases=None):
    vmem = pl.BlockSpec(memory_space=pltpu.VMEM)
    anywhere = pl.BlockSpec(memory_space=pl.ANY)
    return pl.pallas_call(
        body,
        out_shape=[pltpu.VMEM(*out) for out in outs],
        in_specs=[vmem if place else anywhere for place in places],
        out_specs=[vmem] * len(outs),
        input_output_aliases=aliases or {},
        scratch_shapes=scratch,
        cost_estimate=cost,
        compiler_params=pltpu.CompilerParams(vmem_limit_bytes=VMEM_BYTES),
        name=name,
    )(*[near(value) if place else value for value, place in zip(operands, places)])


def pack(directions, geometry):
    count = directions.shape[0]
    out = (count + sum(part.shape[0] for part in geometry), LANES)
    return kernel_call(
        pack_body, "pack", [directions, *geometry], [False, True, True, True], [(out, jnp.bfloat16)],
        [pltpu.SemaphoreType.DMA((COPIES,))], pl.CostEstimate(flops=0, bytes_accessed=2**20, transcendentals=0),
    )[0]


def tile_scratch(count):
    return [pltpu.VMEM((8, count), jnp.float32), pltpu.VMEM((48, count), jnp.bfloat16)]


def home_tile(message, count):
    outs = [((count, LANES), jnp.float32), ((count, 48), jnp.bfloat16)]
    return kernel_call(home_body, "home_tile", [message], [True], outs, tile_scratch(count), tile_cost(count))


def guest_tile(rows, message, total=None, later=()):
    count = rows.shape[0]
    totals = [] if total is None else [total]
    scratch = tile_scratch(count) + [
        pltpu.VMEM((count, LANES), jnp.bfloat16),
        pltpu.VMEM((1 + len(later), message.shape[0] - count, LANES), jnp.bfloat16),
        pltpu.SemaphoreType.DMA((count // min(COL_STEP, count) + 1 + 2 * len(later),)),
    ]
    outs = [((count, LANES), jnp.float32)]
    outs += [((count, LANES), jnp.bfloat16), ((48, count), jnp.bfloat16)] * len(later)
    return kernel_call(
        functools.partial(guest_body, bool(totals), len(later)), "guest_tile", [rows, message, *totals, *later],
        [True, False] + [True] * len(totals) + [False] * len(later), outs, scratch, tile_cost(count),
        {2: 0} if totals else None,
    )


def piece_tile(rows, guest, total, piece):
    count = rows.shape[0]
    directions, factors = guest
    width = count // PIECES
    return kernel_call(
        functools.partial(piece_body, piece * width, width), "piece_tile", [rows, factors, directions, total],
        [True] * 4, [((count, LANES), jnp.float32)], [], tile_cost(count), {3: 0},
    )[0]


def half_gram(message, pair, first, second):
    count = first.shape[0]
    outs = [((2, LANES, LANES), jnp.float32), ((count, LANES), jnp.float32)]
    scratch = [pltpu.VMEM((count, LANES), jnp.bfloat16), pltpu.SemaphoreType.DMA]
    return kernel_call(
        half_gram_body, "half_gram", [message, pair, first, second], [True, False, True, True], outs, scratch,
        tile_cost(count), {2: 1},
    )


def along_blk(value, sizes, target):
    ny, nx, nz, nc = sizes

    def index(y, x, z, c):
        return ((y % ny * nx + x % nx) * nz + z % nz) * nc + c % nc

    pairs = []
    for y in range(ny):
        for x in range(nx):
            for z in range(nz):
                for c in range(nc):
                    pairs.append((index(y, x, z, c), index(*target(y, x, z, c))))
    return lax.ppermute(value, BLK, pairs)


def from_neighbour(value, parity):
    count = lax.axis_size(BLK)
    pairs = []
    for block in range(count):
        chip, core = divmod(block, 2)
        first = chip % 2 == parity
        other = 2 * (chip + 1) + 1 - core if first else 2 * (chip - 1) + core
        pairs.append((block, other % count))
    return lax.ppermute(value, BLK, pairs)


def from_far(value):
    count = lax.axis_size(BLK)
    return lax.ppermute(
        value, BLK, [(b, (b - 3 if b % 2 == 0 else b + 3) % count) for b in range(count)]
    )


def core_swap(value):
    return lax.ppermute(value, "core", [(0, 1), (1, 0)])


def shards(sizes, directions, axial_pos, azimuth, panel_area):
    count = axial_pos.shape[0]
    geometry = [part.reshape(count // LANES, LANES) for part in (axial_pos, azimuth, panel_area)]
    message = pack(directions, geometry)
    other = core_swap(message)
    even = from_neighbour(message, 0)
    odd = from_neighbour(message, 1)

    first, rows = home_tile(message, count)
    first, late = lax.optimization_barrier((first, message))
    far = from_far(late)
    (first,) = guest_tile(rows, other, first)
    first, even, later = lax.optimization_barrier((first, even, directions))
    pair = lax.ppermute(later, "rhs", [(0, 1), (1, 0)])
    even_other = core_swap(even)
    (second,) = guest_tile(rows, even)
    second, odd = lax.optimization_barrier((second, odd))
    odd_other = core_swap(odd)
    (second,) = guest_tile(rows, odd, second)
    second, far = lax.optimization_barrier((second, far))
    first, *fetched = guest_tile(rows, far, first, (even_other, odd_other))
    even_other, odd_other = tuple(fetched[:2]), tuple(fetched[2:])
    half, product = half_gram(message, pair, first, second)

    core = lax.axis_index("core")
    keep = lax.dynamic_index_in_dim(half, core, 0, keepdims=False)
    value = keep + core_swap(lax.dynamic_index_in_dim(half, 1 - core, 0, keepdims=False))

    value, product = lax.optimization_barrier((value, product))
    crossed = lax.ppermute(value, ("core", "rhs"), [(2, 3), (3, 2)])
    product = piece_tile(rows, even_other, product, 0)
    value, crossed, product = lax.optimization_barrier((value, crossed, product))
    value = value + jnp.where(core == 0, value, crossed).T

    work = [(even_other, piece) for piece in range(1, PIECES)] + [(odd_other, piece) for piece in range(PIECES)]
    stages = (
        ((0, 0, 4), 2), ((0, 0, 2), 1), ((0, 0, 1), 1), ((2, 0, 0), 1), ((1, 0, 0), 1), ((0, 1, 0), 1),
    )
    for move, pieces in stages:
        value, product = lax.optimization_barrier((value, product))
        moved = along_blk(
            value, sizes, lambda y, x, z, c, d=move: (y + d[0], x + d[1], z + d[2], c)
        )
        for _ in range(pieces):
            guest, piece = work.pop(0)
            product = piece_tile(rows, guest, product, piece)
        value, product, moved = lax.optimization_barrier((value, product, moved))
        value = value + moved
    value = value / (count * lax.axis_size(BLK))
    swapped = core_swap(value)
    upper = core == lax.axis_index("rhs")
    gram = jnp.concatenate([jnp.where(upper, value, swapped), jnp.where(upper, swapped, value)], axis=0)
    return product, gram


def solution(mesh):
    sizes = (4, 2, 8, 2)
    fine = Mesh(mesh.devices.reshape(sizes + (2,)), BLK + ("rhs",))
    in_specs = (P(BLK, "rhs"), P(BLK), P(BLK), P(BLK))
    out_specs = (P(BLK, "rhs"), P(None, "rhs"))
    return jax.shard_map(
        functools.partial(shards, sizes), mesh=fine, in_specs=in_specs, out_specs=out_specs, check_vma=False
    )
```

time: 96.5 us -> 99.9 us (1.035)
  starting transfers between devices: 26.8 us -> 34.4 us
  Pallas kernels: 49.5 us -> 44.8 us
  local copies, waits for them, and re-layouts: 1.16 us -> 5.71 us
  waiting for transfers between devices: 14.9 us -> 12 us
  other arithmetic: 2.68 us -> 1.59 us
    ppermute x6, starting transfers between devices: 0.75 us -> 9.17 us  [along_blk(): return lax.ppermute(value, BLK, pairs)]
    pallas_call x14 -> x15, Pallas kernels: 49.5 us -> 44.8 us  [kernel_call(): pl.pallas_call(body, out_shape=[pltpu.VMEM(*out) for out in outs], in_spe...]
    unnamed x1 -> x19, local copies, waits for them, and re-layouts: 0.97 us -> 5.53 us
    ppermute x6, waiting for transfers between devices: 13.4 us -> 10.4 us  [along_blk(): return lax.ppermute(value, BLK, pairs)]
    concatenate x1 -> x0, other arithmetic: 1.92 us -> none  [shards(): message = jnp.concatenate([directions] + geometry, axis=0)]
  transfers between devices with their start and end apart: 16 -> 16, of which waited for: 8 -> 8; matrix products, arithmetic and copies ran while one was open for 1% -> 1% of each run, Pallas kernels for 52% -> 42%
where the time goes in v1:
time: 99.9 us; the launch traced here: 99.5 us
  Pallas kernels  44.8 us (45%)
  starting transfers between devices  34.4 us (34%)
  waiting for transfers between devices  12 us (12%)
  local copies, waits for them, and re-layouts  5.71 us (6%)
  other arithmetic  1.59 us (2%)
    pallas_call x15, Pallas kernels, kernel_call(): pl.pallas_call(body, out_shape=[pltpu.VMEM(*out) for out in outs], in_spe...  44.8 us
    ppermute x5, starting transfers between devices, core_swap(): return lax.ppermute(value, 'core', [(0, 1), (1, 0)])  13.1 us
    ppermute x6, waiting for transfers between devices, along_blk(): return lax.ppermute(value, BLK, pairs)  10.4 us
    ppermute x2, starting transfers between devices, from_neighbour(): return lax.ppermute(value, BLK, pairs)  9.49 us
    ppermute x6, starting transfers between devices, along_blk(): return lax.ppermute(value, BLK, pairs)  9.17 us
    unnamed x19, local copies, waits for them, and re-layouts  5.53 us
    ppermute x1, starting transfers between devices, shards(): crossed = lax.ppermute(value, ('core', 'rhs'), [(2, 3), (3, 2)])  2.22 us
  transfers between devices with their start and end apart: 16, of which 8 were waited for; matrix products, arithmetic and copies ran while one was open for 1% of the time, Pallas kernels for 42%

profile of v1, /device:TPU:1, one launch (start us, length us, event | category | flops | bytes accessed | tf_op | source)
XLA Modules:
  0.0 99.5 jit_solution(5636734978141326749)
XLA Ops:
  3.8 3.3 %collective-permute-start = (bf16[2096,128]{1,0:T(8,128)(2,1)S(1)}, bf16[2096,128]{1,0:T(8,128)(2,1)S(1)}, u32[]{:S(2)}, u32[]{:S(2)}) collective-permute-start(bf16[2096,128]{1,0:T(8,128)(2,1)S(1)} %pack.1.message_ref.own_ref), channel_id=1, source_target_pairs={{0,2},{2,0},{1,3},{3,1},{4,6},{6,4},{5,7},{7,5},{8,10},{10,8},{9,1... | collective-permute-start | bytes 1609736 | tf_op jit(solution)/shard_map/ppermute | solution.py:292
  7.2 9.5 %collective-permute-start.3 = (bf16[2096,128]{1,0:T(8,128)(2,1)S(1)}, bf16[2096,128]{1,0:T(8,128)(2,1)}, u32[]{:S(2)}, u32[]{:S(2)}) collective-permute-start(bf16[2096,128]{1,0:T(8,128)(2,1)S(1)} %pack.1.message_ref.own_ref), channel_id=1, source_target_pairs={{0,252},{2,254},{4,10},{6,8},{8,4},{10,6},{12,18},{14,16},{16,12},... | collective-permute-start | bytes 1609736 | tf_op jit(solution)/shard_map/ppermute | solution.py:281
  16.7 4.9 %home_tile.1 = (f32[2048,128]{1,0:T(8,128)S(1)}, bf16[2048,48]{1,0:T(8,128)(2,1)S(1)}) custom-call(bf16[2096,128]{1,0:T(8,128)(2,1)S(1)} %pack.1.message_ref.own_ref), custom_call_target="tpu_custom_call" | custom-call | flops 536870912 | tf_op jit(solution)/shard_map/home_tile/pallas_call | solution.py:190
  21.7 4.8 %guest_tile.4.refs_0_ = f32[2048,128]{1,0:T(8,128)S(1)} custom-call(bf16[2048,48]{1,0:T(8,128)(2,1)S(1)} %get-tuple-element.55.row_ref, bf16[2096,128]{1,0:T(8,128)(2,1)S(1)} %collective-permute-done.message_ref, f32[2048,128]{1,0:T(8,128)S(1)} %get-tuple-element.57.refs_0_), custom_call_target="tpu_custom_call", output_to_operand_aliasing={{}: (2, {})} | custom-call | flops 536870912 | tf_op jit(solution)/shard_map/guest_tile/pallas_call | solution.py:190
  26.5 5.6 %guest_tile.5.refs_0_ = f32[2048,128]{1,0:T(8,128)S(1)} custom-call(bf16[2048,48]{1,0:T(8,128)(2,1)S(1)} %get-tuple-element.55.row_ref, bf16[2096,128]{1,0:T(8,128)(2,1)} %collective-permute-done.1.message_ref), custom_call_target="tpu_custom_call" | custom-call | flops 536870912 | tf_op jit(solution)/shard_map/guest_tile/pallas_call | solution.py:190
  34.2 5.6 %guest_tile.6.second_ref = f32[2048,128]{1,0:T(8,128)S(1)} custom-call(bf16[2048,48]{1,0:T(8,128)(2,1)S(1)} %get-tuple-element.55.row_ref, bf16[2096,128]{1,0:T(8,128)(2,1)} %collective-permute-done.3.message_ref, f32[2048,128]{1,0:T(8,128)S(1)} %guest_tile.5.refs_0_), custom_call_target="tpu_custom_call", output_to_operand_aliasing={{}: (2, {})} | custom-call | flops 536870912 | tf_op jit(solution)/shard_map/guest_tile/pallas_call | solution.py:190
  39.9 5.9 %guest_tile.7 = (f32[2048,128]{1,0:T(8,128)S(1)}, bf16[2048,128]{1,0:T(8,128)(2,1)S(1)}, bf16[48,2048]{1,0:T(8,128)(2,1)S(1)}, bf16[2048,128]{1,0:T(8,128)(2,1)S(1)}, bf16[48,2048]{1,0:T(8,128)(2,1)S(1)}) custom-call(bf16[2048,48]{1,0:T(8,128)(2,1)S(1)} %get-tuple-element.55.row_ref, ...), custom_call_target="tpu_custom_call", output_to_operand_aliasing={{0}: (2, {})} | custom-call | flops 536870912 | tf_op jit(solution)/shard_map/guest_tile/pallas_call | solution.py:190
  47.3 1.8 %half_gram.1 = (f32[2,128,128]{2,1,0:T(8,128)S(1)}, f32[2048,128]{1,0:T(8,128)S(1)}) custom-call(bf16[2096,128]{1,0:T(8,128)(2,1)S(1)} %copy-done.4, bf16[2048,128]{1,0:T(8,128)(2,1)} %collective-permute-done.2.pair_ref, f32[2048,128]{1,0:T(8,128)S(1)} %get-tuple-element.65.first_ref, ...), custom_call_target="tpu_custom_call", output_to_operand_aliasing={{1}: (2, {})} | custom-call | flops 536870912 | tf_op jit(solution)/shard_map/half_gram/pallas_call | solution.py:190
  49.8 3.0 %collective-permute-start.7 = (f32[128,128]{1,0:T(8,128)S(1)}, f32[128,128]{1,0:T(8,128)S(1)}, u32[]{:S(2)}, u32[]{:S(2)}) collective-permute-start(f32[128,128]{1,0:T(8,128)S(1)} %dynamic-slice_bitcast_fusion), channel_id=1, source_target_pairs={{0,2},{2,0},{1,3},{3,1},{4,6},{6,4},{5,7},{7,5},{8,10},{10,8},{9,1... | collective-permute-start | bytes 196616 | tf_op jit(solution)/shard_map/ppermute | solution.py:292
  54.7 2.2 %collective-permute-start.8 = (f32[128,128]{0,1:T(8,128)S(1)}, f32[128,128]{0,1:T(8,128)S(1)}, u32[]{:S(2)}, u32[]{:S(2)}) collective-permute-start(f32[128,128]{0,1:T(8,128)S(1)} %copy.19), channel_id=1, source_target_pairs={{2,3},{3,2},{6,7},{7,6},{10,11},{11,10},{14,15},{15,14},{18,19},{1... | collective-permute-start | bytes 196616 | tf_op jit(solution)/shard_map/ppermute | solution.py:324
  58.0 1.9 %piece_tile.8.total_ref = f32[2048,128]{1,0:T(8,128)S(1)} custom-call(bf16[2048,48]{1,0:T(8,128)(2,1)S(1)} %get-tuple-element.55.row_ref, bf16[48,2048]{1,0:T(8,128)(2,1)S(1)} %get-tuple-element.70.col_ref, bf16[2048,128]{1,0:T(8,128)(2,1)S(1)} %copy-done.1, f32[2048,128]{1,0:T(8,128)S(1)} %get-tuple-element.72.total_ref), custom_call_target="tpu_custom_call", output_to_operand_aliasing={{}: (3, {})} | custom-call | flops 536870912 | tf_op jit(solution)/shard_map/piece_tile/pallas_call | solution.py:190
  60.4 1.9 %piece_tile.9.total_ref = f32[2048,128]{1,0:T(8,128)S(1)} custom-call(bf16[2048,48]{1,0:T(8,128)(2,1)S(1)} %get-tuple-element.55.row_ref, bf16[48,2048]{1,0:T(8,128)(2,1)S(1)} %get-tuple-element.70.col_ref, bf16[2048,128]{1,0:T(8,128)(2,1)S(1)} %copy-done.2, f32[2048,128]{1,0:T(8,128)S(1)} %piece_tile.8.total_ref), custom_call_target="tpu_custom_call", output_to_operand_aliasing={{}: (3, {})} | custom-call | flops 536870912 | tf_op jit(solution)/shard_map/piece_tile/pallas_call | solution.py:190
  62.3 1.9 %piece_tile.10.total_ref = f32[2048,128]{1,0:T(8,128)S(1)} custom-call(bf16[2048,48]{1,0:T(8,128)(2,1)S(1)} %get-tuple-element.55.row_ref, bf16[48,2048]{1,0:T(8,128)(2,1)S(1)} %get-tuple-element.70.col_ref, bf16[2048,128]{1,0:T(8,128)(2,1)S(1)} %copy-done.2, f32[2048,128]{1,0:T(8,128)S(1)} %piece_tile.9.total_ref), custom_call_target="tpu_custom_call", output_to_operand_aliasing={{}: (3, {})} | custom-call | flops 536870912 | tf_op jit(solution)/shard_map/piece_tile/pallas_call | solution.py:190
  64.2 3.0 %collective-permute-done.9 = f32[128,128]{1,0:T(8,128)S(1)} collective-permute-done((f32[128,128]{1,0:T(8,128)S(1)}, f32[128,128]{1,0:T(8,128)S(1)}, u32[]{:S(2)}, u32[]{:S(2)}) %collective-permute-start.9) | collective-permute-done | bytes 65568 | tf_op jit(solution)/shard_map/ppermute | solution.py:270
  67.1 4.0 %collective-permute-start.10 = (f32[128,128]{1,0:T(8,128)S(1)}, f32[128,128]{1,0:T(8,128)S(1)}, u32[]{:S(2)}, u32[]{:S(2)}) collective-permute-start(f32[128,128]{1,0:T(8,128)S(1)} %add.36), channel_id=1, source_target_pairs={{0,8},{2,10},{4,12},{6,14},{8,16},{10,18},{12,20},{14,22},{16,24},... | collective-permute-start | bytes 196616 | tf_op jit(solution)/shard_map/ppermute | solution.py:270
  71.1 1.9 %piece_tile.11.total_ref = f32[2048,128]{1,0:T(8,128)S(1)} custom-call(bf16[2048,48]{1,0:T(8,128)(2,1)S(1)} %get-tuple-element.55.row_ref, bf16[48,2048]{1,0:T(8,128)(2,1)S(1)} %get-tuple-element.70.col_ref, bf16[2048,128]{1,0:T(8,128)(2,1)S(1)} %copy-done.2, f32[2048,128]{1,0:T(8,128)S(1)} %piece_tile.10.total_ref), custom_call_target="tpu_custom_call", output_to_operand_aliasing={{}: (3, {})} | custom-call | flops 536870912 | tf_op jit(solution)/shard_map/piece_tile/pallas_call | solution.py:190
  74.6 1.9 %piece_tile.12.total_ref = f32[2048,128]{1,0:T(8,128)S(1)} custom-call(bf16[2048,48]{1,0:T(8,128)(2,1)S(1)} %get-tuple-element.55.row_ref, bf16[48,2048]{1,0:T(8,128)(2,1)S(1)} %get-tuple-element.87.col_ref, bf16[2048,128]{1,0:T(8,128)(2,1)S(1)} %get-tuple-element.88.directions_ref, f32[2048,128]{1,0:T(8,128)S(1)} %piece_tile.11.total_ref), custom_call_target="tpu_custom_call", output_to_operand_aliasing={{}: (3, {})} | custom-call | flops 536870912 | tf_op jit(solution)/shard_map/piece_tile/pallas_call | solution.py:190
  76.5 2.4 %collective-permute-done.11 = f32[128,128]{1,0:T(8,128)S(1)} collective-permute-done((f32[128,128]{1,0:T(8,128)S(1)}, f32[128,128]{1,0:T(8,128)S(1)}, u32[]{:S(2)}, u32[]{:S(2)}) %collective-permute-start.11) | collective-permute-done | bytes 65568 | tf_op jit(solution)/shard_map/ppermute | solution.py:270
  78.9 2.4 %collective-permute-start.12 = (f32[128,128]{1,0:T(8,128)S(1)}, f32[128,128]{1,0:T(8,128)S(1)}, u32[]{:S(2)}, u32[]{:S(2)}) collective-permute-start(f32[128,128]{1,0:T(8,128)S(1)} %add.38), channel_id=1, source_target_pairs={{0,128},{2,130},{4,132},{6,134},{8,136},{10,138},{12,140},{14,142}... | collective-permute-start | bytes 196616 | tf_op jit(solution)/shard_map/ppermute | solution.py:270
  81.4 1.9 %piece_tile.13.total_ref = f32[2048,128]{1,0:T(8,128)S(1)} custom-call(bf16[2048,48]{1,0:T(8,128)(2,1)S(1)} %get-tuple-element.55.row_ref, bf16[48,2048]{1,0:T(8,128)(2,1)S(1)} %get-tuple-element.87.col_ref, bf16[2048,128]{1,0:T(8,128)(2,1)S(1)} %get-tuple-element.88.directions_ref, f32[2048,128]{1,0:T(8,128)S(1)} %piece_tile.12.total_ref), custom_call_target="tpu_custom_call", output_to_operand_aliasing={{}: (3, {})} | custom-call | flops 536870912 | tf_op jit(solution)/shard_map/piece_tile/pallas_call | solution.py:190
  84.5 1.9 %piece_tile.14.total_ref = f32[2048,128]{1,0:T(8,128)S(1)} custom-call(bf16[2048,48]{1,0:T(8,128)(2,1)S(1)} %get-tuple-element.55.row_ref, bf16[48,2048]{1,0:T(8,128)(2,1)S(1)} %get-tuple-element.87.col_ref, bf16[2048,128]{1,0:T(8,128)(2,1)S(1)} %get-tuple-element.88.directions_ref, f32[2048,128]{1,0:T(8,128)S(1)} %piece_tile.13.total_ref), custom_call_target="tpu_custom_call", output_to_operand_aliasing={{}: (3, {})} | custom-call | flops 536870912 | tf_op jit(solution)/shard_map/piece_tile/pallas_call | solution.py:190
  86.3 1.7 %collective-permute-done.13 = f32[128,128]{1,0:T(8,128)S(1)} collective-permute-done((f32[128,128]{1,0:T(8,128)S(1)}, f32[128,128]{1,0:T(8,128)S(1)}, u32[]{:S(2)}, u32[]{:S(2)}) %collective-permute-start.13) | collective-permute-done | bytes 65568 | tf_op jit(solution)/shard_map/ppermute | solution.py:270
  89.5 1.9 %piece_tile.15 = f32[2048,128]{1,0:T(8,128)S(1)} custom-call(bf16[2048,48]{1,0:T(8,128)(2,1)S(1)} %get-tuple-element.55.row_ref, bf16[48,2048]{1,0:T(8,128)(2,1)S(1)} %get-tuple-element.87.col_ref, bf16[2048,128]{1,0:T(8,128)(2,1)S(1)} %get-tuple-element.88.directions_ref, f32[2048,128]{1,0:T(8,128)S(1)} %piece_tile.14.total_ref), custom_call_target="tpu_custom_call", output_to_operand_aliasing={{}: (3, {})} | custom-call | flops 536870912 | tf_op jit(solution)/shard_map/piece_tile/pallas_call | solution.py:190
  92.8 5.1 %collective-permute-start.15 = (f32[128,128]{1,0:T(8,128)S(1)}, f32[128,128]{1,0:T(8,128)S(1)}, u32[]{:S(2)}, u32[]{:S(2)}) collective-permute-start(f32[128,128]{1,0:T(8,128)S(1)} %add_multiply_fusion), channel_id=1, source_target_pairs={{0,2},{2,0},{1,3},{3,1},{4,6},{6,4},{5,7},{7,5},{8,10},{10,8},{9,1... | collective-permute-start | bytes 196616 | tf_op jit(solution)/shard_map/ppermute | solution.py:292
  (55 shorter events, 18.2 us)
Async XLA Ops:
  0.6 0.7 copy-start.6
  1.3 0.7 copy-start.7
  2.0 0.7 copy-start.8
  3.8 17.8 %copy-start.3 = (bf16[2096,128]{1,0:T(8,128)(2,1)}, bf16[2096,128]{1,0:T(8,128)(2,1)S(1)}, u32[]{:S(2)}) copy-start(bf16[2096,128]{1,0:T(8,128)(2,1)S(1)} %pack.1.message_ref.own_ref) | copy-start | bytes 1609732
  3.8 17.9 %collective-permute-start = (bf16[2096,128]{1,0:T(8,128)(2,1)S(1)}, bf16[2096,128]{1,0:T(8,128)(2,1)S(1)}, u32[]{:S(2)}, u32[]{:S(2)}) collective-permute-start(bf16[2096,128]{1,0:T(8,128)(2,1)S(1)} %pack.1.message_ref.own_ref), channel_id=1, source_target_pairs={{0,2},{2,0},{1,3},{3,1},{4,6},{6,4},{5,7},{7,5},{8,10},{10,8},{9,1... | collective-permute-start | bytes 1609736 | tf_op jit(solution)/shard_map/ppermute | solution.py:292
  7.2 19.4 %collective-permute-start.1 = (bf16[2096,128]{1,0:T(8,128)(2,1)S(1)}, bf16[2096,128]{1,0:T(8,128)(2,1)}, u32[]{:S(2)}, u32[]{:S(2)}) collective-permute-start(bf16[2096,128]{1,0:T(8,128)(2,1)S(1)} %pack.1.message_ref.own_ref), channel_id=1, source_target_pairs={{0,6},{2,4},{4,0},{6,2},{8,14},{10,12},{12,8},{14,10},{16,22},{18,... | collective-permute-start | bytes 1609736 | tf_op jit(solution)/shard_map/ppermute | solution.py:281
  7.2 25.0 %collective-permute-start.3 = (bf16[2096,128]{1,0:T(8,128)(2,1)S(1)}, bf16[2096,128]{1,0:T(8,128)(2,1)}, u32[]{:S(2)}, u32[]{:S(2)}) collective-permute-start(bf16[2096,128]{1,0:T(8,128)(2,1)S(1)} %pack.1.message_ref.own_ref), channel_id=1, source_target_pairs={{0,252},{2,254},{4,10},{6,8},{8,4},{10,6},{12,18},{14,16},{16,12},... | collective-permute-start | bytes 1609736 | tf_op jit(solution)/shard_map/ppermute | solution.py:281
  21.6 18.3 %collective-permute-start.4 = (bf16[2096,128]{1,0:T(8,128)(2,1)S(1)}, bf16[2096,128]{1,0:T(8,128)(2,1)}, u32[]{:S(2)}, u32[]{:S(2)}) collective-permute-start(bf16[2096,128]{1,0:T(8,128)(2,1)S(1)} %pack.1.message_ref.own_ref), channel_id=1, source_target_pairs={{0,250},{2,8},{4,254},{6,12},{8,2},{10,16},{12,6},{14,20},{16,10},... | collective-permute-start | bytes 1609736 | tf_op jit(solution)/shard_map/ppermute | solution.py:286
  32.2 7.7 %collective-permute-start.6 = (bf16[2096,128]{1,0:T(8,128)(2,1)}, bf16[2096,128]{1,0:T(8,128)(2,1)}, u32[]{:S(2)}, u32[]{:S(2)}) collective-permute-start(bf16[2096,128]{1,0:T(8,128)(2,1)} %collective-permute-done.3.message_ref), channel_id=1, source_target_pairs={{0,2},{2,0},{1,3},{3,1},{4,6},{6,4},{5,7},{7,5},{8,10},{10,8},{9,1... | collective-permute-start | bytes 1609736 | tf_op jit(solution)/shard_map/ppermute | solution.py:292
  33.8 6.1 %collective-permute-start.5 = (bf16[2096,128]{1,0:T(8,128)(2,1)}, bf16[2096,128]{1,0:T(8,128)(2,1)}, u32[]{:S(2)}, u32[]{:S(2)}) collective-permute-start(bf16[2096,128]{1,0:T(8,128)(2,1)} %collective-permute-done.1.message_ref), channel_id=1, source_target_pairs={{0,2},{2,0},{1,3},{3,1},{4,6},{6,4},{5,7},{7,5},{8,10},{10,8},{9,1... | collective-permute-start | bytes 1609736 | tf_op jit(solution)/shard_map/ppermute | solution.py:292
  33.9 13.4 %collective-permute-start.2 = (bf16[2048,128]{1,0:T(8,128)(2,1)}, bf16[2048,128]{1,0:T(8,128)(2,1)}, u32[]{:S(2)}, u32[]{:S(2)}) collective-permute-start(bf16[2048,128]{1,0:T(8,128)(2,1)} %directions_ref.1), channel_id=1, source_target_pairs={{0,1},{1,0},{2,3},{3,2},{4,5},{5,4},{6,7},{7,6},{8,9},{9,8},{10,11... | collective-permute-start | bytes 1572872 | tf_op jit(solution)/shard_map/ppermute | solution.py:308
  39.9 7.5 %copy-start.4 = (bf16[2096,128]{1,0:T(8,128)(2,1)S(1)}, bf16[2096,128]{1,0:T(8,128)(2,1)}, u32[]{:S(2)}) copy-start(bf16[2096,128]{1,0:T(8,128)(2,1)} %copy-done.3) | copy-start | bytes 1609732
  45.8 0.8 copy-start
  49.8 3.9 %collective-permute-start.7 = (f32[128,128]{1,0:T(8,128)S(1)}, f32[128,128]{1,0:T(8,128)S(1)}, u32[]{:S(2)}, u32[]{:S(2)}) collective-permute-start(f32[128,128]{1,0:T(8,128)S(1)} %dynamic-slice_bitcast_fusion), channel_id=1, source_target_pairs={{0,2},{2,0},{1,3},{3,1},{4,6},{6,4},{5,7},{7,5},{8,10},{10,8},{9,1... | collective-permute-start | bytes 196616 | tf_op jit(solution)/shard_map/ppermute | solution.py:292
  54.7 5.2 %collective-permute-start.8 = (f32[128,128]{0,1:T(8,128)S(1)}, f32[128,128]{0,1:T(8,128)S(1)}, u32[]{:S(2)}, u32[]{:S(2)}) collective-permute-start(f32[128,128]{0,1:T(8,128)S(1)} %copy.19), channel_id=1, source_target_pairs={{2,3},{3,2},{6,7},{7,6},{10,11},{11,10},{14,15},{15,14},{18,19},{1... | collective-permute-start | bytes 196616 | tf_op jit(solution)/shard_map/ppermute | solution.py:324
  56.9 1.0 %copy-start.1 = (bf16[2048,128]{1,0:T(8,128)(2,1)S(1)}, bf16[2048,128]{1,0:T(8,128)(2,1)}, u32[]{:S(2)}) copy-start(bf16[2048,128]{1,0:T(8,128)(2,1)} %copy-done) | copy-start | bytes 1572868
  58.0 2.4 %copy-start.2 = (bf16[2048,128]{1,0:T(8,128)(2,1)S(1)}, bf16[2048,128]{1,0:T(8,128)(2,1)}, u32[]{:S(2)}) copy-start(bf16[2048,128]{1,0:T(8,128)(2,1)} %copy-done) | copy-start | bytes 1572868
  60.0 7.2 %collective-permute-start.9 = (f32[128,128]{1,0:T(8,128)S(1)}, f32[128,128]{1,0:T(8,128)S(1)}, u32[]{:S(2)}, u32[]{:S(2)}) collective-permute-start(f32[128,128]{1,0:T(8,128)S(1)} %bitcast_add_fusion), channel_id=1, source_target_pairs={{0,16},{2,18},{4,20},{6,22},{8,24},{10,26},{12,28},{14,30},{16,0},... | collective-permute-start | bytes 196616 | tf_op jit(solution)/shard_map/ppermute | solution.py:270
  67.1 7.4 %collective-permute-start.10 = (f32[128,128]{1,0:T(8,128)S(1)}, f32[128,128]{1,0:T(8,128)S(1)}, u32[]{:S(2)}, u32[]{:S(2)}) collective-permute-start(f32[128,128]{1,0:T(8,128)S(1)} %add.36), channel_id=1, source_target_pairs={{0,8},{2,10},{4,12},{6,14},{8,16},{10,18},{12,20},{14,22},{16,24},... | collective-permute-start | bytes 196616 | tf_op jit(solution)/shard_map/ppermute | solution.py:270
  74.5 4.4 %collective-permute-start.11 = (f32[128,128]{1,0:T(8,128)S(1)}, f32[128,128]{1,0:T(8,128)S(1)}, u32[]{:S(2)}, u32[]{:S(2)}) collective-permute-start(f32[128,128]{1,0:T(8,128)S(1)} %add.37), channel_id=1, source_target_pairs={{0,4},{2,6},{4,8},{6,10},{8,12},{10,14},{12,16},{14,18},{16,20},{1... | collective-permute-start | bytes 196616 | tf_op jit(solution)/shard_map/ppermute | solution.py:270
  78.9 4.7 %collective-permute-start.12 = (f32[128,128]{1,0:T(8,128)S(1)}, f32[128,128]{1,0:T(8,128)S(1)}, u32[]{:S(2)}, u32[]{:S(2)}) collective-permute-start(f32[128,128]{1,0:T(8,128)S(1)} %add.38), channel_id=1, source_target_pairs={{0,128},{2,130},{4,132},{6,134},{8,136},{10,138},{12,140},{14,142}... | collective-permute-start | bytes 196616 | tf_op jit(solution)/shard_map/ppermute | solution.py:270
  83.7 4.4 %collective-permute-start.13 = (f32[128,128]{1,0:T(8,128)S(1)}, f32[128,128]{1,0:T(8,128)S(1)}, u32[]{:S(2)}, u32[]{:S(2)}) collective-permute-start(f32[128,128]{1,0:T(8,128)S(1)} %add.39), channel_id=1, source_target_pairs={{0,64},{2,66},{4,68},{6,70},{8,72},{10,74},{12,76},{14,78},{16,80}... | collective-permute-start | bytes 196616 | tf_op jit(solution)/shard_map/ppermute | solution.py:270
  88.1 4.7 %collective-permute-start.14 = (f32[128,128]{1,0:T(8,128)S(1)}, f32[128,128]{1,0:T(8,128)S(1)}, u32[]{:S(2)}, u32[]{:S(2)}) collective-permute-start(f32[128,128]{1,0:T(8,128)S(1)} %add.40), channel_id=1, source_target_pairs={{0,32},{2,34},{4,36},{6,38},{8,40},{10,42},{12,44},{14,46},{16,48}... | collective-permute-start | bytes 196616 | tf_op jit(solution)/shard_map/ppermute | solution.py:270
  92.8 6.1 %collective-permute-start.15 = (f32[128,128]{1,0:T(8,128)S(1)}, f32[128,128]{1,0:T(8,128)S(1)}, u32[]{:S(2)}, u32[]{:S(2)}) collective-permute-start(f32[128,128]{1,0:T(8,128)S(1)} %add_multiply_fusion), channel_id=1, source_target_pairs={{0,2},{2,0},{1,3},{3,1},{4,6},{6,4},{5,7},{7,5},{8,10},{10,8},{9,1... | collective-permute-start | bytes 196616 | tf_op jit(solution)/shard_map/ppermute | solution.py:292
  (1 other events, 0.7 us)

commit v2 on v1

v2 whole, which is shorter than its diff:
```python
import functools

import jax
import jax.numpy as jnp
from jax import lax
from jax.experimental import pallas as pl
from jax.experimental.pallas import tpu as pltpu
from jax.sharding import Mesh, PartitionSpec as P

LANES = 128
VMEM_BYTES = 12 * 2**20
ROW_STEP = 256
COL_STEP = 1024
PIECES = 4
PIECE_ROWS = 1024
COPIES = 4
BLK = ("y", "xh", "z", "core")


def split_parts(base):
    high = base.astype(jnp.bfloat16).astype(jnp.float32)
    rest = base - high
    mid = rest.astype(jnp.bfloat16).astype(jnp.float32)
    low = (rest - mid).astype(jnp.bfloat16).astype(jnp.float32)
    return high, mid, low


def point_values(axial, angle, area):
    axial = axial.astype(jnp.float32) - 4.0
    angle = angle.astype(jnp.float32)
    area = area.astype(jnp.float32)
    cos, sin = jnp.cos(angle), jnp.sin(angle)
    return axial, cos, sin, axial * axial + cos * cos + sin * sin, 1.0 / (area * area)


def lay_rows(base_ref, features):
    groups = features[0].shape[0]
    base_ref[...] = jnp.zeros_like(base_ref)
    for row, feature in enumerate(features):
        for group in range(groups):
            base_ref[row : row + 1, group * LANES : (group + 1) * LANES] = feature[group : group + 1, :]


def column_factors(geometry, base_ref, col_ref):
    axial, cos, sin, norm, scale = point_values(*geometry)
    lay_rows(base_ref, (scale, norm * scale, axial * scale, cos * scale, sin * scale))
    high, mid, low = split_parts(base_ref[...])
    col_ref[...] = jnp.concatenate([high, high, high, mid, mid, low], axis=0).astype(jnp.bfloat16)


def row_factors(geometry, base_ref, row_ref):
    axial, cos, sin, norm, scale = point_values(*geometry)
    count = base_ref.shape[1]
    scale = scale * count
    double = -2.0 * scale
    lay_rows(base_ref, ((norm + 0.01) * scale, scale, axial * double, cos * double, sin * double))
    high, mid, low = split_parts(base_ref[...])
    stacked = jnp.concatenate([high, mid, low, high, mid, high], axis=0)
    for group in range(count // LANES):
        part = stacked[:, group * LANES : (group + 1) * LANES]
        row_ref[group * LANES : (group + 1) * LANES, :] = part.T.astype(jnp.bfloat16)


def tile_product(row_ref, col_ref, directions_ref, out_ref, offset=0, width=None, arrive=None, row_step=ROW_STEP):
    width = width or col_ref.shape[1]
    step_cols = min(COL_STEP, width)

    def step_fn(step, carried):
        start = pl.multiple_of(step * step_cols, step_cols)
        if arrive is not None:
            arrive(step)
        cols = pl.ds(offset + start, step_cols)
        factor, directions = col_ref[:, cols], directions_ref[cols, :]
        for low in range(0, row_ref.shape[0], row_step):
            rows = slice(low, low + row_step)
            inverse = jnp.dot(row_ref[rows, :], factor, preferred_element_type=jnp.float32)
            values = lax.rsqrt(inverse).astype(jnp.bfloat16)
            out_ref[rows, :] += jnp.dot(values, directions, preferred_element_type=jnp.float32)
        return carried

    lax.fori_loop(0, width // step_cols, step_fn, 0)


def geometry_of(ref):
    groups = ref.shape[0] // 3
    return tuple(ref[k * groups : (k + 1) * groups, :].astype(jnp.float32) for k in range(3))


def geometry_copy(message_ref, geometry_ref, sem):
    rows = geometry_ref.shape[0]
    return pltpu.make_async_copy(message_ref.at[pl.ds(message_ref.shape[0] - rows, rows)], geometry_ref, sem)


def pack_body(directions_ref, axial_ref, angle_ref, area_ref, out_ref, sems):
    count = directions_ref.shape[0]
    part = count // COPIES
    copies = [
        pltpu.make_async_copy(
            directions_ref.at[pl.ds(k * part, part)], out_ref.at[pl.ds(k * part, part)], sems.at[k]
        )
        for k in range(COPIES)
    ]
    groups = axial_ref.shape[0]
    for k, ref in enumerate((axial_ref, angle_ref, area_ref)):
        rows = out_ref.at[pl.ds(count + k * groups, groups)]
        copies.append(pltpu.make_async_copy(ref, rows, sems.at[COPIES + k]))
    for copy in copies:
        copy.start()
    for copy in copies:
        copy.wait()


def home_body(message_ref, out_ref, row_ref, base_ref, col_ref):
    count = row_ref.shape[0]
    geometry = geometry_of(message_ref.at[pl.ds(count, message_ref.shape[0] - count)])
    row_factors(geometry, base_ref, row_ref)
    column_factors(geometry, base_ref, col_ref)
    out_ref[...] = jnp.zeros_like(out_ref)
    tile_product(row_ref, col_ref, message_ref, out_ref)


def guest_body(has_total, n_held, n_later, row_ref, message_ref, *refs):
    refs = list(refs)
    del refs[: has_total + n_held]
    later = [refs.pop(0) for _ in range(n_later)]
    out_ref = refs.pop(0)
    del refs[:n_held]
    outs = [refs.pop(0) for _ in range(n_later)]
    base_ref, col_ref, directions_ref, geometry_ref, sems = refs
    part = min(COL_STEP, row_ref.shape[0])
    steps = row_ref.shape[0] // part

    def piece_copy(step):
        rows = pl.ds(pl.multiple_of(step * part, part), part)
        return pltpu.make_async_copy(message_ref.at[rows], directions_ref.at[rows], sems.at[step])

    copies = [
        geometry_copy(ref, geometry_ref.at[k], sems.at[steps + k]) for k, ref in enumerate([message_ref, *later])
    ]
    copies[0].start()
    for step in range(steps):
        piece_copy(step).start()
    for copy in copies[1:]:
        copy.start()
    copies[0].wait()
    column_factors(geometry_of(geometry_ref.at[0]), base_ref, col_ref)
    if not has_total:
        out_ref[...] = jnp.zeros_like(out_ref)
    tile_product(row_ref, col_ref, directions_ref, out_ref, arrive=lambda step: piece_copy(step).wait())
    for k, factors in enumerate(outs):
        copies[k + 1].wait()
        column_factors(geometry_of(geometry_ref.at[k + 1]), base_ref, factors)


def piece_body(offset, last, row_ref, col_ref, message_ref, total_ref, out_ref, directions_ref, sem):
    width = directions_ref.shape[0]
    copy = pltpu.make_async_copy(message_ref.at[pl.ds(offset, width)], directions_ref, sem)
    copy.start()
    factor = col_ref[:, offset : offset + width]
    for low in range(0, row_ref.shape[0], PIECE_ROWS):
        rows = slice(low, low + PIECE_ROWS)
        inverse = jnp.dot(row_ref[rows, :], factor, preferred_element_type=jnp.float32)
        values = lax.rsqrt(inverse).astype(jnp.bfloat16)
        if low == 0:
            copy.wait()
        part = jnp.dot(values, directions_ref[...], preferred_element_type=jnp.float32)
        if last:
            out_ref[rows, :] = total_ref[rows, :] + part
        else:
            out_ref[rows, :] += part


def fold_body(core_ref, value_ref, crossed_ref, out_ref):
    first = core_ref[0] == 0

    @pl.when(first)
    def _():
        out_ref[...] = value_ref[...] + value_ref[...].T

    @pl.when(jnp.logical_not(first))
    def _():
        out_ref[...] = value_ref[...] + crossed_ref[...].T


def half_gram_body(
    core_ref, own_ref, pair_ref, first_ref, second_ref, keep_ref, give_ref, sum_ref, directions_ref, sems
):
    copies = [
        pltpu.make_async_copy(ref, directions_ref.at[k], sems.at[k]) for k, ref in enumerate((own_ref, pair_ref))
    ]
    for copy in copies:
        copy.start()
    first, second = first_ref[...], second_ref[...]
    value = 0.5 * first + second
    sum_ref[...] = first + second
    high = value.astype(jnp.bfloat16)
    low = (value - high.astype(jnp.float32)).astype(jnp.bfloat16)
    both = jnp.concatenate([high, low], axis=1)
    blocks = []
    for k, copy in enumerate(copies):
        copy.wait()
        part = lax.dot_general(
            directions_ref[k], both, (((0,), (0,)), ((), ())), preferred_element_type=jnp.float32
        )
        blocks.append(part[:, :LANES] + part[:, LANES:])
    on_first = core_ref[0] == 0
    keep_ref[...] = jnp.where(on_first, blocks[0], blocks[1])
    give_ref[...] = jnp.where(on_first, blocks[1], blocks[0])


def tile_cost(count):
    return pl.CostEstimate(flops=count * count * 16, bytes_accessed=0, transcendentals=0)


def kernel_call(body, name, operands, places, outs, scratch, cost, aliases=None):
    spaces = {"v": pltpu.VMEM, "s": pltpu.SMEM, "a": pl.ANY, "h": pltpu.HBM}
    fixed = {"v": pltpu.VMEM, "h": pltpu.HBM}
    operands = [
        pltpu.with_memory_space_constraint(value, fixed[place]) if place in fixed else value
        for value, place in zip(operands, places)
    ]
    return pl.pallas_call(
        body,
        out_shape=outs,
        in_specs=[pl.BlockSpec(memory_space=spaces[place]) for place in places],
        out_specs=[pl.BlockSpec(memory_space=pltpu.VMEM)] * len(outs),
        input_output_aliases=aliases or {},
        scratch_shapes=scratch,
        cost_estimate=cost,
        compiler_params=pltpu.CompilerParams(vmem_limit_bytes=VMEM_BYTES),
        name=name,
    )(*operands)


def pack(directions, geometry):
    count = directions.shape[0]
    out = (count + sum(part.shape[0] for part in geometry), LANES)
    return kernel_call(
        pack_body, "pack", [directions, *geometry], "hhhh", [pltpu.VMEM(out, jnp.bfloat16)],
        [pltpu.SemaphoreType.DMA((COPIES + 3,))], pl.CostEstimate(flops=0, bytes_accessed=2**20, transcendentals=0),
    )[0]


def tile_scratch(count):
    return [pltpu.VMEM((8, count), jnp.float32), pltpu.VMEM((48, count), jnp.bfloat16)]


def home_tile(message, count):
    outs = [pltpu.VMEM((count, LANES), jnp.float32), pltpu.VMEM((count, 48), jnp.bfloat16)]
    return kernel_call(home_body, "home_tile", [message], "v", outs, tile_scratch(count), tile_cost(count))


def guest_tile(rows, message, total=None, held=(), later=(), place="h"):
    count = rows.shape[0]
    totals = [] if total is None else [total]
    scratch = tile_scratch(count) + [
        pltpu.VMEM((count, LANES), jnp.bfloat16),
        pltpu.VMEM((1 + len(later), message.shape[0] - count, LANES), jnp.bfloat16),
        pltpu.SemaphoreType.DMA((count // min(COL_STEP, count) + 1 + len(later),)),
    ]
    outs = [pltpu.VMEM((count, LANES), jnp.float32)] * (1 + len(held))
    outs += [pltpu.VMEM((48, count), jnp.bfloat16)] * len(later)
    aliases = {2: 0} if totals else {}
    aliases.update({2 + len(totals) + k: 1 + k for k in range(len(held))})
    return kernel_call(
        functools.partial(guest_body, len(totals), len(held), len(later)), "guest_tile",
        [rows, message, *totals, *held, *later],
        "v" + place + "v" * (len(totals) + len(held)) + "h" * len(later),
        outs, scratch, tile_cost(count), aliases,
    )


def piece_tile(rows, guest, total, piece, last):
    count = rows.shape[0]
    message, factors = guest
    width = count // PIECES
    out = jax.ShapeDtypeStruct if last else pltpu.VMEM
    return kernel_call(
        functools.partial(piece_body, piece * width, last), "piece_tile", [rows, factors, message, total], "vvhv",
        [out((count, LANES), jnp.float32)], [pltpu.VMEM((width, LANES), jnp.bfloat16), pltpu.SemaphoreType.DMA],
        tile_cost(count), None if last else {3: 0},
    )[0]


def half_gram(core, own, pair, first, second):
    count = first.shape[0]
    block = pltpu.VMEM((LANES, LANES), jnp.float32)
    return kernel_call(
        half_gram_body, "half_gram", [core, own, pair, first, second], "shhvv",
        [block, block, pltpu.VMEM((count, LANES), jnp.float32)],
        [pltpu.VMEM((2, count, LANES), jnp.bfloat16), pltpu.SemaphoreType.DMA((2,))], tile_cost(count), {3: 2},
    )


def fold(core, value, crossed):
    out = pltpu.VMEM((LANES, LANES), jnp.float32)
    cost = pl.CostEstimate(flops=0, bytes_accessed=2**17, transcendentals=0)
    return kernel_call(fold_body, "fold", [core, value, crossed], "svv", [out], [], cost)[0]


def along_blk(value, sizes, target):
    ny, nx, nz, nc = sizes

    def index(y, x, z, c):
        return ((y % ny * nx + x % nx) * nz + z % nz) * nc + c % nc

    pairs = []
    for y in range(ny):
        for x in range(nx):
            for z in range(nz):
                for c in range(nc):
                    pairs.append((index(y, x, z, c), index(*target(y, x, z, c))))
    return lax.ppermute(value, BLK, pairs)


def from_neighbour(value, parity):
    count = lax.axis_size(BLK)
    pairs = []
    for block in range(count):
        chip, core = divmod(block, 2)
        first = chip % 2 == parity
        other = 2 * (chip + 1) + 1 - core if first else 2 * (chip - 1) + core
        pairs.append((block, other % count))
    return lax.ppermute(value, BLK, pairs)


def from_far(value):
    count = lax.axis_size(BLK)
    return lax.ppermute(
        value, BLK, [(b, (b - 3 if b % 2 == 0 else b + 3) % count) for b in range(count)]
    )


def core_swap(value):
    return lax.ppermute(value, "core", [(0, 1), (1, 0)])


def shards(sizes, directions, axial_pos, azimuth, panel_area):
    count = axial_pos.shape[0]
    geometry = [part.reshape(count // LANES, LANES) for part in (axial_pos, azimuth, panel_area)]
    message = pack(directions, geometry)
    other = core_swap(message)
    even = from_neighbour(message, 0)
    odd = from_neighbour(message, 1)

    first, rows = home_tile(message, count)
    first, late = lax.optimization_barrier((first, message))
    far = from_far(late)
    (first,) = guest_tile(rows, other, first, place="a")
    first, even, later = lax.optimization_barrier((first, even, directions))
    pair = lax.ppermute(later, "rhs", [(0, 1), (1, 0)])
    even_other = core_swap(even)
    second, first = guest_tile(rows, even, None, (first,), place="a")
    second, odd = lax.optimization_barrier((second, odd))
    odd_other = core_swap(odd)
    second, first = guest_tile(rows, odd, second, (first,))
    second, far = lax.optimization_barrier((second, far))
    first, second, *factors = guest_tile(rows, far, first, (second,), (even_other, odd_other))
    core = lax.axis_index("core").astype(jnp.int32)
    keep, give, product = half_gram(core.reshape(1), directions, pair, first, second)

    value = keep + core_swap(give)
    value, product = lax.optimization_barrier((value, product))
    crossed = lax.ppermute(value, ("core", "rhs"), [(2, 3), (3, 2)])
    work = [(guest, piece) for guest in zip((even_other, odd_other), factors) for piece in range(PIECES)]

    def advance(product):
        guest, piece = work.pop(0)
        return piece_tile(rows, guest, product, piece, not work)

    product = advance(product)
    value, crossed, product = lax.optimization_barrier((value, crossed, product))
    value = fold(core.reshape(1), value, crossed)

    stages = (
        ((0, 0, 4), 2), ((0, 0, 2), 1), ((0, 0, 1), 1), ((2, 0, 0), 1), ((1, 0, 0), 1), ((0, 1, 0), 1),
    )
    for move, pieces in stages:
        sent = value.astype(jnp.bfloat16)
        value, product, sent = lax.optimization_barrier((value, product, sent))
        moved = along_blk(
            sent, sizes, lambda y, x, z, c, d=move: (y + d[0], x + d[1], z + d[2], c)
        )
        for _ in range(pieces):
            product = advance(product)
        sent, product, moved = lax.optimization_barrier((sent, product, moved))
        value = sent.astype(jnp.float32) + moved.astype(jnp.float32)
    value = value / (count * lax.axis_size(BLK))
    swapped = core_swap(value)
    upper = core == lax.axis_index("rhs")
    gram = jnp.concatenate([jnp.where(upper, value, swapped), jnp.where(upper, swapped, value)], axis=0)
    return product, gram


def solution(mesh):
    sizes = (4, 2, 8, 2)
    fine = Mesh(mesh.devices.reshape(sizes + (2,)), BLK + ("rhs",))
    in_specs = (P(BLK, "rhs"), P(BLK), P(BLK), P(BLK))
    out_specs = (P(BLK, "rhs"), P(None, "rhs"))
    return jax.shard_map(
        functools.partial(shards, sizes), mesh=fine, in_specs=in_specs, out_specs=out_specs, check_vma=False
    )
```

time: 99.9 us -> 92.7 us (0.928)
  local copies, waits for them, and re-layouts: 5.71 us -> 0 us
  starting transfers between devices: 34.4 us -> 32.8 us
  Pallas kernels: 44.8 us -> 46.1 us
    unnamed x19 -> x0, local copies, waits for them, and re-layouts: 5.53 us -> none
    ppermute x6, waiting for transfers between devices: 10.4 us -> 7.39 us  [along_blk(): return lax.ppermute(value, BLK, pairs)]
    ppermute x5, starting transfers between devices: 13.1 us -> 11.7 us  [core_swap(): return lax.ppermute(value, 'core', [(0, 1), (1, 0)])]
    pallas_call x15 -> x16, Pallas kernels: 44.8 us -> 46.1 us  [kernel_call(): pl.pallas_call(body, out_shape=outs, in_specs=[pl.BlockSpec(memory_space=...]
  transfers between devices with their start and end apart: 16 -> 16, of which waited for: 8 -> 9; matrix products, arithmetic and copies ran while one was open for 1% -> 0% of each run, Pallas kernels for 42% -> 47%
where the time goes in v2:
time: 92.7 us; the launch traced here: 92.3 us
  Pallas kernels  46.1 us (50%)
  starting transfers between devices  32.8 us (35%)
  waiting for transfers between devices  11.7 us (13%)
    pallas_call x16, Pallas kernels, kernel_call(): pl.pallas_call(body, out_shape=outs, in_specs=[pl.BlockSpec(memory_space=...  46.1 us
    ppermute x5, starting transfers between devices, core_swap(): return lax.ppermute(value, 'core', [(0, 1), (1, 0)])  11.7 us
    ppermute x2, starting transfers between devices, from_neighbour(): return lax.ppermute(value, BLK, pairs)  9.49 us
    ppermute x6, starting transfers between devices, along_blk(): return lax.ppermute(value, BLK, pairs)  8.99 us
    ppermute x6, waiting for transfers between devices, along_blk(): return lax.ppermute(value, BLK, pairs)  7.39 us
    ppermute x1, starting transfers between devices, shards(): crossed = lax.ppermute(value, ('core', 'rhs'), [(2, 3), (3, 2)])  2.21 us
  transfers between devices with their start and end apart: 16, of which 9 were waited for; matrix products, arithmetic and copies ran while one was open for 0% of the time, Pallas kernels for 47%

profile of v2, /device:TPU:1, one launch (start us, length us, event | category | flops | bytes accessed | tf_op | source)
XLA Modules:
  0.0 92.3 jit_solution(11284224911831493044)
XLA Ops:
  1.8 3.3 %collective-permute-start = (bf16[2096,128]{1,0:T(8,128)(2,1)S(1)}, bf16[2096,128]{1,0:T(8,128)(2,1)S(1)}, u32[]{:S(2)}, u32[]{:S(2)}) collective-permute-start(bf16[2096,128]{1,0:T(8,128)(2,1)S(1)} %pack.1.message_ref), channel_id=1, source_target_pairs={{0,2},{2,0},{1,3},{3,1},{4,6},{6,4},{5,7},{7,5},{8,10},{10,8},{9,1... | collective-permute-start | bytes 1609736 | tf_op jit(solution)/shard_map/ppermute | solution.py:335
  5.1 9.5 %collective-permute-start.3 = (bf16[2096,128]{1,0:T(8,128)(2,1)S(1)}, bf16[2096,128]{1,0:T(8,128)(2,1)}, u32[]{:S(2)}, u32[]{:S(2)}) collective-permute-start(bf16[2096,128]{1,0:T(8,128)(2,1)S(1)} %pack.1.message_ref), channel_id=1, source_target_pairs={{0,252},{2,254},{4,10},{6,8},{8,4},{10,6},{12,18},{14,16},{16,12},... | collective-permute-start | bytes 1609736 | tf_op jit(solution)/shard_map/ppermute | solution.py:324
  14.6 4.9 %home_tile.1 = (f32[2048,128]{1,0:T(8,128)S(1)}, bf16[2048,48]{1,0:T(8,128)(2,1)S(1)}) custom-call(bf16[2096,128]{1,0:T(8,128)(2,1)S(1)} %pack.1.message_ref), custom_call_target="tpu_custom_call" | custom-call | flops 67108864 | tf_op jit(solution)/shard_map/home_tile/pallas_call | solution.py:222
  19.7 4.8 %guest_tile.4.refs_0_ = f32[2048,128]{1,0:T(8,128)S(1)} custom-call(bf16[2048,48]{1,0:T(8,128)(2,1)S(1)} %get-tuple-element.59.row_ref, bf16[2096,128]{1,0:T(8,128)(2,1)S(1)} %collective-permute-done.message_ref, f32[2048,128]{1,0:T(8,128)S(1)} %get-tuple-element.61.refs_0_), custom_call_target="tpu_custom_call", output_to_operand_aliasing={{}: (2, {})} | custom-call | flops 67108864 | tf_op jit(solution)/shard_map/guest_tile/pallas_call | solution.py:222
  24.5 5.6 %guest_tile.5 = (f32[2048,128]{1,0:T(8,128)S(1)}, f32[2048,128]{1,0:T(8,128)S(1)}) custom-call(bf16[2048,48]{1,0:T(8,128)(2,1)S(1)} %get-tuple-element.59.row_ref, bf16[2096,128]{1,0:T(8,128)(2,1)} %collective-permute-done.1.message_ref, f32[2048,128]{1,0:T(8,128)S(1)} %guest_tile.4.refs_0_), custom_call_target="tpu_custom_call", output_to_operand_aliasing={{1}: (2, {})} | custom-call | flops 67108864 | tf_op jit(solution)/shard_map/guest_tile/pallas_call | solution.py:222
  32.2 5.6 %guest_tile.6 = (f32[2048,128]{1,0:T(8,128)S(1)}, f32[2048,128]{1,0:T(8,128)S(1)}) custom-call(bf16[2048,48]{1,0:T(8,128)(2,1)S(1)} %get-tuple-element.59.row_ref, bf16[2096,128]{1,0:T(8,128)(2,1)} %collective-permute-done.3.message_ref, f32[2048,128]{1,0:T(8,128)S(1)} %get-tuple-element.67.refs_0_, ...), custom_call_target="tpu_custom_call", output_to_operand_aliasing={{0}: (2, {}), {1}: (3, {})} | custom-call | flops 67108864 | tf_op jit(solution)/shard_map/guest_tile/pallas_call | solution.py:222
  37.8 5.8 %guest_tile.7 = (f32[2048,128]{1,0:T(8,128)S(1)}, f32[2048,128]{1,0:T(8,128)S(1)}, bf16[48,2048]{1,0:T(8,128)(2,1)S(1)}, bf16[48,2048]{1,0:T(8,128)(2,1)S(1)}) custom-call(bf16[2048,48]{1,0:T(8,128)(2,1)S(1)} %get-tuple-element.59.row_ref, bf16[2096,128]{1,0:T(8,128)(2,1)} %collective-permute-done.4.message_ref, ...), custom_call_target="tpu_custom_call", output_to_operand_aliasing={{0}: (2, {}), {1}: (3, {})} | custom-call | flops 67108864 | tf_op jit(solution)/shard_map/guest_tile/pallas_call | solution.py:222
  45.3 1.9 %half_gram.1 = (f32[128,128]{1,0:T(8,128)S(1)}, f32[128,128]{1,0:T(8,128)S(1)}, f32[2048,128]{1,0:T(8,128)S(1)}) custom-call(s32[1]{0:T(128)} %bitcast.core_ref, bf16[2048,128]{1,0:T(8,128)(2,1)} %own_ref.1, bf16[2048,128]{1,0:T(8,128)(2,1)} %collective-permute-done.2.pair_ref, ...), custom_call_target="tpu_custom_call", output_to_operand_aliasing={{2}: (3, {})} | custom-call | flops 67108864 | tf_op jit(solution)/shard_map/half_gram/pallas_call | solution.py:222
  47.2 2.3 %collective-permute-start.7 = (f32[128,128]{1,0:T(8,128)S(1)}, f32[128,128]{1,0:T(8,128)S(1)}, u32[]{:S(2)}, u32[]{:S(2)}) collective-permute-start(f32[128,128]{1,0:T(8,128)S(1)} %get-tuple-element.77), channel_id=1, source_target_pairs={{0,2},{2,0},{1,3},{3,1},{4,6},{6,4},{5,7},{7,5},{8,10},{10,8},{9,1... | collective-permute-start | bytes 196616 | tf_op jit(solution)/shard_map/ppermute | solution.py:335
  50.4 2.2 %collective-permute-start.8 = (f32[128,128]{1,0:T(8,128)S(1)}, f32[128,128]{1,0:T(8,128)S(1)}, u32[]{:S(2)}, u32[]{:S(2)}) collective-permute-start(f32[128,128]{1,0:T(8,128)S(1)} %add.21.value_ref), channel_id=1, source_target_pairs={{2,3},{3,2},{6,7},{7,6},{10,11},{11,10},{14,15},{15,14},{18,19},{1... | collective-permute-start | bytes 196616 | tf_op jit(solution)/shard_map/ppermute | solution.py:364
  52.7 1.9 %piece_tile.8.total_ref = f32[2048,128]{1,0:T(8,128)S(1)} custom-call(bf16[2048,48]{1,0:T(8,128)(2,1)S(1)} %get-tuple-element.59.row_ref, bf16[48,2048]{1,0:T(8,128)(2,1)S(1)} %get-tuple-element.80.col_ref, bf16[2096,128]{1,0:T(8,128)(2,1)} %collective-permute-done.5.refs_2_.message_ref, ...), custom_call_target="tpu_custom_call", output_to_operand_aliasing={{}: (3, {})} | custom-call | flops 67108864 | tf_op jit(solution)/shard_map/piece_tile/pallas_call | solution.py:222
  55.9 1.9 %piece_tile.9.total_ref = f32[2048,128]{1,0:T(8,128)S(1)} custom-call(bf16[2048,48]{1,0:T(8,128)(2,1)S(1)} %get-tuple-element.59.row_ref, bf16[48,2048]{1,0:T(8,128)(2,1)S(1)} %get-tuple-element.80.col_ref, bf16[2096,128]{1,0:T(8,128)(2,1)} %collective-permute-done.5.refs_2_.message_ref, ...), custom_call_target="tpu_custom_call", output_to_operand_aliasing={{}: (3, {})} | custom-call | flops 67108864 | tf_op jit(solution)/shard_map/piece_tile/pallas_call | solution.py:222
  57.8 1.9 %piece_tile.10.total_ref = f32[2048,128]{1,0:T(8,128)S(1)} custom-call(bf16[2048,48]{1,0:T(8,128)(2,1)S(1)} %get-tuple-element.59.row_ref, bf16[48,2048]{1,0:T(8,128)(2,1)S(1)} %get-tuple-element.80.col_ref, bf16[2096,128]{1,0:T(8,128)(2,1)} %collective-permute-done.5.refs_2_.message_ref, ...), custom_call_target="tpu_custom_call", output_to_operand_aliasing={{}: (3, {})} | custom-call | flops 67108864 | tf_op jit(solution)/shard_map/piece_tile/pallas_call | solution.py:222
  59.7 2.7 %collective-permute-done.9 = bf16[128,128]{1,0:T(8,128)(2,1)S(1)} collective-permute-done((bf16[128,128]{1,0:T(8,128)(2,1)S(1)}, bf16[128,128]{1,0:T(8,128)(2,1)S(1)}, u32[]{:S(2)}, u32[]{:S(2)}) %collective-permute-start.9) | collective-permute-done | bytes 32800 | tf_op jit(solution)/shard_map/ppermute | solution.py:313
  62.4 4.6 %collective-permute-start.10 = (bf16[128,128]{1,0:T(8,128)(2,1)S(1)}, bf16[128,128]{1,0:T(8,128)(2,1)S(1)}, u32[]{:S(2)}, u32[]{:S(2)}) collective-permute-start(bf16[128,128]{1,0:T(8,128)(2,1)S(1)} %fusion), channel_id=1, source_target_pairs={{0,8},{2,10},{4,12},{6,14},{8,16},{10,18},{12,20},{14,22},{16,24},... | collective-permute-start | bytes 98312 | tf_op jit(solution)/shard_map/ppermute | solution.py:313
  67.1 1.9 %piece_tile.11.total_ref = f32[2048,128]{1,0:T(8,128)S(1)} custom-call(bf16[2048,48]{1,0:T(8,128)(2,1)S(1)} %get-tuple-element.59.row_ref, bf16[48,2048]{1,0:T(8,128)(2,1)S(1)} %get-tuple-element.80.col_ref, bf16[2096,128]{1,0:T(8,128)(2,1)} %collective-permute-done.5.refs_2_.message_ref, ...), custom_call_target="tpu_custom_call", output_to_operand_aliasing={{}: (3, {})} | custom-call | flops 67108864 | tf_op jit(solution)/shard_map/piece_tile/pallas_call | solution.py:222
  69.3 1.9 %piece_tile.12.total_ref = f32[2048,128]{1,0:T(8,128)S(1)} custom-call(bf16[2048,48]{1,0:T(8,128)(2,1)S(1)} %get-tuple-element.59.row_ref, bf16[48,2048]{1,0:T(8,128)(2,1)S(1)} %get-tuple-element.96.col_ref, bf16[2096,128]{1,0:T(8,128)(2,1)} %collective-permute-done.6.refs_3_.message_ref, ...), custom_call_target="tpu_custom_call", output_to_operand_aliasing={{}: (3, {})} | custom-call | flops 67108864 | tf_op jit(solution)/shard_map/piece_tile/pallas_call | solution.py:222
  71.2 2.1 %collective-permute-done.11 = bf16[128,128]{1,0:T(8,128)(2,1)S(1)} collective-permute-done((bf16[128,128]{1,0:T(8,128)(2,1)S(1)}, bf16[128,128]{1,0:T(8,128)(2,1)S(1)}, u32[]{:S(2)}, u32[]{:S(2)}) %collective-permute-start.11) | collective-permute-done | bytes 32800 | tf_op jit(solution)/shard_map/ppermute | solution.py:313
  73.3 1.9 %collective-permute-start.12 = (bf16[128,128]{1,0:T(8,128)(2,1)S(1)}, bf16[128,128]{1,0:T(8,128)(2,1)S(1)}, u32[]{:S(2)}, u32[]{:S(2)}) collective-permute-start(bf16[128,128]{1,0:T(8,128)(2,1)S(1)} %fusion.2), channel_id=1, source_target_pairs={{0,128},{2,130},{4,132},{6,134},{8,136},{10,138},{12,140},{14,142}... | collective-permute-start | bytes 98312 | tf_op jit(solution)/shard_map/ppermute | solution.py:313
  75.2 1.9 %piece_tile.13.total_ref = f32[2048,128]{1,0:T(8,128)S(1)} custom-call(bf16[2048,48]{1,0:T(8,128)(2,1)S(1)} %get-tuple-element.59.row_ref, bf16[48,2048]{1,0:T(8,128)(2,1)S(1)} %get-tuple-element.96.col_ref, bf16[2096,128]{1,0:T(8,128)(2,1)} %collective-permute-done.6.refs_3_.message_ref, ...), custom_call_target="tpu_custom_call", output_to_operand_aliasing={{}: (3, {})} | custom-call | flops 67108864 | tf_op jit(solution)/shard_map/piece_tile/pallas_call | solution.py:222
  77.9 1.9 %piece_tile.14.total_ref = f32[2048,128]{1,0:T(8,128)S(1)} custom-call(bf16[2048,48]{1,0:T(8,128)(2,1)S(1)} %get-tuple-element.59.row_ref, bf16[48,2048]{1,0:T(8,128)(2,1)S(1)} %get-tuple-element.96.col_ref, bf16[2096,128]{1,0:T(8,128)(2,1)} %collective-permute-done.6.refs_3_.message_ref, ...), custom_call_target="tpu_custom_call", output_to_operand_aliasing={{}: (3, {})} | custom-call | flops 67108864 | tf_op jit(solution)/shard_map/piece_tile/pallas_call | solution.py:222
  79.8 1.9 %collective-permute-done.13 = bf16[128,128]{1,0:T(8,128)(2,1)S(1)} collective-permute-done((bf16[128,128]{1,0:T(8,128)(2,1)S(1)}, bf16[128,128]{1,0:T(8,128)(2,1)S(1)}, u32[]{:S(2)}, u32[]{:S(2)}) %collective-permute-start.13) | collective-permute-done | bytes 32800 | tf_op jit(solution)/shard_map/ppermute | solution.py:313
  83.5 2.9 %piece_tile.15 = f32[2048,128]{1,0:T(8,128)} custom-call(bf16[2048,48]{1,0:T(8,128)(2,1)S(1)} %get-tuple-element.59.row_ref, bf16[48,2048]{1,0:T(8,128)(2,1)S(1)} %get-tuple-element.96.col_ref, bf16[2096,128]{1,0:T(8,128)(2,1)} %collective-permute-done.6.refs_3_.message_ref, f32[2048,128]{1,0:T(8,128)S(1)} %piece_tile.14.total_ref), custom_call_target="tpu_custom_call" | custom-call | flops 67108864 | tf_op jit(solution)/shard_map/piece_tile/pallas_call | solution.py:222
  86.4 4.3 %collective-permute-start.15 = (f32[128,128]{1,0:T(8,128)S(1)}, f32[128,128]{1,0:T(8,128)S(1)}, u32[]{:S(2)}, u32[]{:S(2)}) collective-permute-start(f32[128,128]{1,0:T(8,128)S(1)} %add_multiply_fusion), channel_id=1, source_target_pairs={{0,2},{2,0},{1,3},{3,1},{4,6},{6,4},{5,7},{7,5},{8,10},{10,8},{9,1... | collective-permute-start | bytes 196616 | tf_op jit(solution)/shard_map/ppermute | solution.py:335
  (34 shorter events, 11.7 us)
Async XLA Ops:
  1.8 17.8 %collective-permute-start = (bf16[2096,128]{1,0:T(8,128)(2,1)S(1)}, bf16[2096,128]{1,0:T(8,128)(2,1)S(1)}, u32[]{:S(2)}, u32[]{:S(2)}) collective-permute-start(bf16[2096,128]{1,0:T(8,128)(2,1)S(1)} %pack.1.message_ref), channel_id=1, source_target_pairs={{0,2},{2,0},{1,3},{3,1},{4,6},{6,4},{5,7},{7,5},{8,10},{10,8},{9,1... | collective-permute-start | bytes 1609736 | tf_op jit(solution)/shard_map/ppermute | solution.py:335
  5.1 19.3 %collective-permute-start.1 = (bf16[2096,128]{1,0:T(8,128)(2,1)S(1)}, bf16[2096,128]{1,0:T(8,128)(2,1)}, u32[]{:S(2)}, u32[]{:S(2)}) collective-permute-start(bf16[2096,128]{1,0:T(8,128)(2,1)S(1)} %pack.1.message_ref), channel_id=1, source_target_pairs={{0,6},{2,4},{4,0},{6,2},{8,14},{10,12},{12,8},{14,10},{16,22},{18,... | collective-permute-start | bytes 1609736 | tf_op jit(solution)/shard_map/ppermute | solution.py:324
  5.1 25.0 %collective-permute-start.3 = (bf16[2096,128]{1,0:T(8,128)(2,1)S(1)}, bf16[2096,128]{1,0:T(8,128)(2,1)}, u32[]{:S(2)}, u32[]{:S(2)}) collective-permute-start(bf16[2096,128]{1,0:T(8,128)(2,1)S(1)} %pack.1.message_ref), channel_id=1, source_target_pairs={{0,252},{2,254},{4,10},{6,8},{8,4},{10,6},{12,18},{14,16},{16,12},... | collective-permute-start | bytes 1609736 | tf_op jit(solution)/shard_map/ppermute | solution.py:324
  19.5 18.3 %collective-permute-start.4 = (bf16[2096,128]{1,0:T(8,128)(2,1)S(1)}, bf16[2096,128]{1,0:T(8,128)(2,1)}, u32[]{:S(2)}, u32[]{:S(2)}) collective-permute-start(bf16[2096,128]{1,0:T(8,128)(2,1)S(1)} %pack.1.message_ref), channel_id=1, source_target_pairs={{0,250},{2,8},{4,254},{6,12},{8,2},{10,16},{12,6},{14,20},{16,10},... | collective-permute-start | bytes 1609736 | tf_op jit(solution)/shard_map/ppermute | solution.py:329
  30.1 7.7 %collective-permute-start.6 = (bf16[2096,128]{1,0:T(8,128)(2,1)}, bf16[2096,128]{1,0:T(8,128)(2,1)}, u32[]{:S(2)}, u32[]{:S(2)}) collective-permute-start(bf16[2096,128]{1,0:T(8,128)(2,1)} %collective-permute-done.3.message_ref), channel_id=1, source_target_pairs={{0,2},{2,0},{1,3},{3,1},{4,6},{6,4},{5,7},{7,5},{8,10},{10,8},{9,1... | collective-permute-start | bytes 1609736 | tf_op jit(solution)/shard_map/ppermute | solution.py:335
  31.8 6.1 %collective-permute-start.5 = (bf16[2096,128]{1,0:T(8,128)(2,1)}, bf16[2096,128]{1,0:T(8,128)(2,1)}, u32[]{:S(2)}, u32[]{:S(2)}) collective-permute-start(bf16[2096,128]{1,0:T(8,128)(2,1)} %collective-permute-done.1.message_ref), channel_id=1, source_target_pairs={{0,2},{2,0},{1,3},{3,1},{4,6},{6,4},{5,7},{7,5},{8,10},{10,8},{9,1... | collective-permute-start | bytes 1609736 | tf_op jit(solution)/shard_map/ppermute | solution.py:335
  31.9 13.4 %collective-permute-start.2 = (bf16[2048,128]{1,0:T(8,128)(2,1)}, bf16[2048,128]{1,0:T(8,128)(2,1)}, u32[]{:S(2)}, u32[]{:S(2)}) collective-permute-start(bf16[2048,128]{1,0:T(8,128)(2,1)} %own_ref.1), channel_id=1, source_target_pairs={{0,1},{1,0},{2,3},{3,2},{4,5},{5,4},{6,7},{7,6},{8,9},{9,8},{10,11... | collective-permute-start | bytes 1572872 | tf_op jit(solution)/shard_map/ppermute | solution.py:351
  47.2 3.2 %collective-permute-start.7 = (f32[128,128]{1,0:T(8,128)S(1)}, f32[128,128]{1,0:T(8,128)S(1)}, u32[]{:S(2)}, u32[]{:S(2)}) collective-permute-start(f32[128,128]{1,0:T(8,128)S(1)} %get-tuple-element.77), channel_id=1, source_target_pairs={{0,2},{2,0},{1,3},{3,1},{4,6},{6,4},{5,7},{7,5},{8,10},{10,8},{9,1... | collective-permute-start | bytes 196616 | tf_op jit(solution)/shard_map/ppermute | solution.py:335
  50.4 5.0 %collective-permute-start.8 = (f32[128,128]{1,0:T(8,128)S(1)}, f32[128,128]{1,0:T(8,128)S(1)}, u32[]{:S(2)}, u32[]{:S(2)}) collective-permute-start(f32[128,128]{1,0:T(8,128)S(1)} %add.21.value_ref), channel_id=1, source_target_pairs={{2,3},{3,2},{6,7},{7,6},{10,11},{11,10},{14,15},{15,14},{18,19},{1... | collective-permute-start | bytes 196616 | tf_op jit(solution)/shard_map/ppermute | solution.py:364
  55.6 6.9 %collective-permute-start.9 = (bf16[128,128]{1,0:T(8,128)(2,1)S(1)}, bf16[128,128]{1,0:T(8,128)(2,1)S(1)}, u32[]{:S(2)}, u32[]{:S(2)}) collective-permute-start(bf16[128,128]{1,0:T(8,128)(2,1)S(1)} %convert_element_type.54), channel_id=1, source_target_pairs={{0,16},{2,18},{4,20},{6,22},{8,24},{10,26},{12,28},{14,30},{16,0},... | collective-permute-start | bytes 98312 | tf_op jit(solution)/shard_map/ppermute | solution.py:313
  62.4 6.8 %collective-permute-start.10 = (bf16[128,128]{1,0:T(8,128)(2,1)S(1)}, bf16[128,128]{1,0:T(8,128)(2,1)S(1)}, u32[]{:S(2)}, u32[]{:S(2)}) collective-permute-start(bf16[128,128]{1,0:T(8,128)(2,1)S(1)} %fusion), channel_id=1, source_target_pairs={{0,8},{2,10},{4,12},{6,14},{8,16},{10,18},{12,20},{14,22},{16,24},... | collective-permute-start | bytes 98312 | tf_op jit(solution)/shard_map/ppermute | solution.py:313
  69.2 4.1 %collective-permute-start.11 = (bf16[128,128]{1,0:T(8,128)(2,1)S(1)}, bf16[128,128]{1,0:T(8,128)(2,1)S(1)}, u32[]{:S(2)}, u32[]{:S(2)}) collective-permute-start(bf16[128,128]{1,0:T(8,128)(2,1)S(1)} %fusion.1), channel_id=1, source_target_pairs={{0,4},{2,6},{4,8},{6,10},{8,12},{10,14},{12,16},{14,18},{16,20},{1... | collective-permute-start | bytes 98312 | tf_op jit(solution)/shard_map/ppermute | solution.py:313
  73.3 4.4 %collective-permute-start.12 = (bf16[128,128]{1,0:T(8,128)(2,1)S(1)}, bf16[128,128]{1,0:T(8,128)(2,1)S(1)}, u32[]{:S(2)}, u32[]{:S(2)}) collective-permute-start(bf16[128,128]{1,0:T(8,128)(2,1)S(1)} %fusion.2), channel_id=1, source_target_pairs={{0,128},{2,130},{4,132},{6,134},{8,136},{10,138},{12,140},{14,142}... | collective-permute-start | bytes 98312 | tf_op jit(solution)/shard_map/ppermute | solution.py:313
  77.7 4.1 %collective-permute-start.13 = (bf16[128,128]{1,0:T(8,128)(2,1)S(1)}, bf16[128,128]{1,0:T(8,128)(2,1)S(1)}, u32[]{:S(2)}, u32[]{:S(2)}) collective-permute-start(bf16[128,128]{1,0:T(8,128)(2,1)S(1)} %fusion.3), channel_id=1, source_target_pairs={{0,64},{2,66},{4,68},{6,70},{8,72},{10,74},{12,76},{14,78},{16,80}... | collective-permute-start | bytes 98312 | tf_op jit(solution)/shard_map/ppermute | solution.py:313
  81.7 4.6 %collective-permute-start.14 = (bf16[128,128]{1,0:T(8,128)(2,1)S(1)}, bf16[128,128]{1,0:T(8,128)(2,1)S(1)}, u32[]{:S(2)}, u32[]{:S(2)}) collective-permute-start(bf16[128,128]{1,0:T(8,128)(2,1)S(1)} %fusion.4), channel_id=1, source_target_pairs={{0,32},{2,34},{4,36},{6,38},{8,40},{10,42},{12,44},{14,46},{16,48}... | collective-permute-start | bytes 98312 | tf_op jit(solution)/shard_map/ppermute | solution.py:313
  86.4 5.2 %collective-permute-start.15 = (f32[128,128]{1,0:T(8,128)S(1)}, f32[128,128]{1,0:T(8,128)S(1)}, u32[]{:S(2)}, u32[]{:S(2)}) collective-permute-start(f32[128,128]{1,0:T(8,128)S(1)} %add_multiply_fusion), channel_id=1, source_target_pairs={{0,2},{2,0},{1,3},{3,1},{4,6},{6,4},{5,7},{7,5},{8,10},{10,8},{9,1... | collective-permute-start | bytes 196616 | tf_op jit(solution)/shard_map/ppermute | solution.py:335

commit v3 on v2

--- a/solution.py
+++ b/solution.py
@@ -119,14 +119,9 @@
     tile_product(row_ref, col_ref, message_ref, out_ref)
 
 
-def guest_body(has_total, n_held, n_later, row_ref, message_ref, *refs):
-    refs = list(refs)
-    del refs[: has_total + n_held]
-    later = [refs.pop(0) for _ in range(n_later)]
-    out_ref = refs.pop(0)
-    del refs[:n_held]
-    outs = [refs.pop(0) for _ in range(n_later)]
-    base_ref, col_ref, directions_ref, geometry_ref, sems = refs
+def guest_body(has_total, n_held, row_ref, message_ref, *refs):
+    out_ref, *refs = refs[has_total + n_held :]
+    base_ref, col_ref, directions_ref, geometry_ref, sems = refs[n_held:]
     part = min(COL_STEP, row_ref.shape[0])
     steps = row_ref.shape[0] // part
 
@@ -134,32 +129,29 @@
         rows = pl.ds(pl.multiple_of(step * part, part), part)
         return pltpu.make_async_copy(message_ref.at[rows], directions_ref.at[rows], sems.at[step])
 
-    copies = [
-        geometry_copy(ref, geometry_ref.at[k], sems.at[steps + k]) for k, ref in enumerate([message_ref, *later])
-    ]
-    copies[0].start()
+    geometry = geometry_copy(message_ref, geometry_ref, sems.at[steps])
+    geometry.start()
     for step in range(steps):
         piece_copy(step).start()
-    for copy in copies[1:]:
-        copy.start()
-    copies[0].wait()
-    column_factors(geometry_of(geometry_ref.at[0]), base_ref, col_ref)
+    geometry.wait()
+    column_factors(geometry_of(geometry_ref), base_ref, col_ref)
     if not has_total:
         out_ref[...] = jnp.zeros_like(out_ref)
     tile_product(row_ref, col_ref, directions_ref, out_ref, arrive=lambda step: piece_copy(step).wait())
-    for k, factors in enumerate(outs):
-        copies[k + 1].wait()
-        column_factors(geometry_of(geometry_ref.at[k + 1]), base_ref, factors)
-
-
-def piece_body(offset, last, row_ref, col_ref, message_ref, total_ref, out_ref, directions_ref, sem):
+
+
+def piece_body(offset, last, row_ref, message_ref, total_ref, out_ref, base_ref, col_ref, directions_ref, geometry_ref, sems):
     width = directions_ref.shape[0]
-    copy = pltpu.make_async_copy(message_ref.at[pl.ds(offset, width)], directions_ref, sem)
+    geometry = geometry_copy(message_ref, geometry_ref, sems.at[0])
+    copy = pltpu.make_async_copy(message_ref.at[pl.ds(offset, width)], directions_ref, sems.at[1])
+    geometry.start()
     copy.start()
-    factor = col_ref[:, offset : offset + width]
+    geometry.wait()
+    part = slice(offset // LANES, (offset + width) // LANES)
+    column_factors([value[part] for value in geometry_of(geometry_ref)], base_ref, col_ref)
     for low in range(0, row_ref.shape[0], PIECE_ROWS):
         rows = slice(low, low + PIECE_ROWS)
-        inverse = jnp.dot(row_ref[rows, :], factor, preferred_element_type=jnp.float32)
+        inverse = jnp.dot(row_ref[rows, :], col_ref[...], preferred_element_type=jnp.float32)
         values = lax.rsqrt(inverse).astype(jnp.bfloat16)
         if low == 0:
             copy.wait()
@@ -170,16 +162,17 @@
             out_ref[rows, :] += part
 
 
-def fold_body(core_ref, value_ref, crossed_ref, out_ref):
+def fold_body(core_ref, keep_ref, swapped_ref, crossed_ref, far_crossed_ref, out_ref):
     first = core_ref[0] == 0
+    value = keep_ref[...] + swapped_ref[...]
 
     @pl.when(first)
     def _():
-        out_ref[...] = value_ref[...] + value_ref[...].T
+        out_ref[...] = value + value.T
 
     @pl.when(jnp.logical_not(first))
     def _():
-        out_ref[...] = value_ref[...] + crossed_ref[...].T
+        out_ref[...] = value + (crossed_ref[...] + far_crossed_ref[...]).T
 
 
 def half_gram_body(
@@ -250,35 +243,35 @@
     return kernel_call(home_body, "home_tile", [message], "v", outs, tile_scratch(count), tile_cost(count))
 
 
-def guest_tile(rows, message, total=None, held=(), later=(), place="h"):
+def guest_tile(rows, message, total=None, held=()):
     count = rows.shape[0]
     totals = [] if total is None else [total]
     scratch = tile_scratch(count) + [
         pltpu.VMEM((count, LANES), jnp.bfloat16),
-        pltpu.VMEM((1 + len(later), message.shape[0] - count, LANES), jnp.bfloat16),
-        pltpu.SemaphoreType.DMA((count // min(COL_STEP, count) + 1 + len(later),)),
-    ]
-    outs = [pltpu.VMEM((count, LANES), jnp.float32)] * (1 + len(held))
-    outs += [pltpu.VMEM((48, count), jnp.bfloat16)] * len(later)
+        pltpu.VMEM((message.shape[0] - count, LANES), jnp.bfloat16),
+        pltpu.SemaphoreType.DMA((count // min(COL_STEP, count) + 1,)),
+    ]
     aliases = {2: 0} if totals else {}
     aliases.update({2 + len(totals) + k: 1 + k for k in range(len(held))})
     return kernel_call(
-        functools.partial(guest_body, len(totals), len(held), len(later)), "guest_tile",
-        [rows, message, *totals, *held, *later],
-        "v" + place + "v" * (len(totals) + len(held)) + "h" * len(later),
-        outs, scratch, tile_cost(count), aliases,
-    )
-
-
-def piece_tile(rows, guest, total, piece, last):
+        functools.partial(guest_body, len(totals), len(held)), "guest_tile", [rows, message, *totals, *held],
+        "va" + "v" * (len(totals) + len(held)), [pltpu.VMEM((count, LANES), jnp.float32)] * (1 + len(held)),
+        scratch, tile_cost(count), aliases,
+    )
+
+
+def piece_tile(rows, message, total, piece, last):
     count = rows.shape[0]
-    message, factors = guest
     width = count // PIECES
     out = jax.ShapeDtypeStruct if last else pltpu.VMEM
+    scratch = tile_scratch(width) + [
+        pltpu.VMEM((width, LANES), jnp.bfloat16),
+        pltpu.VMEM((message.shape[0] - count, LANES), jnp.bfloat16),
+        pltpu.SemaphoreType.DMA((2,)),
+    ]
     return kernel_call(
-        functools.partial(piece_body, piece * width, last), "piece_tile", [rows, factors, message, total], "vvhv",
-        [out((count, LANES), jnp.float32)], [pltpu.VMEM((width, LANES), jnp.bfloat16), pltpu.SemaphoreType.DMA],
-        tile_cost(count), None if last else {3: 0},
+        functools.partial(piece_body, piece * width, last), "piece_tile", [rows, message, total], "vav",
+        [out((count, LANES), jnp.float32)], scratch, tile_cost(count), None if last else {2: 0},
     )[0]
 
 
@@ -286,16 +279,16 @@
     count = first.shape[0]
     block = pltpu.VMEM((LANES, LANES), jnp.float32)
     return kernel_call(
-        half_gram_body, "half_gram", [core, own, pair, first, second], "shhvv",
+        half_gram_body, "half_gram", [core, own, pair, first, second], "shavv",
         [block, block, pltpu.VMEM((count, LANES), jnp.float32)],
         [pltpu.VMEM((2, count, LANES), jnp.bfloat16), pltpu.SemaphoreType.DMA((2,))], tile_cost(count), {3: 2},
     )
 
 
-def fold(core, value, crossed):
+def fold(core, *blocks):
     out = pltpu.VMEM((LANES, LANES), jnp.float32)
     cost = pl.CostEstimate(flops=0, bytes_accessed=2**17, transcendentals=0)
-    return kernel_call(fold_body, "fold", [core, value, crossed], "svv", [out], [], cost)[0]
+    return kernel_call(fold_body, "fold", [core, *blocks], "svvvv", [out], [], cost)[0]
 
 
 def along_blk(value, sizes, target):
@@ -346,43 +339,36 @@
     first, rows = home_tile(message, count)
     first, late = lax.optimization_barrier((first, message))
     far = from_far(late)
-    (first,) = guest_tile(rows, other, first, place="a")
+    (first,) = guest_tile(rows, other, first)
     first, even, later = lax.optimization_barrier((first, even, directions))
     pair = lax.ppermute(later, "rhs", [(0, 1), (1, 0)])
     even_other = core_swap(even)
-    second, first = guest_tile(rows, even, None, (first,), place="a")
+    second, first = guest_tile(rows, even, None, (first,))
     second, odd = lax.optimization_barrier((second, odd))
     odd_other = core_swap(odd)
     second, first = guest_tile(rows, odd, second, (first,))
     second, far = lax.optimization_barrier((second, far))
-    first, second, *factors = guest_tile(rows, far, first, (second,), (even_other, odd_other))
+    first, second = guest_tile(rows, far, first, (second,))
     core = lax.axis_index("core").astype(jnp.int32)
     keep, give, product = half_gram(core.reshape(1), directions, pair, first, second)
 
-    value = keep + core_swap(give)
-    value, product = lax.optimization_barrier((value, product))
-    crossed = lax.ppermute(value, ("core", "rhs"), [(2, 3), (3, 2)])
-    work = [(guest, piece) for guest in zip((even_other, odd_other), factors) for piece in range(PIECES)]
-
-    def advance(product):
-        guest, piece = work.pop(0)
-        return piece_tile(rows, guest, product, piece, not work)
-
-    product = advance(product)
-    value, crossed, product = lax.optimization_barrier((value, crossed, product))
-    value = fold(core.reshape(1), value, crossed)
-
+    swapped = core_swap(give)
+    crossed = lax.ppermute(keep, ("core", "rhs"), [(2, 3), (3, 2)])
+    far_crossed = lax.ppermute(give, ("core", "rhs"), [(0, 3), (1, 2)])
+    value = fold(core.reshape(1), keep, swapped, crossed, far_crossed)
+
+    work = [(guest, piece) for guest in (even_other, odd_other) for piece in range(PIECES)]
     stages = (
-        ((0, 0, 4), 2), ((0, 0, 2), 1), ((0, 0, 1), 1), ((2, 0, 0), 1), ((1, 0, 0), 1), ((0, 1, 0), 1),
-    )
-    for move, pieces in stages:
-        sent = value.astype(jnp.bfloat16)
-        value, product, sent = lax.optimization_barrier((value, product, sent))
-        moved = along_blk(
-            sent, sizes, lambda y, x, z, c, d=move: (y + d[0], x + d[1], z + d[2], c)
-        )
+        ((0, 0, 4), 2, False), ((0, 0, 2), 2, True), ((0, 0, 1), 1, False),
+        ((2, 0, 0), 1, True), ((1, 0, 0), 1, False), ((0, 1, 0), 1, True),
+    )
+    for move, pieces, rounded in stages:
+        sent = value.astype(jnp.bfloat16) if rounded else value
+        product, sent = lax.optimization_barrier((product, sent))
+        moved = along_blk(sent, sizes, lambda y, x, z, c, d=move: (y ^ d[0], x ^ d[1], z ^ d[2], c))
         for _ in range(pieces):
-            product = advance(product)
+            guest, piece = work.pop(0)
+            product = piece_tile(rows, guest, product, piece, not work)
         sent, product, moved = lax.optimization_barrier((sent, product, moved))
         value = sent.astype(jnp.float32) + moved.astype(jnp.float32)
     value = value / (count * lax.axis_size(BLK))

time: 92.7 us -> 92.4 us (level)
  waiting for transfers between devices: 11.7 us -> 17 us
  Pallas kernels: 46.1 us -> 43.2 us
  starting transfers between devices: 32.8 us -> 30.2 us
    ppermute x6, starting transfers between devices: 8.99 us -> 0.59 us  [along_blk(): return lax.ppermute(value, BLK, pairs)]
    ppermute x5, starting transfers between devices: 11.7 us -> 16.2 us  [core_swap(): return lax.ppermute(value, 'core', [(0, 1), (1, 0)])]
    ppermute x6, waiting for transfers between devices: 7.39 us -> 11.8 us  [along_blk(): return lax.ppermute(value, BLK, pairs)]
    ppermute x1 -> x2, waiting for transfers between devices: 0.89 us -> 4.27 us  [the longest x1 2.8 us: shards(): far_crossed = lax.ppermute(give, ('core', 'rhs'), [(0, 3), (1, 2)])]
    pallas_call x16, Pallas kernels: 46.1 us -> 43.2 us  [kernel_call(): pl.pallas_call(body, out_shape=outs, in_specs=[pl.BlockSpec(memory_space=...]
    ppermute x1, waiting for transfers between devices: 1.59 us -> 0.01 us  [shards(): pair = lax.ppermute(later, 'rhs', [(0, 1), (1, 0)])]
    ppermute x1 -> x2, starting transfers between devices: 2.21 us -> 3.5 us  [the longest x1 2.2 us: shards(): crossed = lax.ppermute(keep, ('core', 'rhs'), [(2, 3), (3, 2)])]
  transfers between devices with their start and end apart: 16 -> 17, of which waited for: 9 -> 9; matrix products, arithmetic and copies ran while one was open for 0% -> 0% of each run, Pallas kernels for 47% -> 46%
where the time goes in v3:
time: 92.4 us; the launch traced here: 92.1 us
  Pallas kernels  43.2 us (47%)
  starting transfers between devices  30.2 us (33%)
  waiting for transfers between devices  17 us (18%)
    pallas_call x16, Pallas kernels, kernel_call(): pl.pallas_call(body, out_shape=outs, in_specs=[pl.BlockSpec(memory_space=...  43.2 us
    ppermute x5, starting transfers between devices, core_swap(): return lax.ppermute(value, 'core', [(0, 1), (1, 0)])  16.2 us
    ppermute x6, waiting for transfers between devices, along_blk(): return lax.ppermute(value, BLK, pairs)  11.8 us
    ppermute x2, starting transfers between devices, from_neighbour(): return lax.ppermute(value, BLK, pairs)  9.49 us
    ppermute x1, waiting for transfers between devices, shards(): far_crossed = lax.ppermute(give, ('core', 'rhs'), [(0, 3), (1, 2)])  2.8 us
    ppermute x1, starting transfers between devices, shards(): crossed = lax.ppermute(keep, ('core', 'rhs'), [(2, 3), (3, 2)])  2.2 us
  transfers between devices with their start and end apart: 17, of which 9 were waited for; matrix products, arithmetic and copies ran while one was open for 0% of the time, Pallas kernels for 46%

profile of v3, /device:TPU:1, one launch (start us, length us, event | category | flops | bytes accessed | tf_op | source)
XLA Modules:
  0.0 92.1 jit_solution(15959320642024713790)
XLA Ops:
  1.8 3.3 %collective-permute-start = (bf16[2096,128]{1,0:T(8,128)(2,1)S(1)}, bf16[2096,128]{1,0:T(8,128)(2,1)S(1)}, u32[]{:S(2)}, u32[]{:S(2)}) collective-permute-start(bf16[2096,128]{1,0:T(8,128)(2,1)S(1)} %pack.1.message_ref), channel_id=1, source_target_pairs={{0,2},{2,0},{1,3},{3,1},{4,6},{6,4},{5,7},{7,5},{8,10},{10,8},{9,1... | collective-permute-start | bytes 1609736 | tf_op jit(solution)/shard_map/ppermute | solution.py:328
  5.1 9.5 %collective-permute-start.3 = (bf16[2096,128]{1,0:T(8,128)(2,1)S(1)}, bf16[2096,128]{1,0:T(8,128)(2,1)S(1)}, u32[]{:S(2)}, u32[]{:S(2)}) collective-permute-start(bf16[2096,128]{1,0:T(8,128)(2,1)S(1)} %pack.1.message_ref), channel_id=1, source_target_pairs={{0,252},{2,254},{4,10},{6,8},{8,4},{10,6},{12,18},{14,16},{16,12},... | collective-permute-start | bytes 1609736 | tf_op jit(solution)/shard_map/ppermute | solution.py:317
  14.6 4.9 %home_tile.1 = (f32[2048,128]{1,0:T(8,128)S(1)}, bf16[2048,48]{1,0:T(8,128)(2,1)S(1)}) custom-call(bf16[2096,128]{1,0:T(8,128)(2,1)S(1)} %pack.1.message_ref), custom_call_target="tpu_custom_call" | custom-call | flops 67108864 | tf_op jit(solution)/shard_map/home_tile/pallas_call | solution.py:215
  19.7 4.8 %guest_tile.4.refs_0_ = f32[2048,128]{1,0:T(8,128)S(1)} custom-call(bf16[2048,48]{1,0:T(8,128)(2,1)S(1)} %get-tuple-element.52.row_ref, bf16[2096,128]{1,0:T(8,128)(2,1)S(1)} %collective-permute-done.message_ref, f32[2048,128]{1,0:T(8,128)S(1)} %get-tuple-element.54.refs_0_), custom_call_target="tpu_custom_call", output_to_operand_aliasing={{}: (2, {})} | custom-call | flops 67108864 | tf_op jit(solution)/shard_map/guest_tile/pallas_call | solution.py:215
  24.9 1.8 %collective-permute-start.8 = (bf16[2096,128]{1,0:T(8,128)(2,1)}, bf16[2096,128]{1,0:T(8,128)(2,1)S(1)}, u32[]{:S(2)}, u32[]{:S(2)}) collective-permute-start(bf16[2096,128]{1,0:T(8,128)(2,1)} %collective-permute-done.1.message_ref), channel_id=1, source_target_pairs={{0,2},{2,0},{1,3},{3,1},{4,6},{6,4},{5,7},{7,5},{8,10},{10,8},{9,1... | collective-permute-start | bytes 1609736 | tf_op jit(solution)/shard_map/ppermute | solution.py:328
  26.7 5.6 %guest_tile.5 = (f32[2048,128]{1,0:T(8,128)S(1)}, f32[2048,128]{1,0:T(8,128)S(1)}) custom-call(bf16[2048,48]{1,0:T(8,128)(2,1)S(1)} %get-tuple-element.52.row_ref, bf16[2096,128]{1,0:T(8,128)(2,1)} %collective-permute-done.1.message_ref, f32[2048,128]{1,0:T(8,128)S(1)} %guest_tile.4.refs_0_), custom_call_target="tpu_custom_call", output_to_operand_aliasing={{1}: (2, {})} | custom-call | flops 67108864 | tf_op jit(solution)/shard_map/guest_tile/pallas_call | solution.py:215
  32.3 4.8 %guest_tile.6 = (f32[2048,128]{1,0:T(8,128)S(1)}, f32[2048,128]{1,0:T(8,128)S(1)}) custom-call(bf16[2048,48]{1,0:T(8,128)(2,1)S(1)} %get-tuple-element.52.row_ref, bf16[2096,128]{1,0:T(8,128)(2,1)S(1)} %collective-permute-done.3.message_ref, f32[2048,128]{1,0:T(8,128)S(1)} %get-tuple-element.60.refs_0_, ...), custom_call_target="tpu_custom_call", output_to_operand_aliasing={{0}: (2, {}), {1}: (3, {})} | custom-call | flops 67108864 | tf_op jit(solution)/shard_map/guest_tile/pallas_call | solution.py:215
  37.2 5.6 %guest_tile.7 = (f32[2048,128]{1,0:T(8,128)S(1)}, f32[2048,128]{1,0:T(8,128)S(1)}) custom-call(bf16[2048,48]{1,0:T(8,128)(2,1)S(1)} %get-tuple-element.52.row_ref, bf16[2096,128]{1,0:T(8,128)(2,1)} %collective-permute-done.4.message_ref, f32[2048,128]{1,0:T(8,128)S(1)} %get-tuple-element.65.refs_0_, ...), custom_call_target="tpu_custom_call", output_to_operand_aliasing={{0}: (2, {}), {1}: (3, {})} | custom-call | flops 67108864 | tf_op jit(solution)/shard_map/guest_tile/pallas_call | solution.py:215
  42.8 1.9 %half_gram.1 = (f32[128,128]{1,0:T(8,128)S(1)}, f32[128,128]{1,0:T(8,128)S(1)}, f32[2048,128]{1,0:T(8,128)S(1)}) custom-call(s32[1]{0:T(128)} %bitcast.core_ref, bf16[2048,128]{1,0:T(8,128)(2,1)} %own_ref.1, bf16[2048,128]{1,0:T(8,128)(2,1)} %collective-permute-done.2.pair_ref, ...), custom_call_target="tpu_custom_call", output_to_operand_aliasing={{2}: (3, {})} | custom-call | flops 67108864 | tf_op jit(solution)/shard_map/half_gram/pallas_call | solution.py:215
  44.8 4.6 %collective-permute-start.5 = (f32[128,128]{1,0:T(8,128)S(1)}, f32[128,128]{1,0:T(8,128)S(1)}, u32[]{:S(2)}, u32[]{:S(2)}) collective-permute-start(f32[128,128]{1,0:T(8,128)S(1)} %get-tuple-element.71), channel_id=1, source_target_pairs={{0,2},{2,0},{1,3},{3,1},{4,6},{6,4},{5,7},{7,5},{8,10},{10,8},{9,1... | collective-permute-start | bytes 196616 | tf_op jit(solution)/shard_map/ppermute | solution.py:328
  49.3 2.2 %collective-permute-start.6 = (f32[128,128]{1,0:T(8,128)S(1)}, f32[128,128]{1,0:T(8,128)S(1)}, u32[]{:S(2)}, u32[]{:S(2)}) collective-permute-start(f32[128,128]{1,0:T(8,128)S(1)} %get-tuple-element.70.keep_ref), channel_id=1, source_target_pairs={{2,3},{3,2},{6,7},{7,6},{10,11},{11,10},{14,15},{15,14},{18,19},{1... | collective-permute-start | bytes 196616 | tf_op jit(solution)/shard_map/ppermute | solution.py:356
  54.3 2.8 %collective-permute-done.7.far_crossed_ref = f32[128,128]{1,0:T(8,128)S(1)} collective-permute-done((f32[128,128]{1,0:T(8,128)S(1)}, f32[128,128]{1,0:T(8,128)S(1)}, u32[]{:S(2)}, u32[]{:S(2)}) %collective-permute-start.7) | collective-permute-done | bytes 65568 | tf_op jit(solution)/shard_map/ppermute | solution.py:357
  57.7 1.7 %piece_tile.8.total_ref = f32[2048,128]{1,0:T(8,128)S(1)} custom-call(bf16[2048,48]{1,0:T(8,128)(2,1)S(1)} %get-tuple-element.52.row_ref, bf16[2096,128]{1,0:T(8,128)(2,1)S(1)} %collective-permute-done.8.message_ref, f32[2048,128]{1,0:T(8,128)S(1)} %get-tuple-element.73.total_ref), custom_call_target="tpu_custom_call", output_to_operand_aliasing={{}: (2, {})} | custom-call | flops 67108864 | tf_op jit(solution)/shard_map/piece_tile/pallas_call | solution.py:215
  59.3 1.7 %piece_tile.9.total_ref = f32[2048,128]{1,0:T(8,128)S(1)} custom-call(bf16[2048,48]{1,0:T(8,128)(2,1)S(1)} %get-tuple-element.52.row_ref, bf16[2096,128]{1,0:T(8,128)(2,1)S(1)} %collective-permute-done.8.message_ref, f32[2048,128]{1,0:T(8,128)S(1)} %piece_tile.8.total_ref), custom_call_target="tpu_custom_call", output_to_operand_aliasing={{}: (2, {})} | custom-call | flops 67108864 | tf_op jit(solution)/shard_map/piece_tile/pallas_call | solution.py:215
  61.0 4.1 %collective-permute-done.9 = f32[128,128]{1,0:T(8,128)S(1)} collective-permute-done((f32[128,128]{1,0:T(8,128)S(1)}, f32[128,128]{1,0:T(8,128)S(1)}, u32[]{:S(2)}, u32[]{:S(2)}) %collective-permute-start.9) | collective-permute-done | bytes 65568 | tf_op jit(solution)/shard_map/ppermute | solution.py:306
  65.2 1.7 %piece_tile.10.total_ref = f32[2048,128]{1,0:T(8,128)S(1)} custom-call(bf16[2048,48]{1,0:T(8,128)(2,1)S(1)} %get-tuple-element.52.row_ref, bf16[2096,128]{1,0:T(8,128)(2,1)S(1)} %collective-permute-done.8.message_ref, f32[2048,128]{1,0:T(8,128)S(1)} %piece_tile.9.total_ref), custom_call_target="tpu_custom_call", output_to_operand_aliasing={{}: (2, {})} | custom-call | flops 67108864 | tf_op jit(solution)/shard_map/piece_tile/pallas_call | solution.py:215
  66.9 1.7 %piece_tile.11.total_ref = f32[2048,128]{1,0:T(8,128)S(1)} custom-call(bf16[2048,48]{1,0:T(8,128)(2,1)S(1)} %get-tuple-element.52.row_ref, bf16[2096,128]{1,0:T(8,128)(2,1)S(1)} %collective-permute-done.8.message_ref, f32[2048,128]{1,0:T(8,128)S(1)} %piece_tile.10.total_ref), custom_call_target="tpu_custom_call", output_to_operand_aliasing={{}: (2, {})} | custom-call | flops 67108864 | tf_op jit(solution)/shard_map/piece_tile/pallas_call | solution.py:215
  69.0 1.7 %piece_tile.12.total_ref = f32[2048,128]{1,0:T(8,128)S(1)} custom-call(bf16[2048,48]{1,0:T(8,128)(2,1)S(1)} %get-tuple-element.52.row_ref, bf16[2096,128]{1,0:T(8,128)(2,1)S(1)} %collective-permute-done.11.message_ref, f32[2048,128]{1,0:T(8,128)S(1)} %piece_tile.11.total_ref), custom_call_target="tpu_custom_call", output_to_operand_aliasing={{}: (2, {})} | custom-call | flops 67108864 | tf_op jit(solution)/shard_map/piece_tile/pallas_call | solution.py:215
  72.2 1.7 %piece_tile.13.total_ref = f32[2048,128]{1,0:T(8,128)S(1)} custom-call(bf16[2048,48]{1,0:T(8,128)(2,1)S(1)} %get-tuple-element.52.row_ref, bf16[2096,128]{1,0:T(8,128)(2,1)S(1)} %collective-permute-done.11.message_ref, f32[2048,128]{1,0:T(8,128)S(1)} %piece_tile.12.total_ref), custom_call_target="tpu_custom_call", output_to_operand_aliasing={{}: (2, {})} | custom-call | flops 67108864 | tf_op jit(solution)/shard_map/piece_tile/pallas_call | solution.py:215
  73.9 2.6 %collective-permute-done.13 = bf16[128,128]{1,0:T(8,128)(2,1)S(1)} collective-permute-done((bf16[128,128]{1,0:T(8,128)(2,1)S(1)}, bf16[128,128]{1,0:T(8,128)(2,1)S(1)}, u32[]{:S(2)}, u32[]{:S(2)}) %collective-permute-start.13) | collective-permute-done | bytes 32800 | tf_op jit(solution)/shard_map/ppermute | solution.py:306
  76.6 1.7 %piece_tile.14.total_ref = f32[2048,128]{1,0:T(8,128)S(1)} custom-call(bf16[2048,48]{1,0:T(8,128)(2,1)S(1)} %get-tuple-element.52.row_ref, bf16[2096,128]{1,0:T(8,128)(2,1)S(1)} %collective-permute-done.11.message_ref, f32[2048,128]{1,0:T(8,128)S(1)} %piece_tile.13.total_ref), custom_call_target="tpu_custom_call", output_to_operand_aliasing={{}: (2, {})} | custom-call | flops 67108864 | tf_op jit(solution)/shard_map/piece_tile/pallas_call | solution.py:215
  78.2 1.7 %collective-permute-done.14 = f32[128,128]{1,0:T(8,128)S(1)} collective-permute-done((f32[128,128]{1,0:T(8,128)S(1)}, f32[128,128]{1,0:T(8,128)S(1)}, u32[]{:S(2)}, u32[]{:S(2)}) %collective-permute-start.14) | collective-permute-done | bytes 65568 | tf_op jit(solution)/shard_map/ppermute | solution.py:306
  80.1 2.6 %piece_tile.15 = f32[2048,128]{1,0:T(8,128)} custom-call(bf16[2048,48]{1,0:T(8,128)(2,1)S(1)} %get-tuple-element.52.row_ref, bf16[2096,128]{1,0:T(8,128)(2,1)S(1)} %collective-permute-done.11.message_ref, f32[2048,128]{1,0:T(8,128)S(1)} %piece_tile.14.total_ref), custom_call_target="tpu_custom_call" | custom-call | flops 67108864 | tf_op jit(solution)/shard_map/piece_tile/pallas_call | solution.py:215
  84.4 6.2 %collective-permute-start.16 = (f32[128,128]{1,0:T(8,128)S(1)}, f32[128,128]{1,0:T(8,128)S(1)}, u32[]{:S(2)}, u32[]{:S(2)}) collective-permute-start(f32[128,128]{1,0:T(8,128)S(1)} %add_multiply_fusion), channel_id=1, source_target_pairs={{0,2},{2,0},{1,3},{3,1},{4,6},{6,4},{5,7},{7,5},{8,10},{10,8},{9,1... | collective-permute-start | bytes 196616 | tf_op jit(solution)/shard_map/ppermute | solution.py:328
  (34 shorter events, 10.5 us)
Async XLA Ops:
  1.8 17.9 %collective-permute-start = (bf16[2096,128]{1,0:T(8,128)(2,1)S(1)}, bf16[2096,128]{1,0:T(8,128)(2,1)S(1)}, u32[]{:S(2)}, u32[]{:S(2)}) collective-permute-start(bf16[2096,128]{1,0:T(8,128)(2,1)S(1)} %pack.1.message_ref), channel_id=1, source_target_pairs={{0,2},{2,0},{1,3},{3,1},{4,6},{6,4},{5,7},{7,5},{8,10},{10,8},{9,1... | collective-permute-start | bytes 1609736 | tf_op jit(solution)/shard_map/ppermute | solution.py:328
  5.1 19.3 %collective-permute-start.1 = (bf16[2096,128]{1,0:T(8,128)(2,1)S(1)}, bf16[2096,128]{1,0:T(8,128)(2,1)}, u32[]{:S(2)}, u32[]{:S(2)}) collective-permute-start(bf16[2096,128]{1,0:T(8,128)(2,1)S(1)} %pack.1.message_ref), channel_id=1, source_target_pairs={{0,6},{2,4},{4,0},{6,2},{8,14},{10,12},{12,8},{14,10},{16,22},{18,... | collective-permute-start | bytes 1609736 | tf_op jit(solution)/shard_map/ppermute | solution.py:317
  5.1 27.2 %collective-permute-start.3 = (bf16[2096,128]{1,0:T(8,128)(2,1)S(1)}, bf16[2096,128]{1,0:T(8,128)(2,1)S(1)}, u32[]{:S(2)}, u32[]{:S(2)}) collective-permute-start(bf16[2096,128]{1,0:T(8,128)(2,1)S(1)} %pack.1.message_ref), channel_id=1, source_target_pairs={{0,252},{2,254},{4,10},{6,8},{8,4},{10,6},{12,18},{14,16},{16,12},... | collective-permute-start | bytes 1609736 | tf_op jit(solution)/shard_map/ppermute | solution.py:317
  19.6 17.6 %collective-permute-start.4 = (bf16[2096,128]{1,0:T(8,128)(2,1)S(1)}, bf16[2096,128]{1,0:T(8,128)(2,1)}, u32[]{:S(2)}, u32[]{:S(2)}) collective-permute-start(bf16[2096,128]{1,0:T(8,128)(2,1)S(1)} %pack.1.message_ref), channel_id=1, source_target_pairs={{0,250},{2,8},{4,254},{6,12},{8,2},{10,16},{12,6},{14,20},{16,10},... | collective-permute-start | bytes 1609736 | tf_op jit(solution)/shard_map/ppermute | solution.py:322
  24.5 18.3 %collective-permute-start.2 = (bf16[2048,128]{1,0:T(8,128)(2,1)}, bf16[2048,128]{1,0:T(8,128)(2,1)}, u32[]{:S(2)}, u32[]{:S(2)}) collective-permute-start(bf16[2048,128]{1,0:T(8,128)(2,1)} %own_ref.1), channel_id=1, source_target_pairs={{0,1},{1,0},{2,3},{3,2},{4,5},{5,4},{6,7},{7,6},{8,9},{9,8},{10,11... | collective-permute-start | bytes 1572872 | tf_op jit(solution)/shard_map/ppermute | solution.py:344
  24.9 32.8 %collective-permute-start.8 = (bf16[2096,128]{1,0:T(8,128)(2,1)}, bf16[2096,128]{1,0:T(8,128)(2,1)S(1)}, u32[]{:S(2)}, u32[]{:S(2)}) collective-permute-start(bf16[2096,128]{1,0:T(8,128)(2,1)} %collective-permute-done.1.message_ref), channel_id=1, source_target_pairs={{0,2},{2,0},{1,3},{3,1},{4,6},{6,4},{5,7},{7,5},{8,10},{10,8},{9,1... | collective-permute-start | bytes 1609736 | tf_op jit(solution)/shard_map/ppermute | solution.py:328
  44.8 8.1 %collective-permute-start.5 = (f32[128,128]{1,0:T(8,128)S(1)}, f32[128,128]{1,0:T(8,128)S(1)}, u32[]{:S(2)}, u32[]{:S(2)}) collective-permute-start(f32[128,128]{1,0:T(8,128)S(1)} %get-tuple-element.71), channel_id=1, source_target_pairs={{0,2},{2,0},{1,3},{3,1},{4,6},{6,4},{5,7},{7,5},{8,10},{10,8},{9,1... | collective-permute-start | bytes 196616 | tf_op jit(solution)/shard_map/ppermute | solution.py:328
  49.3 5.0 %collective-permute-start.6 = (f32[128,128]{1,0:T(8,128)S(1)}, f32[128,128]{1,0:T(8,128)S(1)}, u32[]{:S(2)}, u32[]{:S(2)}) collective-permute-start(f32[128,128]{1,0:T(8,128)S(1)} %get-tuple-element.70.keep_ref), channel_id=1, source_target_pairs={{2,3},{3,2},{6,7},{7,6},{10,11},{11,10},{14,15},{15,14},{18,19},{1... | collective-permute-start | bytes 196616 | tf_op jit(solution)/shard_map/ppermute | solution.py:356
  51.5 5.6 %collective-permute-start.7 = (f32[128,128]{1,0:T(8,128)S(1)}, f32[128,128]{1,0:T(8,128)S(1)}, u32[]{:S(2)}, u32[]{:S(2)}) collective-permute-start(f32[128,128]{1,0:T(8,128)S(1)} %get-tuple-element.71), channel_id=1, source_target_pairs={{0,3},{1,2},{4,7},{5,6},{8,11},{9,10},{12,15},{13,14},{16,19},{17,... | collective-permute-start | bytes 196616 | tf_op jit(solution)/shard_map/ppermute | solution.py:357
  57.2 7.9 %collective-permute-start.9 = (f32[128,128]{1,0:T(8,128)S(1)}, f32[128,128]{1,0:T(8,128)S(1)}, u32[]{:S(2)}, u32[]{:S(2)}) collective-permute-start(f32[128,128]{1,0:T(8,128)S(1)} %fold.1), channel_id=1, source_target_pairs={{0,16},{2,18},{4,20},{6,22},{8,24},{10,26},{12,28},{14,30},{16,0},... | collective-permute-start | bytes 196616 | tf_op jit(solution)/shard_map/ppermute | solution.py:306
  57.3 11.7 %collective-permute-start.11 = (bf16[2096,128]{1,0:T(8,128)(2,1)S(1)}, bf16[2096,128]{1,0:T(8,128)(2,1)S(1)}, u32[]{:S(2)}, u32[]{:S(2)}) collective-permute-start(bf16[2096,128]{1,0:T(8,128)(2,1)S(1)} %collective-permute-done.3.message_ref), channel_id=1, source_target_pairs={{0,2},{2,0},{1,3},{3,1},{4,6},{6,4},{5,7},{7,5},{8,10},{10,8},{9,1... | collective-permute-start | bytes 1609736 | tf_op jit(solution)/shard_map/ppermute | solution.py:328
  65.1 3.8 %collective-permute-start.10 = (bf16[128,128]{1,0:T(8,128)(2,1)S(1)}, bf16[128,128]{1,0:T(8,128)(2,1)S(1)}, u32[]{:S(2)}, u32[]{:S(2)}) collective-permute-start(bf16[128,128]{1,0:T(8,128)(2,1)S(1)} %add_convert_fusion.2), channel_id=1, source_target_pairs={{0,8},{2,10},{4,12},{6,14},{8,0},{10,2},{12,4},{14,6},{16,24},{18,... | collective-permute-start | bytes 98312 | tf_op jit(solution)/shard_map/ppermute | solution.py:306
  68.9 3.2 %collective-permute-start.12 = (f32[128,128]{1,0:T(8,128)S(1)}, f32[128,128]{1,0:T(8,128)S(1)}, u32[]{:S(2)}, u32[]{:S(2)}) collective-permute-start(f32[128,128]{1,0:T(8,128)S(1)} %convert_add_fusion.1), channel_id=1, source_target_pairs={{0,4},{2,6},{4,0},{6,2},{8,12},{10,14},{12,8},{14,10},{16,20},{18,... | collective-permute-start | bytes 196616 | tf_op jit(solution)/shard_map/ppermute | solution.py:306
  72.1 4.4 %collective-permute-start.13 = (bf16[128,128]{1,0:T(8,128)(2,1)S(1)}, bf16[128,128]{1,0:T(8,128)(2,1)S(1)}, u32[]{:S(2)}, u32[]{:S(2)}) collective-permute-start(bf16[128,128]{1,0:T(8,128)(2,1)S(1)} %add_convert_fusion.1), channel_id=1, source_target_pairs={{0,128},{2,130},{4,132},{6,134},{8,136},{10,138},{12,140},{14,142}... | collective-permute-start | bytes 98312 | tf_op jit(solution)/shard_map/ppermute | solution.py:306
  76.5 3.5 %collective-permute-start.14 = (f32[128,128]{1,0:T(8,128)S(1)}, f32[128,128]{1,0:T(8,128)S(1)}, u32[]{:S(2)}, u32[]{:S(2)}) collective-permute-start(f32[128,128]{1,0:T(8,128)S(1)} %convert_add_fusion), channel_id=1, source_target_pairs={{0,64},{2,66},{4,68},{6,70},{8,72},{10,74},{12,76},{14,78},{16,80}... | collective-permute-start | bytes 196616 | tf_op jit(solution)/shard_map/ppermute | solution.py:306
  80.0 4.4 %collective-permute-start.15 = (bf16[128,128]{1,0:T(8,128)(2,1)S(1)}, bf16[128,128]{1,0:T(8,128)(2,1)S(1)}, u32[]{:S(2)}, u32[]{:S(2)}) collective-permute-start(bf16[128,128]{1,0:T(8,128)(2,1)S(1)} %add_convert_fusion), channel_id=1, source_target_pairs={{0,32},{2,34},{4,36},{6,38},{8,40},{10,42},{12,44},{14,46},{16,48}... | collective-permute-start | bytes 98312 | tf_op jit(solution)/shard_map/ppermute | solution.py:306
  84.4 7.1 %collective-permute-start.16 = (f32[128,128]{1,0:T(8,128)S(1)}, f32[128,128]{1,0:T(8,128)S(1)}, u32[]{:S(2)}, u32[]{:S(2)}) collective-permute-start(f32[128,128]{1,0:T(8,128)S(1)} %add_multiply_fusion), channel_id=1, source_target_pairs={{0,2},{2,0},{1,3},{3,1},{4,6},{6,4},{5,7},{7,5},{8,10},{10,8},{9,1... | collective-permute-start | bytes 196616 | tf_op jit(solution)/shard_map/ppermute | solution.py:328

commit v4 on v3

--- a/solution.py
+++ b/solution.py
@@ -162,17 +162,16 @@
             out_ref[rows, :] += part
 
 
-def fold_body(core_ref, keep_ref, swapped_ref, crossed_ref, far_crossed_ref, out_ref):
+def fold_body(core_ref, value_ref, crossed_ref, out_ref):
     first = core_ref[0] == 0
-    value = keep_ref[...] + swapped_ref[...]
 
     @pl.when(first)
     def _():
-        out_ref[...] = value + value.T
+        out_ref[...] = value_ref[...] + value_ref[...].T
 
     @pl.when(jnp.logical_not(first))
     def _():
-        out_ref[...] = value + (crossed_ref[...] + far_crossed_ref[...]).T
+        out_ref[...] = value_ref[...] + crossed_ref[...].T
 
 
 def half_gram_body(
@@ -288,7 +287,7 @@
 def fold(core, *blocks):
     out = pltpu.VMEM((LANES, LANES), jnp.float32)
     cost = pl.CostEstimate(flops=0, bytes_accessed=2**17, transcendentals=0)
-    return kernel_call(fold_body, "fold", [core, *blocks], "svvvv", [out], [], cost)[0]
+    return kernel_call(fold_body, "fold", [core, *blocks], "svv", [out], [], cost)[0]
 
 
 def along_blk(value, sizes, target):
@@ -352,27 +351,44 @@
     core = lax.axis_index("core").astype(jnp.int32)
     keep, give, product = half_gram(core.reshape(1), directions, pair, first, second)
 
-    swapped = core_swap(give)
-    crossed = lax.ppermute(keep, ("core", "rhs"), [(2, 3), (3, 2)])
-    far_crossed = lax.ppermute(give, ("core", "rhs"), [(0, 3), (1, 2)])
-    value = fold(core.reshape(1), keep, swapped, crossed, far_crossed)
-
     work = [(guest, piece) for guest in (even_other, odd_other) for piece in range(PIECES)]
+
+    def advance(product, pieces):
+        for _ in range(pieces):
+            guest, piece = work.pop(0)
+            product = piece_tile(rows, guest, product, piece, not work)
+        return product
+
+    value = keep + core_swap(give)
+    value, product = lax.optimization_barrier((value, product))
+    crossed = lax.ppermute(value, ("core", "rhs"), [(2, 3), (3, 2)])
+    product = advance(product, 1)
+    value, crossed, product = lax.optimization_barrier((value, crossed, product))
+    value = fold(core.reshape(1), value, crossed)
+
+    def moved_by(sent, move):
+        return along_blk(
+            sent, sizes, lambda y, x, z, c: (y ^ move[0], x ^ move[1], z ^ move[2], c ^ move[3])
+        )
+
     stages = (
-        ((0, 0, 4), 2, False), ((0, 0, 2), 2, True), ((0, 0, 1), 1, False),
-        ((2, 0, 0), 1, True), ((1, 0, 0), 1, False), ((0, 1, 0), 1, True),
+        ((0, 0, 4, 0), 2, True), ((0, 0, 2, 0), 1, True), ((0, 0, 1, 0), 1, False),
+        ((2, 0, 0, 0), 1, True), ((1, 0, 0, 0), 1, False),
     )
     for move, pieces, rounded in stages:
         sent = value.astype(jnp.bfloat16) if rounded else value
         product, sent = lax.optimization_barrier((product, sent))
-        moved = along_blk(sent, sizes, lambda y, x, z, c, d=move: (y ^ d[0], x ^ d[1], z ^ d[2], c))
-        for _ in range(pieces):
-            guest, piece = work.pop(0)
-            product = piece_tile(rows, guest, product, piece, not work)
+        moved = moved_by(sent, move)
+        product = advance(product, pieces)
         sent, product, moved = lax.optimization_barrier((sent, product, moved))
         value = sent.astype(jnp.float32) + moved.astype(jnp.float32)
-    value = value / (count * lax.axis_size(BLK))
-    swapped = core_swap(value)
+
+    product, value = lax.optimization_barrier((product, value))
+    moved = [moved_by(value, move) for move in ((0, 1, 0, 0), (0, 0, 0, 1), (0, 1, 0, 1))]
+    product = advance(product, len(work))
+    product, value, *moved = lax.optimization_barrier((product, value, *moved))
+    scale = 1.0 / (count * lax.axis_size(BLK))
+    value, swapped = (value + moved[0]) * scale, (moved[1] + moved[2]) * scale
     upper = core == lax.axis_index("rhs")
     gram = jnp.concatenate([jnp.where(upper, value, swapped), jnp.where(upper, swapped, value)], axis=0)
     return product, gram

time: 92.4 us -> 88.2 us (0.955)
  waiting for transfers between devices: 17 us -> 13.1 us
    ppermute x6 -> x8, starting transfers between devices: 0.59 us -> 7.83 us  [along_blk(): return lax.ppermute(value, BLK, pairs)]
    ppermute x5 -> x4, starting transfers between devices: 16.2 us -> 10 us  [core_swap(): return lax.ppermute(value, 'core', [(0, 1), (1, 0)])]
    ppermute x2 -> x1, waiting for transfers between devices: 4.27 us -> 1.12 us  [shards(): crossed = lax.ppermute(value, ('core', 'rhs'), [(2, 3), (3, 2)])]
    ppermute x2 -> x1, starting transfers between devices: 3.5 us -> 2.22 us  [shards(): crossed = lax.ppermute(value, ('core', 'rhs'), [(2, 3), (3, 2)])]
    ppermute x6 -> x8, waiting for transfers between devices: 11.8 us -> 11 us  [along_blk(): return lax.ppermute(value, BLK, pairs)]
  transfers between devices with their start and end apart: 17 -> 17, of which waited for: 9 -> 8; matrix products, arithmetic and copies ran while one was open for 0% -> 0% of each run, Pallas kernels for 46% -> 48%
where the time goes in v4:
time: 88.2 us; the launch traced here: 88 us
  Pallas kernels  43.2 us (49%)
  starting transfers between devices  30 us (34%)
  waiting for transfers between devices  13.1 us (15%)
  between operations  0.94 us (1%)
    pallas_call x16, Pallas kernels, kernel_call(): pl.pallas_call(body, out_shape=outs, in_specs=[pl.BlockSpec(memory_space=...  43.2 us
    ppermute x8, waiting for transfers between devices, along_blk(): return lax.ppermute(value, BLK, pairs)  11 us
    ppermute x4, starting transfers between devices, core_swap(): return lax.ppermute(value, 'core', [(0, 1), (1, 0)])  10 us
    ppermute x2, starting transfers between devices, from_neighbour(): return lax.ppermute(value, BLK, pairs)  9.49 us
    ppermute x8, starting transfers between devices, along_blk(): return lax.ppermute(value, BLK, pairs)  7.83 us
    ppermute x1, starting transfers between devices, shards(): crossed = lax.ppermute(value, ('core', 'rhs'), [(2, 3), (3, 2)])  2.22 us
  transfers between devices with their start and end apart: 17, of which 8 were waited for; matrix products, arithmetic and copies ran while one was open for 0% of the time, Pallas kernels for 48%

profile of v4, /device:TPU:1, one launch (start us, length us, event | category | flops | bytes accessed | tf_op | source)
XLA Modules:
  0.0 88.0 jit_solution(5695175435827168498)
XLA Ops:
  1.8 3.3 %collective-permute-start = (bf16[2096,128]{1,0:T(8,128)(2,1)S(1)}, bf16[2096,128]{1,0:T(8,128)(2,1)S(1)}, u32[]{:S(2)}, u32[]{:S(2)}) collective-permute-start(bf16[2096,128]{1,0:T(8,128)(2,1)S(1)} %pack.1.message_ref), channel_id=1, source_target_pairs={{0,2},{2,0},{1,3},{3,1},{4,6},{6,4},{5,7},{7,5},{8,10},{10,8},{9,1... | collective-permute-start | bytes 1609736 | tf_op jit(solution)/shard_map/ppermute | solution.py:327
  5.1 9.5 %collective-permute-start.2 = (bf16[2096,128]{1,0:T(8,128)(2,1)S(1)}, bf16[2096,128]{1,0:T(8,128)(2,1)S(1)}, u32[]{:S(2)}, u32[]{:S(2)}) collective-permute-start(bf16[2096,128]{1,0:T(8,128)(2,1)S(1)} %pack.1.message_ref), channel_id=1, source_target_pairs={{0,252},{2,254},{4,10},{6,8},{8,4},{10,6},{12,18},{14,16},{16,12},... | collective-permute-start | bytes 1609736 | tf_op jit(solution)/shard_map/ppermute | solution.py:316
  14.6 4.9 %home_tile.1 = (f32[2048,128]{1,0:T(8,128)S(1)}, bf16[2048,48]{1,0:T(8,128)(2,1)S(1)}) custom-call(bf16[2096,128]{1,0:T(8,128)(2,1)S(1)} %pack.1.message_ref), custom_call_target="tpu_custom_call" | custom-call | flops 67108864 | tf_op jit(solution)/shard_map/home_tile/pallas_call | solution.py:214
  19.7 4.8 %guest_tile.4.refs_0_ = f32[2048,128]{1,0:T(8,128)S(1)} custom-call(bf16[2048,48]{1,0:T(8,128)(2,1)S(1)} %get-tuple-element.59.row_ref, bf16[2096,128]{1,0:T(8,128)(2,1)S(1)} %collective-permute-done.message_ref, f32[2048,128]{1,0:T(8,128)S(1)} %get-tuple-element.61.refs_0_), custom_call_target="tpu_custom_call", output_to_operand_aliasing={{}: (2, {})} | custom-call | flops 67108864 | tf_op jit(solution)/shard_map/guest_tile/pallas_call | solution.py:214
  24.9 1.8 %collective-permute-start.8 = (bf16[2096,128]{1,0:T(8,128)(2,1)}, bf16[2096,128]{1,0:T(8,128)(2,1)S(1)}, u32[]{:S(2)}, u32[]{:S(2)}) collective-permute-start(bf16[2096,128]{1,0:T(8,128)(2,1)} %collective-permute-done.1.message_ref), channel_id=1, source_target_pairs={{0,2},{2,0},{1,3},{3,1},{4,6},{6,4},{5,7},{7,5},{8,10},{10,8},{9,1... | collective-permute-start | bytes 1609736 | tf_op jit(solution)/shard_map/ppermute | solution.py:327
  26.7 5.6 %guest_tile.5 = (f32[2048,128]{1,0:T(8,128)S(1)}, f32[2048,128]{1,0:T(8,128)S(1)}) custom-call(bf16[2048,48]{1,0:T(8,128)(2,1)S(1)} %get-tuple-element.59.row_ref, bf16[2096,128]{1,0:T(8,128)(2,1)} %collective-permute-done.1.message_ref, f32[2048,128]{1,0:T(8,128)S(1)} %guest_tile.4.refs_0_), custom_call_target="tpu_custom_call", output_to_operand_aliasing={{1}: (2, {})} | custom-call | flops 67108864 | tf_op jit(solution)/shard_map/guest_tile/pallas_call | solution.py:214
  32.3 4.8 %guest_tile.6 = (f32[2048,128]{1,0:T(8,128)S(1)}, f32[2048,128]{1,0:T(8,128)S(1)}) custom-call(bf16[2048,48]{1,0:T(8,128)(2,1)S(1)} %get-tuple-element.59.row_ref, bf16[2096,128]{1,0:T(8,128)(2,1)S(1)} %collective-permute-done.2.message_ref, f32[2048,128]{1,0:T(8,128)S(1)} %get-tuple-element.67.refs_0_, ...), custom_call_target="tpu_custom_call", output_to_operand_aliasing={{0}: (2, {}), {1}: (3, {})} | custom-call | flops 67108864 | tf_op jit(solution)/shard_map/guest_tile/pallas_call | solution.py:214
  37.2 5.6 %guest_tile.7 = (f32[2048,128]{1,0:T(8,128)S(1)}, f32[2048,128]{1,0:T(8,128)S(1)}) custom-call(bf16[2048,48]{1,0:T(8,128)(2,1)S(1)} %get-tuple-element.59.row_ref, bf16[2096,128]{1,0:T(8,128)(2,1)} %collective-permute-done.5.message_ref, f32[2048,128]{1,0:T(8,128)S(1)} %get-tuple-element.72.refs_0_, ...), custom_call_target="tpu_custom_call", output_to_operand_aliasing={{0}: (2, {}), {1}: (3, {})} | custom-call | flops 67108864 | tf_op jit(solution)/shard_map/guest_tile/pallas_call | solution.py:214
  42.8 1.9 %half_gram.1 = (f32[128,128]{1,0:T(8,128)S(1)}, f32[128,128]{1,0:T(8,128)S(1)}, f32[2048,128]{1,0:T(8,128)S(1)}) custom-call(s32[1]{0:T(128)} %bitcast.3.core_ref, bf16[2048,128]{1,0:T(8,128)(2,1)} %own_ref.1, bf16[2048,128]{1,0:T(8,128)(2,1)} %collective-permute-done.4.pair_ref, ...), custom_call_target="tpu_custom_call", output_to_operand_aliasing={{2}: (3, {})} | custom-call | flops 67108864 | tf_op jit(solution)/shard_map/half_gram/pallas_call | solution.py:214
  44.8 4.6 %collective-permute-start.6 = (f32[128,128]{1,0:T(8,128)S(1)}, f32[128,128]{1,0:T(8,128)S(1)}, u32[]{:S(2)}, u32[]{:S(2)}) collective-permute-start(f32[128,128]{1,0:T(8,128)S(1)} %get-tuple-element.77), channel_id=1, source_target_pairs={{0,2},{2,0},{1,3},{3,1},{4,6},{6,4},{5,7},{7,5},{8,10},{10,8},{9,1... | collective-permute-start | bytes 196616 | tf_op jit(solution)/shard_map/ppermute | solution.py:327
  50.2 2.2 %collective-permute-start.7 = (f32[128,128]{1,0:T(8,128)S(1)}, f32[128,128]{1,0:T(8,128)S(1)}, u32[]{:S(2)}, u32[]{:S(2)}) collective-permute-start(f32[128,128]{1,0:T(8,128)S(1)} %add.24.value_ref), channel_id=1, source_target_pairs={{2,3},{3,2},{6,7},{7,6},{10,11},{11,10},{14,15},{15,14},{18,19},{1... | collective-permute-start | bytes 196616 | tf_op jit(solution)/shard_map/ppermute | solution.py:364
  52.5 1.6 %piece_tile.8.total_ref = f32[2048,128]{1,0:T(8,128)S(1)} custom-call(bf16[2048,48]{1,0:T(8,128)(2,1)S(1)} %get-tuple-element.59.row_ref, bf16[2096,128]{1,0:T(8,128)(2,1)S(1)} %collective-permute-done.8.message_ref, f32[2048,128]{1,0:T(8,128)S(1)} %get-tuple-element.80.total_ref), custom_call_target="tpu_custom_call", output_to_operand_aliasing={{}: (2, {})} | custom-call | flops 67108864 | tf_op jit(solution)/shard_map/piece_tile/pallas_call | solution.py:214
  55.8 1.6 %piece_tile.9.total_ref = f32[2048,128]{1,0:T(8,128)S(1)} custom-call(bf16[2048,48]{1,0:T(8,128)(2,1)S(1)} %get-tuple-element.59.row_ref, bf16[2096,128]{1,0:T(8,128)(2,1)S(1)} %collective-permute-done.8.message_ref, f32[2048,128]{1,0:T(8,128)S(1)} %piece_tile.8.total_ref), custom_call_target="tpu_custom_call", output_to_operand_aliasing={{}: (2, {})} | custom-call | flops 67108864 | tf_op jit(solution)/shard_map/piece_tile/pallas_call | solution.py:214
  57.4 1.6 %piece_tile.10.total_ref = f32[2048,128]{1,0:T(8,128)S(1)} custom-call(bf16[2048,48]{1,0:T(8,128)(2,1)S(1)} %get-tuple-element.59.row_ref, bf16[2096,128]{1,0:T(8,128)(2,1)S(1)} %collective-permute-done.8.message_ref, f32[2048,128]{1,0:T(8,128)S(1)} %piece_tile.9.total_ref), custom_call_target="tpu_custom_call", output_to_operand_aliasing={{}: (2, {})} | custom-call | flops 67108864 | tf_op jit(solution)/shard_map/piece_tile/pallas_call | solution.py:214
  59.1 3.0 %collective-permute-done.9 = bf16[128,128]{1,0:T(8,128)(2,1)S(1)} collective-permute-done((bf16[128,128]{1,0:T(8,128)(2,1)S(1)}, bf16[128,128]{1,0:T(8,128)(2,1)S(1)}, u32[]{:S(2)}, u32[]{:S(2)}) %collective-permute-start.9) | collective-permute-done | bytes 32800 | tf_op jit(solution)/shard_map/ppermute | solution.py:305
  62.2 1.7 %piece_tile.11.total_ref = f32[2048,128]{1,0:T(8,128)S(1)} custom-call(bf16[2048,48]{1,0:T(8,128)(2,1)S(1)} %get-tuple-element.59.row_ref, bf16[2096,128]{1,0:T(8,128)(2,1)S(1)} %collective-permute-done.8.message_ref, f32[2048,128]{1,0:T(8,128)S(1)} %piece_tile.10.total_ref), custom_call_target="tpu_custom_call", output_to_operand_aliasing={{}: (2, {})} | custom-call | flops 67108864 | tf_op jit(solution)/shard_map/piece_tile/pallas_call | solution.py:214
  63.9 2.0 %collective-permute-done.10 = bf16[128,128]{1,0:T(8,128)(2,1)S(1)} collective-permute-done((bf16[128,128]{1,0:T(8,128)(2,1)S(1)}, bf16[128,128]{1,0:T(8,128)(2,1)S(1)}, u32[]{:S(2)}, u32[]{:S(2)}) %collective-permute-start.10) | collective-permute-done | bytes 32800 | tf_op jit(solution)/shard_map/ppermute | solution.py:305
  66.0 1.7 %piece_tile.12.total_ref = f32[2048,128]{1,0:T(8,128)S(1)} custom-call(bf16[2048,48]{1,0:T(8,128)(2,1)S(1)} %get-tuple-element.59.row_ref, bf16[2096,128]{1,0:T(8,128)(2,1)S(1)} %collective-permute-done.3.message_ref, f32[2048,128]{1,0:T(8,128)S(1)} %piece_tile.11.total_ref), custom_call_target="tpu_custom_call", output_to_operand_aliasing={{}: (2, {})} | custom-call | flops 67108864 | tf_op jit(solution)/shard_map/piece_tile/pallas_call | solution.py:214
  69.2 1.7 %piece_tile.13.total_ref = f32[2048,128]{1,0:T(8,128)S(1)} custom-call(bf16[2048,48]{1,0:T(8,128)(2,1)S(1)} %get-tuple-element.59.row_ref, bf16[2096,128]{1,0:T(8,128)(2,1)S(1)} %collective-permute-done.3.message_ref, f32[2048,128]{1,0:T(8,128)S(1)} %piece_tile.12.total_ref), custom_call_target="tpu_custom_call", output_to_operand_aliasing={{}: (2, {})} | custom-call | flops 67108864 | tf_op jit(solution)/shard_map/piece_tile/pallas_call | solution.py:214
  70.9 2.6 %collective-permute-done.12 = bf16[128,128]{1,0:T(8,128)(2,1)S(1)} collective-permute-done((bf16[128,128]{1,0:T(8,128)(2,1)S(1)}, bf16[128,128]{1,0:T(8,128)(2,1)S(1)}, u32[]{:S(2)}, u32[]{:S(2)}) %collective-permute-start.12) | collective-permute-done | bytes 32800 | tf_op jit(solution)/shard_map/ppermute | solution.py:305
  73.6 1.7 %piece_tile.14.total_ref = f32[2048,128]{1,0:T(8,128)S(1)} custom-call(bf16[2048,48]{1,0:T(8,128)(2,1)S(1)} %get-tuple-element.59.row_ref, bf16[2096,128]{1,0:T(8,128)(2,1)S(1)} %collective-permute-done.3.message_ref, f32[2048,128]{1,0:T(8,128)S(1)} %piece_tile.13.total_ref), custom_call_target="tpu_custom_call", output_to_operand_aliasing={{}: (2, {})} | custom-call | flops 67108864 | tf_op jit(solution)/shard_map/piece_tile/pallas_call | solution.py:214
  76.8 4.2 %collective-permute-start.15 = (f32[128,128]{1,0:T(8,128)S(1)}, f32[128,128]{1,0:T(8,128)S(1)}, u32[]{:S(2)}, u32[]{:S(2)}) collective-permute-start(f32[128,128]{1,0:T(8,128)S(1)} %add.29), channel_id=1, source_target_pairs={{0,2},{2,0},{4,6},{6,4},{8,10},{10,8},{12,14},{14,12},{16,18},{18,... | collective-permute-start | bytes 196616 | tf_op jit(solution)/shard_map/ppermute | solution.py:305
  81.1 3.0 %collective-permute-start.16 = (f32[128,128]{1,0:T(8,128)S(1)}, f32[128,128]{1,0:T(8,128)S(1)}, u32[]{:S(2)}, u32[]{:S(2)}) collective-permute-start(f32[128,128]{1,0:T(8,128)S(1)} %add.29), channel_id=1, source_target_pairs={{0,34},{2,32},{4,38},{6,36},{8,42},{10,40},{12,46},{14,44},{16,50}... | collective-permute-start | bytes 196616 | tf_op jit(solution)/shard_map/ppermute | solution.py:305
  84.1 2.6 %piece_tile.15 = f32[2048,128]{1,0:T(8,128)} custom-call(bf16[2048,48]{1,0:T(8,128)(2,1)S(1)} %get-tuple-element.59.row_ref, bf16[2096,128]{1,0:T(8,128)(2,1)S(1)} %collective-permute-done.3.message_ref, f32[2048,128]{1,0:T(8,128)S(1)} %piece_tile.14.total_ref), custom_call_target="tpu_custom_call" | custom-call | flops 67108864 | tf_op jit(solution)/shard_map/piece_tile/pallas_call | solution.py:214
  (35 shorter events, 8.8 us)
Async XLA Ops:
  1.8 17.9 %collective-permute-start = (bf16[2096,128]{1,0:T(8,128)(2,1)S(1)}, bf16[2096,128]{1,0:T(8,128)(2,1)S(1)}, u32[]{:S(2)}, u32[]{:S(2)}) collective-permute-start(bf16[2096,128]{1,0:T(8,128)(2,1)S(1)} %pack.1.message_ref), channel_id=1, source_target_pairs={{0,2},{2,0},{1,3},{3,1},{4,6},{6,4},{5,7},{7,5},{8,10},{10,8},{9,1... | collective-permute-start | bytes 1609736 | tf_op jit(solution)/shard_map/ppermute | solution.py:327
  5.1 19.3 %collective-permute-start.1 = (bf16[2096,128]{1,0:T(8,128)(2,1)S(1)}, bf16[2096,128]{1,0:T(8,128)(2,1)}, u32[]{:S(2)}, u32[]{:S(2)}) collective-permute-start(bf16[2096,128]{1,0:T(8,128)(2,1)S(1)} %pack.1.message_ref), channel_id=1, source_target_pairs={{0,6},{2,4},{4,0},{6,2},{8,14},{10,12},{12,8},{14,10},{16,22},{18,... | collective-permute-start | bytes 1609736 | tf_op jit(solution)/shard_map/ppermute | solution.py:316
  5.1 27.2 %collective-permute-start.2 = (bf16[2096,128]{1,0:T(8,128)(2,1)S(1)}, bf16[2096,128]{1,0:T(8,128)(2,1)S(1)}, u32[]{:S(2)}, u32[]{:S(2)}) collective-permute-start(bf16[2096,128]{1,0:T(8,128)(2,1)S(1)} %pack.1.message_ref), channel_id=1, source_target_pairs={{0,252},{2,254},{4,10},{6,8},{8,4},{10,6},{12,18},{14,16},{16,12},... | collective-permute-start | bytes 1609736 | tf_op jit(solution)/shard_map/ppermute | solution.py:316
  19.6 17.6 %collective-permute-start.5 = (bf16[2096,128]{1,0:T(8,128)(2,1)S(1)}, bf16[2096,128]{1,0:T(8,128)(2,1)}, u32[]{:S(2)}, u32[]{:S(2)}) collective-permute-start(bf16[2096,128]{1,0:T(8,128)(2,1)S(1)} %pack.1.message_ref), channel_id=1, source_target_pairs={{0,250},{2,8},{4,254},{6,12},{8,2},{10,16},{12,6},{14,20},{16,10},... | collective-permute-start | bytes 1609736 | tf_op jit(solution)/shard_map/ppermute | solution.py:321
  24.5 18.3 %collective-permute-start.4 = (bf16[2048,128]{1,0:T(8,128)(2,1)}, bf16[2048,128]{1,0:T(8,128)(2,1)}, u32[]{:S(2)}, u32[]{:S(2)}) collective-permute-start(bf16[2048,128]{1,0:T(8,128)(2,1)} %own_ref.1), channel_id=1, source_target_pairs={{0,1},{1,0},{2,3},{3,2},{4,5},{5,4},{6,7},{7,6},{8,9},{9,8},{10,11... | collective-permute-start | bytes 1572872 | tf_op jit(solution)/shard_map/ppermute | solution.py:343
  24.9 27.6 %collective-permute-start.8 = (bf16[2096,128]{1,0:T(8,128)(2,1)}, bf16[2096,128]{1,0:T(8,128)(2,1)S(1)}, u32[]{:S(2)}, u32[]{:S(2)}) collective-permute-start(bf16[2096,128]{1,0:T(8,128)(2,1)} %collective-permute-done.1.message_ref), channel_id=1, source_target_pairs={{0,2},{2,0},{1,3},{3,1},{4,6},{6,4},{5,7},{7,5},{8,10},{10,8},{9,1... | collective-permute-start | bytes 1609736 | tf_op jit(solution)/shard_map/ppermute | solution.py:327
  44.8 5.5 %collective-permute-start.6 = (f32[128,128]{1,0:T(8,128)S(1)}, f32[128,128]{1,0:T(8,128)S(1)}, u32[]{:S(2)}, u32[]{:S(2)}) collective-permute-start(f32[128,128]{1,0:T(8,128)S(1)} %get-tuple-element.77), channel_id=1, source_target_pairs={{0,2},{2,0},{1,3},{3,1},{4,6},{6,4},{5,7},{7,5},{8,10},{10,8},{9,1... | collective-permute-start | bytes 196616 | tf_op jit(solution)/shard_map/ppermute | solution.py:327
  50.2 5.0 %collective-permute-start.7 = (f32[128,128]{1,0:T(8,128)S(1)}, f32[128,128]{1,0:T(8,128)S(1)}, u32[]{:S(2)}, u32[]{:S(2)}) collective-permute-start(f32[128,128]{1,0:T(8,128)S(1)} %add.24.value_ref), channel_id=1, source_target_pairs={{2,3},{3,2},{6,7},{7,6},{10,11},{11,10},{14,15},{15,14},{18,19},{1... | collective-permute-start | bytes 196616 | tf_op jit(solution)/shard_map/ppermute | solution.py:364
  55.4 6.8 %collective-permute-start.9 = (bf16[128,128]{1,0:T(8,128)(2,1)S(1)}, bf16[128,128]{1,0:T(8,128)(2,1)S(1)}, u32[]{:S(2)}, u32[]{:S(2)}) collective-permute-start(bf16[128,128]{1,0:T(8,128)(2,1)S(1)} %convert_element_type.27), channel_id=1, source_target_pairs={{0,16},{2,18},{4,20},{6,22},{8,24},{10,26},{12,28},{14,30},{16,0},... | collective-permute-start | bytes 98312 | tf_op jit(solution)/shard_map/ppermute | solution.py:305
  55.5 10.6 %collective-permute-start.3 = (bf16[2096,128]{1,0:T(8,128)(2,1)S(1)}, bf16[2096,128]{1,0:T(8,128)(2,1)S(1)}, u32[]{:S(2)}, u32[]{:S(2)}) collective-permute-start(bf16[2096,128]{1,0:T(8,128)(2,1)S(1)} %collective-permute-done.2.message_ref), channel_id=1, source_target_pairs={{0,2},{2,0},{1,3},{3,1},{4,6},{6,4},{5,7},{7,5},{8,10},{10,8},{9,1... | collective-permute-start | bytes 1609736 | tf_op jit(solution)/shard_map/ppermute | solution.py:327
  62.1 3.8 %collective-permute-start.10 = (bf16[128,128]{1,0:T(8,128)(2,1)S(1)}, bf16[128,128]{1,0:T(8,128)(2,1)S(1)}, u32[]{:S(2)}, u32[]{:S(2)}) collective-permute-start(bf16[128,128]{1,0:T(8,128)(2,1)S(1)} %add_convert_fusion.1), channel_id=1, source_target_pairs={{0,8},{2,10},{4,12},{6,14},{8,0},{10,2},{12,4},{14,6},{16,24},{18,... | collective-permute-start | bytes 98312 | tf_op jit(solution)/shard_map/ppermute | solution.py:305
  65.9 3.2 %collective-permute-start.11 = (f32[128,128]{1,0:T(8,128)S(1)}, f32[128,128]{1,0:T(8,128)S(1)}, u32[]{:S(2)}, u32[]{:S(2)}) collective-permute-start(f32[128,128]{1,0:T(8,128)S(1)} %convert_add_fusion.1), channel_id=1, source_target_pairs={{0,4},{2,6},{4,0},{6,2},{8,12},{10,14},{12,8},{14,10},{16,20},{18,... | collective-permute-start | bytes 196616 | tf_op jit(solution)/shard_map/ppermute | solution.py:305
  69.1 4.4 %collective-permute-start.12 = (bf16[128,128]{1,0:T(8,128)(2,1)S(1)}, bf16[128,128]{1,0:T(8,128)(2,1)S(1)}, u32[]{:S(2)}, u32[]{:S(2)}) collective-permute-start(bf16[128,128]{1,0:T(8,128)(2,1)S(1)} %add_convert_fusion), channel_id=1, source_target_pairs={{0,128},{2,130},{4,132},{6,134},{8,136},{10,138},{12,140},{14,142}... | collective-permute-start | bytes 98312 | tf_op jit(solution)/shard_map/ppermute | solution.py:305
  73.5 3.2 %collective-permute-start.13 = (f32[128,128]{1,0:T(8,128)S(1)}, f32[128,128]{1,0:T(8,128)S(1)}, u32[]{:S(2)}, u32[]{:S(2)}) collective-permute-start(f32[128,128]{1,0:T(8,128)S(1)} %convert_add_fusion), channel_id=1, source_target_pairs={{0,64},{2,66},{4,68},{6,70},{8,72},{10,74},{12,76},{14,78},{16,80}... | collective-permute-start | bytes 196616 | tf_op jit(solution)/shard_map/ppermute | solution.py:305
  76.7 10.0 %collective-permute-start.14 = (f32[128,128]{1,0:T(8,128)S(1)}, f32[128,128]{1,0:T(8,128)S(1)}, u32[]{:S(2)}, u32[]{:S(2)}) collective-permute-start(f32[128,128]{1,0:T(8,128)S(1)} %add.29), channel_id=1, source_target_pairs={{0,32},{2,34},{4,36},{6,38},{8,40},{10,42},{12,44},{14,46},{16,48}... | collective-permute-start | bytes 196616 | tf_op jit(solution)/shard_map/ppermute | solution.py:305
  76.8 9.9 %collective-permute-start.15 = (f32[128,128]{1,0:T(8,128)S(1)}, f32[128,128]{1,0:T(8,128)S(1)}, u32[]{:S(2)}, u32[]{:S(2)}) collective-permute-start(f32[128,128]{1,0:T(8,128)S(1)} %add.29), channel_id=1, source_target_pairs={{0,2},{2,0},{4,6},{6,4},{8,10},{10,8},{12,14},{14,12},{16,18},{18,... | collective-permute-start | bytes 196616 | tf_op jit(solution)/shard_map/ppermute | solution.py:305
  81.1 6.2 %collective-permute-start.16 = (f32[128,128]{1,0:T(8,128)S(1)}, f32[128,128]{1,0:T(8,128)S(1)}, u32[]{:S(2)}, u32[]{:S(2)}) collective-permute-start(f32[128,128]{1,0:T(8,128)S(1)} %add.29), channel_id=1, source_target_pairs={{0,34},{2,32},{4,38},{6,36},{8,42},{10,40},{12,46},{14,44},{16,50}... | collective-permute-start | bytes 196616 | tf_op jit(solution)/shard_map/ppermute | solution.py:305

commit v5 on v4

v5 whole, which is shorter than its diff:
```python
import functools

import jax
import jax.numpy as jnp
from jax import lax
from jax.experimental import pallas as pl
from jax.experimental.pallas import tpu as pltpu
from jax.sharding import Mesh, PartitionSpec as P

LANES = 128
VMEM_BYTES = 12 * 2**20
STEP = 256
HALVES = 2
PIECES = 4
COPIES = 4
BLK = ("y", "xh", "z", "core")


def split_parts(base):
    high = base.astype(jnp.bfloat16).astype(jnp.float32)
    rest = base - high
    mid = rest.astype(jnp.bfloat16).astype(jnp.float32)
    low = (rest - mid).astype(jnp.bfloat16).astype(jnp.float32)
    return high, mid, low


def point_values(axial, angle, area):
    axial = axial.astype(jnp.float32) - 4.0
    angle = angle.astype(jnp.float32)
    area = area.astype(jnp.float32)
    cos, sin = jnp.cos(angle), jnp.sin(angle)
    return axial, cos, sin, axial * axial + cos * cos + sin * sin, 1.0 / (area * area)


def lay_rows(base_ref, features):
    groups = features[0].shape[0]
    base_ref[...] = jnp.zeros_like(base_ref)
    for row, feature in enumerate(features):
        for group in range(groups):
            base_ref[row : row + 1, group * LANES : (group + 1) * LANES] = feature[group : group + 1, :]


def guest_factors(geometry, base_ref, row_ref):
    axial, cos, sin, norm, scale = point_values(*geometry)
    lay_rows(base_ref, (scale, norm * scale, axial * scale, cos * scale, sin * scale))
    high, mid, low = split_parts(base_ref[...])
    stacked = jnp.concatenate([high, high, high, mid, mid, low], axis=0)
    for group in range(row_ref.shape[0] // LANES):
        part = stacked[:, group * LANES : (group + 1) * LANES]
        row_ref[group * LANES : (group + 1) * LANES, :] = part.T.astype(jnp.bfloat16)


def home_factors(geometry, base_ref, col_ref):
    axial, cos, sin, norm, scale = point_values(*geometry)
    scale = scale * base_ref.shape[1]
    double = -2.0 * scale
    lay_rows(base_ref, ((norm + 0.01) * scale, scale, axial * double, cos * double, sin * double))
    high, mid, low = split_parts(base_ref[...])
    col_ref[...] = jnp.concatenate([high, mid, low, high, mid, high], axis=0).astype(jnp.bfloat16)


def add_panels(total, row_ref, directions_ref, home, start, count, where=0):
    for low in range(0, count, STEP):
        at = start + low
        inverse = jnp.dot(row_ref[pl.ds(at, STEP), :], home, preferred_element_type=jnp.float32)
        values = lax.rsqrt(inverse).astype(jnp.bfloat16)
        directions = directions_ref[:, pl.ds(where + at, STEP)]
        total = total + jnp.dot(directions, values, preferred_element_type=jnp.float32)
    return total


def tile_product(home_ref, row_ref, directions_ref, out_ref, arrive=None):
    count = row_ref.shape[0] // HALVES

    def step_fn(step, carried):
        if arrive is not None:
            arrive(step)
        start = pl.multiple_of(step * count, count)
        out_ref[...] = add_panels(out_ref[...], row_ref, directions_ref, home_ref[...], start, count)
        return carried

    lax.fori_loop(0, HALVES, step_fn, 0)


def geometry_of(ref):
    groups = ref.shape[0] // 3
    return tuple(ref[k * groups : (k + 1) * groups, :].astype(jnp.float32) for k in range(3))


def geometry_copy(message_ref, geometry_ref, sem):
    count = message_ref.shape[1] - LANES
    return pltpu.make_async_copy(
        message_ref.at[pl.ds(0, geometry_ref.shape[0]), pl.ds(count, LANES)], geometry_ref, sem
    )


def pack_body(directions_ref, axial_ref, angle_ref, area_ref, out_ref, held_ref, sems):
    count = directions_ref.shape[0]
    part = count // COPIES
    copies = []
    for k in range(COPIES):
        rows = pl.ds(k * part, part)
        copies.append(pltpu.make_async_copy(directions_ref.at[rows], held_ref.at[rows], sems.at[k]))
    groups = axial_ref.shape[0]
    for k, ref in enumerate((axial_ref, angle_ref, area_ref)):
        place = out_ref.at[pl.ds(k * groups, groups), pl.ds(count, LANES)]
        copies.append(pltpu.make_async_copy(ref, place, sems.at[COPIES + k]))
    for copy in copies:
        copy.start()
    out_ref[3 * groups :, count:] = jnp.zeros((LANES - 3 * groups, LANES), jnp.bfloat16)
    for k in range(COPIES):
        copies[k].wait()
        for low in range(k * part, (k + 1) * part, LANES):
            out_ref[:, low : low + LANES] = held_ref[low : low + LANES, :].T
    for copy in copies[COPIES:]:
        copy.wait()


def home_body(message_ref, out_ref, home_ref, base_ref, row_ref):
    count = row_ref.shape[0]
    geometry = geometry_of(message_ref.at[pl.ds(0, 3 * count // LANES), pl.ds(count, LANES)])
    home_factors(geometry, base_ref, home_ref)
    guest_factors(geometry, base_ref, row_ref)
    out_ref[...] = jnp.zeros_like(out_ref)
    tile_product(home_ref, row_ref, message_ref, out_ref)


def guest_body(has_total, n_held, n_sources, *refs):
    refs = list(refs)
    choice_ref = refs.pop(0) if n_sources > 1 else None
    home_ref = refs.pop(0)
    sources = [refs.pop(0) for _ in range(n_sources)]
    out_ref, *refs = refs[has_total + n_held :]
    base_ref, row_ref, directions_ref, geometry_ref, sems = refs[n_held:]
    part = row_ref.shape[0] // HALVES

    def part_copy(ref, step):
        columns = pl.ds(pl.multiple_of(step * part, part), part)
        return pltpu.make_async_copy(ref.at[:, columns], directions_ref.at[:, columns], sems.at[step])

    def fetch(ref):
        geometry_copy(ref, geometry_ref, sems.at[HALVES]).start()
        for step in range(HALVES):
            part_copy(ref, step).start()

    if choice_ref is None:
        fetch(sources[0])
    else:
        for k, ref in enumerate(sources):
            pl.when(choice_ref[0] == k)(functools.partial(fetch, ref))
    geometry_copy(sources[0], geometry_ref, sems.at[HALVES]).wait()
    guest_factors(geometry_of(geometry_ref), base_ref, row_ref)
    if not has_total:
        out_ref[...] = jnp.zeros_like(out_ref)
    tile_product(
        home_ref, row_ref, directions_ref, out_ref, arrive=lambda step: part_copy(sources[0], step).wait()
    )


def piece_body(
    offset, last, home_ref, message_ref, total_ref, out_ref, base_ref, row_ref, directions_ref, geometry_ref, sems
):
    width = row_ref.shape[0]
    geometry = geometry_copy(message_ref, geometry_ref, sems.at[0])
    copy = pltpu.make_async_copy(message_ref.at[:, pl.ds(offset, width)], directions_ref, sems.at[1])
    geometry.start()
    copy.start()
    geometry.wait()
    part = slice(offset // LANES, (offset + width) // LANES)
    guest_factors([value[part] for value in geometry_of(geometry_ref)], base_ref, row_ref)
    copy.wait()
    total = add_panels(total_ref[...], row_ref, directions_ref, home_ref[...], 0, width)
    out_ref[...] = total.T if last else total


def fold_body(core_ref, value_ref, crossed_ref, out_ref):
    first = core_ref[0] == 0

    @pl.when(first)
    def _():
        out_ref[...] = value_ref[...] + value_ref[...].T

    @pl.when(jnp.logical_not(first))
    def _():
        out_ref[...] = value_ref[...].T + crossed_ref[...]


def half_gram_body(
    core_ref, own_ref, pair_ref, first_ref, second_ref, keep_ref, give_ref, sum_ref, directions_ref, sems
):
    copies = [
        pltpu.make_async_copy(ref, directions_ref.at[k], sems.at[k]) for k, ref in enumerate((own_ref, pair_ref))
    ]
    for copy in copies:
        copy.start()
    first, second = first_ref[...], second_ref[...]
    value = 0.5 * first + second
    sum_ref[...] = first + second
    high = value.astype(jnp.bfloat16)
    low = (value - high.astype(jnp.float32)).astype(jnp.bfloat16)
    both = jnp.concatenate([high, low], axis=0)
    for copy in copies:
        copy.wait()
    directions = jnp.concatenate([directions_ref[0], directions_ref[1]], axis=1)
    part = jnp.dot(both, directions, preferred_element_type=jnp.float32)
    part = part[:LANES] + part[LANES:]
    on_first = core_ref[0] == 0
    keep_ref[...] = jnp.where(on_first, part[:, :LANES], part[:, LANES:])
    give_ref[...] = jnp.where(on_first, part[:, LANES:], part[:, :LANES])


def tile_cost(count):
    return pl.CostEstimate(flops=count * count * 16, bytes_accessed=0, transcendentals=0)


def kernel_call(body, name, operands, places, outs, scratch, cost, aliases=None):
    spaces = {"v": pltpu.VMEM, "s": pltpu.SMEM, "a": pl.ANY, "h": pltpu.HBM}
    fixed = {"v": pltpu.VMEM, "h": pltpu.HBM}
    operands = [
        pltpu.with_memory_space_constraint(value, fixed[place]) if place in fixed else value
        for value, place in zip(operands, places)
    ]
    return pl.pallas_call(
        body,
        out_shape=outs,
        in_specs=[pl.BlockSpec(memory_space=spaces[place]) for place in places],
        out_specs=[pl.BlockSpec(memory_space=pltpu.VMEM)] * len(outs),
        input_output_aliases=aliases or {},
        scratch_shapes=scratch,
        cost_estimate=cost,
        compiler_params=pltpu.CompilerParams(vmem_limit_bytes=VMEM_BYTES),
        name=name,
    )(*operands)


def pack(directions, geometry):
    count = directions.shape[0]
    return kernel_call(
        pack_body, "pack", [directions, *geometry], "hhhh", [pltpu.VMEM((LANES, count + LANES), jnp.bfloat16)],
        [pltpu.VMEM((count, LANES), jnp.bfloat16), pltpu.SemaphoreType.DMA((COPIES + 3,))],
        pl.CostEstimate(flops=0, bytes_accessed=2**20, transcendentals=0),
    )[0]


def tile_scratch(count):
    return [pltpu.VMEM((8, count), jnp.float32), pltpu.VMEM((count, 48), jnp.bfloat16)]


def fetch_scratch(count, geometry_rows, copies):
    return tile_scratch(count) + [
        pltpu.VMEM((LANES, count), jnp.bfloat16),
        pltpu.VMEM((geometry_rows, LANES), jnp.bfloat16),
        pltpu.SemaphoreType.DMA((copies,)),
    ]


def home_tile(message, count):
    outs = [pltpu.VMEM((LANES, count), jnp.float32), pltpu.VMEM((48, count), jnp.bfloat16)]
    return kernel_call(home_body, "home_tile", [message], "v", outs, tile_scratch(count), tile_cost(count))


def guest_tile(home, sources, total=None, held=(), choice=None):
    count = home.shape[1]
    totals = [] if total is None else [total]
    choices = [] if choice is None else [choice]
    place = len(choices) + 1 + len(sources)
    aliases = {place: 0} if totals else {}
    aliases.update({place + len(totals) + k: 1 + k for k in range(len(held))})
    return kernel_call(
        functools.partial(guest_body, len(totals), len(held), len(sources)), "guest_tile",
        [*choices, home, *sources, *totals, *held],
        "s" * len(choices) + "v" + "a" * len(sources) + "v" * (len(totals) + len(held)),
        [pltpu.VMEM((LANES, count), jnp.float32)] * (1 + len(held)),
        fetch_scratch(count, 3 * count // LANES, HALVES + 1), tile_cost(count), aliases,
    )


def piece_tile(home, message, total, piece, last):
    count = home.shape[1]
    width = count // PIECES
    out = jax.ShapeDtypeStruct((count, LANES), jnp.float32) if last else pltpu.VMEM((LANES, count), jnp.float32)
    return kernel_call(
        functools.partial(piece_body, piece * width, last), "piece_tile", [home, message, total], "vav", [out],
        fetch_scratch(width, 3 * count // LANES, 2), tile_cost(count), None if last else {2: 0},
    )[0]


def half_gram(core, own, pair, first, second):
    count = first.shape[1]
    block = pltpu.VMEM((LANES, LANES), jnp.float32)
    return kernel_call(
        half_gram_body, "half_gram", [core, own, pair, first, second], "shavv",
        [block, block, pltpu.VMEM((LANES, count), jnp.float32)],
        [pltpu.VMEM((2, count, LANES), jnp.bfloat16), pltpu.SemaphoreType.DMA((2,))], tile_cost(count), {3: 2},
    )


def fold(core, *blocks):
    out = pltpu.VMEM((LANES, LANES), jnp.float32)
    cost = pl.CostEstimate(flops=0, bytes_accessed=2**17, transcendentals=0)
    return kernel_call(fold_body, "fold", [core, *blocks], "svv", [out], [], cost)[0]


def along_blk(value, sizes, target):
    ny, nx, nz, nc = sizes

    def index(y, x, z, c):
        return ((y % ny * nx + x % nx) * nz + z % nz) * nc + c % nc

    pairs = []
    for y in range(ny):
        for x in range(nx):
            for z in range(nz):
                for c in range(nc):
                    pairs.append((index(y, x, z, c), index(*target(y, x, z, c))))
    return lax.ppermute(value, BLK, pairs)


def from_neighbour(value, parity):
    count = lax.axis_size(BLK)
    pairs = []
    for block in range(count):
        chip, core = divmod(block, 2)
        first = chip % 2 == parity
        other = 2 * (chip + 1) + 1 - core if first else 2 * (chip - 1) + core
        pairs.append((block, other % count))
    return lax.ppermute(value, BLK, pairs)


def from_far(length):
    count = lax.axis_size(BLK)
    direct, passed = [], []
    for block in range(count):
        place = block // 2 % length
        if block % 2 == 0:
            source, between, over = block - 3, block - 2, place == 1
        else:
            source, between, over = block + 3, block + 1, place == length - 2
        if over:
            passed.append((between % count, block))
        else:
            direct.append((source % count, block))
    return tuple(functools.partial(lax.ppermute, axis_name=BLK, perm=pairs) for pairs in (direct, passed))


def core_swap(value):
    return lax.ppermute(value, "core", [(0, 1), (1, 0)])


def shards(sizes, directions, axial_pos, azimuth, panel_area):
    count = axial_pos.shape[0]
    geometry = [part.reshape(count // LANES, LANES) for part in (axial_pos, azimuth, panel_area)]
    message = pack(directions, geometry)
    other = core_swap(message)
    even = from_neighbour(message, 0)
    odd = from_neighbour(message, 1)

    first, home = home_tile(message, count)
    first, late = lax.optimization_barrier((first, message))
    direct, passed = from_far(sizes[2])
    far = direct(late)
    (first,) = guest_tile(home, (other,), first)
    first, even, later = lax.optimization_barrier((first, even, directions))
    pair = lax.ppermute(later, "rhs", [(0, 1), (1, 0)])
    even_other = core_swap(even)
    second, first = guest_tile(home, (even,), None, (first,))
    second, odd = lax.optimization_barrier((second, odd))
    over = passed(odd)
    odd_other = core_swap(odd)
    second, first = guest_tile(home, (odd,), second, (first,))
    second, far, over = lax.optimization_barrier((second, far, over))
    core = lax.axis_index("core").astype(jnp.int32)
    place = lax.axis_index("z")
    is_over = jnp.where(core == 0, place == 1, place == sizes[2] - 2).astype(jnp.int32).reshape(1)
    first, second = guest_tile(home, (far, over), first, (second,), is_over)
    keep, give, product = half_gram(core.reshape(1), directions, pair, first, second)

    work = [(guest, piece) for guest in (even_other, odd_other) for piece in range(PIECES)]

    def advance(product, pieces):
        for _ in range(pieces):
            guest, piece = work.pop(0)
            product = piece_tile(home, guest, product, piece, not work)
        return product

    value = keep + core_swap(give)
    value, product = lax.optimization_barrier((value, product))
    crossed = lax.ppermute(value, ("core", "rhs"), [(2, 3), (3, 2)])
    product = advance(product, 1)
    value, crossed, product = lax.optimization_barrier((value, crossed, product))
    value = fold(core.reshape(1), value, crossed)

    def moved_by(sent, move):
        return along_blk(
            sent, sizes, lambda y, x, z, c: (y ^ move[0], x ^ move[1], z ^ move[2], c ^ move[3])
        )

    stages = (
        ((0, 0, 4, 0), 2, True), ((0, 0, 2, 0), 1, True), ((0, 0, 1, 0), 1, False),
        ((2, 0, 0, 0), 1, True), ((1, 0, 0, 0), 1, False),
    )
    for move, pieces, rounded in stages:
        sent = value.astype(jnp.bfloat16) if rounded else value
        product, sent = lax.optimization_barrier((product, sent))
        moved = moved_by(sent, move)
        product = advance(product, pieces)
        sent, product, moved = lax.optimization_barrier((sent, product, moved))
        value = sent.astype(jnp.float32) + moved.astype(jnp.float32)

    product, value = lax.optimization_barrier((product, value))
    moved = [moved_by(value, move) for move in ((0, 1, 0, 0), (0, 0, 0, 1), (0, 1, 0, 1))]
    product = advance(product, len(work))
    product, value, *moved = lax.optimization_barrier((product, value, *moved))
    scale = 1.0 / (count * lax.axis_size(BLK))
    value, swapped = (value + moved[0]) * scale, (moved[1] + moved[2]) * scale
    upper = core == lax.axis_index("rhs")
    gram = jnp.concatenate([jnp.where(upper, value, swapped), jnp.where(upper, swapped, value)], axis=0)
    return product, gram


def solution(mesh):
    sizes = (4, 2, 8, 2)
    fine = Mesh(mesh.devices.reshape(sizes + (2,)), BLK + ("rhs",))
    in_specs = (P(BLK, "rhs"), P(BLK), P(BLK), P(BLK))
    out_specs = (P(BLK, "rhs"), P(None, "rhs"))
    return jax.shard_map(
        functools.partial(shards, sizes), mesh=fine, in_specs=in_specs, out_specs=out_specs, check_vma=False
    )
```

time: 88.2 us -> 90.3 us (1.024)
  Pallas kernels: 43.2 us -> 36.9 us
  starting transfers between devices: 30 us -> 34.3 us
  waiting for transfers between devices: 13.1 us -> 17.2 us
    pallas_call x16, Pallas kernels: 43.2 us -> 36.9 us  [kernel_call(): pl.pallas_call(body, out_shape=outs, in_specs=[pl.BlockSpec(memory_space=...]
    ppermute x8, waiting for transfers between devices: 11 us -> 14.4 us  [along_blk(): return lax.ppermute(value, BLK, pairs)]
    ppermute x1 -> x2, starting transfers between devices: 0.09 us -> 3.39 us  [the longest x1 1.92 us: shards(): far = direct(late)]
    ppermute x8, starting transfers between devices: 7.83 us -> 9.29 us  [along_blk(): return lax.ppermute(value, BLK, pairs)]
    ppermute x4, starting transfers between devices: 10 us -> 9 us  [core_swap(): return lax.ppermute(value, 'core', [(0, 1), (1, 0)])]
  transfers between devices with their start and end apart: 17 -> 18, of which waited for: 8 -> 9; matrix products, arithmetic and copies ran while one was open for 0% -> 0% of each run, Pallas kernels for 48% -> 39%
where the time goes in v5:
time: 90.3 us; the launch traced here: 90.1 us
  Pallas kernels  36.9 us (41%)
  starting transfers between devices  34.3 us (38%)
  waiting for transfers between devices  17.2 us (19%)
    pallas_call x16, Pallas kernels, kernel_call(): pl.pallas_call(body, out_shape=outs, in_specs=[pl.BlockSpec(memory_space=...  36.9 us
    ppermute x8, waiting for transfers between devices, along_blk(): return lax.ppermute(value, BLK, pairs)  14.4 us
    ppermute x2, starting transfers between devices, from_neighbour(): return lax.ppermute(value, BLK, pairs)  9.49 us
    ppermute x8, starting transfers between devices, along_blk(): return lax.ppermute(value, BLK, pairs)  9.29 us
    ppermute x4, starting transfers between devices, core_swap(): return lax.ppermute(value, 'core', [(0, 1), (1, 0)])  9 us
    ppermute x1, starting transfers between devices, shards(): crossed = lax.ppermute(value, ('core', 'rhs'), [(2, 3), (3, 2)])  2.23 us
    ppermute x1, starting transfers between devices, shards(): far = direct(late)  1.92 us
  transfers between devices with their start and end apart: 18, of which 9 were waited for; matrix products, arithmetic and copies ran while one was open for 0% of the time, Pallas kernels for 39%

profile of v5, /device:TPU:1, one launch (start us, length us, event | category | flops | bytes accessed | tf_op | source)
XLA Modules:
  0.0 90.1 jit_solution(792006887232553129)
XLA Ops:
  0.6 1.3 %pack.1.message_ref = bf16[128,2176]{1,0:T(8,128)(2,1)S(1)} custom-call(bf16[2048,128]{1,0:T(8,128)(2,1)} %own_ref.1, bf16[16,128]{1,0:T(8,128)(2,1)} %bitcast.5, bf16[16,128]{1,0:T(8,128)(2,1)} %bitcast.6, bf16[16,128]{1,0:T(8,128)(2,1)} %bitcast.7), custom_call_target="tpu_custom_call" | custom-call | bytes 1048576 | tf_op jit(solution)/shard_map/pack/pallas_call | solution.py:223
  2.0 3.3 %collective-permute-start = (bf16[128,2176]{1,0:T(8,128)(2,1)S(1)}, bf16[128,2176]{1,0:T(8,128)(2,1)S(1)}, u32[]{:S(2)}, u32[]{:S(2)}) collective-permute-start(bf16[128,2176]{1,0:T(8,128)(2,1)S(1)} %pack.1.message_ref), channel_id=1, source_target_pairs={{0,2},{2,0},{1,3},{3,1},{4,6},{6,4},{5,7},{7,5},{8,10},{10,8},{9,1... | collective-permute-start | bytes 1671176 | tf_op jit(solution)/shard_map/ppermute | solution.py:347
  5.3 9.5 %collective-permute-start.2 = (bf16[128,2176]{1,0:T(8,128)(2,1)S(1)}, bf16[128,2176]{1,0:T(8,128)(2,1)}, u32[]{:S(2)}, u32[]{:S(2)}) collective-permute-start(bf16[128,2176]{1,0:T(8,128)(2,1)S(1)} %pack.1.message_ref), channel_id=1, source_target_pairs={{0,252},{2,254},{4,10},{6,8},{8,4},{10,6},{12,18},{14,16},{16,12},... | collective-permute-start | bytes 1671176 | tf_op jit(solution)/shard_map/ppermute | solution.py:327
  14.8 4.1 %home_tile.1 = (f32[128,2048]{1,0:T(8,128)S(1)}, bf16[48,2048]{1,0:T(8,128)(2,1)S(1)}) custom-call(bf16[128,2176]{1,0:T(8,128)(2,1)S(1)} %pack.1.message_ref), custom_call_target="tpu_custom_call" | custom-call | flops 67108864 | tf_op jit(solution)/shard_map/home_tile/pallas_call | solution.py:223
  18.9 1.9 %collective-permute-start.5 = (bf16[128,2176]{1,0:T(8,128)(2,1)S(1)}, bf16[128,2176]{1,0:T(8,128)(2,1)}, u32[]{:S(2)}, u32[]{:S(2)}) collective-permute-start(bf16[128,2176]{1,0:T(8,128)(2,1)S(1)} %pack.1.message_ref), channel_id=1, source_target_pairs={{250,0},{8,2},{12,6},{2,8},{16,10},{6,12},{20,14},{10,16},{24,18},... | collective-permute-start | bytes 1671176 | tf_op jit(solution)/shard_map/ppermute | solution.py:361
  20.8 4.2 %guest_tile.4.refs_2_ = f32[128,2048]{1,0:T(8,128)S(1)} custom-call(bf16[48,2048]{1,0:T(8,128)(2,1)S(1)} %get-tuple-element.60.refs_0_.refs_1_.home_ref, bf16[128,2176]{1,0:T(8,128)(2,1)S(1)} %collective-permute-done.refs_1_, f32[128,2048]{1,0:T(8,128)S(1)} %get-tuple-element.62.refs_2_), custom_call_target="tpu_custom_call", output_to_operand_aliasing={{}: (2, {})} | custom-call | flops 67108864 | tf_op jit(solution)/shard_map/guest_tile/pallas_call | solution.py:223
  25.0 4.9 %guest_tile.5 = (f32[128,2048]{1,0:T(8,128)S(1)}, f32[128,2048]{1,0:T(8,128)S(1)}) custom-call(bf16[48,2048]{1,0:T(8,128)(2,1)S(1)} %get-tuple-element.60.refs_0_.refs_1_.home_ref, bf16[128,2176]{1,0:T(8,128)(2,1)} %collective-permute-done.1.refs_1_, f32[128,2048]{1,0:T(8,128)S(1)} %guest_tile.4.refs_2_), custom_call_target="tpu_custom_call", output_to_operand_aliasing={{1}: (2, {})} | custom-call | flops 67108864 | tf_op jit(solution)/shard_map/guest_tile/pallas_call | solution.py:223
  30.3 1.5 %collective-permute-start.6 = (bf16[128,2176]{1,0:T(8,128)(2,1)}, bf16[128,2176]{1,0:T(8,128)(2,1)}, u32[]{:S(2)}, u32[]{:S(2)}) collective-permute-start(bf16[128,2176]{1,0:T(8,128)(2,1)} %collective-permute-done.2.refs_1_), channel_id=1, source_target_pairs={{0,4},{28,26},{32,36},{60,58},{64,68},{92,90},{96,100},{124,122},{... | collective-permute-start | bytes 1671176 | tf_op jit(solution)/shard_map/ppermute | solution.py:368
  32.7 3.2 %collective-permute-start.9 = (bf16[128,2176]{1,0:T(8,128)(2,1)}, bf16[128,2176]{1,0:T(8,128)(2,1)S(1)}, u32[]{:S(2)}, u32[]{:S(2)}) collective-permute-start(bf16[128,2176]{1,0:T(8,128)(2,1)} %collective-permute-done.1.refs_1_), channel_id=1, source_target_pairs={{0,2},{2,0},{1,3},{3,1},{4,6},{6,4},{5,7},{7,5},{8,10},{10,8},{9,1... | collective-permute-start | bytes 1671176 | tf_op jit(solution)/shard_map/ppermute | solution.py:347
  35.9 4.8 %guest_tile.6 = (f32[128,2048]{1,0:T(8,128)S(1)}, f32[128,2048]{1,0:T(8,128)S(1)}) custom-call(bf16[48,2048]{1,0:T(8,128)(2,1)S(1)} %get-tuple-element.60.refs_0_.refs_1_.home_ref, bf16[128,2176]{1,0:T(8,128)(2,1)} %collective-permute-done.2.refs_1_, f32[128,2048]{1,0:T(8,128)S(1)} %get-tuple-element.68.refs_2_, ...), custom_call_target="tpu_custom_call", output_to_operand_aliasing={{0}: (2, {}), {1}: (3, {})} | custom-call | flops 67108864 | tf_op jit(solution)/shard_map/guest_tile/pallas_call | solution.py:223
  40.8 4.8 %guest_tile.7 = (f32[128,2048]{1,0:T(8,128)S(1)}, f32[128,2048]{1,0:T(8,128)S(1)}) custom-call(s32[1]{0:T(128)} %bitcast.4.refs_0_, bf16[48,2048]{1,0:T(8,128)(2,1)S(1)} %get-tuple-element.60.refs_0_.refs_1_.home_ref, bf16[128,2176]{1,0:T(8,128)(2,1)} %collective-permute-done.5.refs_2_, ...), custom_call_target="tpu_custom_call", output_to_operand_aliasing={{0}: (4, {}), {1}: (5, {})} | custom-call | flops 67108864 | tf_op jit(solution)/shard_map/guest_tile/pallas_call | solution.py:223
  45.6 1.7 %half_gram.1 = (f32[128,128]{1,0:T(8,128)S(1)}, f32[128,128]{1,0:T(8,128)S(1)}, f32[128,2048]{1,0:T(8,128)S(1)}) custom-call(s32[1]{0:T(128)} %bitcast.3.core_ref, bf16[2048,128]{1,0:T(8,128)(2,1)} %own_ref.1, bf16[2048,128]{1,0:T(8,128)(2,1)} %collective-permute-done.4.pair_ref, ...), custom_call_target="tpu_custom_call", output_to_operand_aliasing={{2}: (3, {})} | custom-call | flops 67108864 | tf_op jit(solution)/shard_map/half_gram/pallas_call | solution.py:223
  47.3 2.5 %collective-permute-start.7 = (f32[128,128]{1,0:T(8,128)S(1)}, f32[128,128]{1,0:T(8,128)S(1)}, u32[]{:S(2)}, u32[]{:S(2)}) collective-permute-start(f32[128,128]{1,0:T(8,128)S(1)} %get-tuple-element.79), channel_id=1, source_target_pairs={{0,2},{2,0},{1,3},{3,1},{4,6},{6,4},{5,7},{7,5},{8,10},{10,8},{9,1... | collective-permute-start | bytes 196616 | tf_op jit(solution)/shard_map/ppermute | solution.py:347
  50.7 2.2 %collective-permute-start.8 = (f32[128,128]{1,0:T(8,128)S(1)}, f32[128,128]{1,0:T(8,128)S(1)}, u32[]{:S(2)}, u32[]{:S(2)}) collective-permute-start(f32[128,128]{1,0:T(8,128)S(1)} %add.24.value_ref), channel_id=1, source_target_pairs={{2,3},{3,2},{6,7},{7,6},{10,11},{11,10},{14,15},{15,14},{18,19},{1... | collective-permute-start | bytes 196616 | tf_op jit(solution)/shard_map/ppermute | solution.py:388
  54.2 1.5 %collective-permute-done.8.crossed_ref = f32[128,128]{1,0:T(8,128)S(1)} collective-permute-done((f32[128,128]{1,0:T(8,128)S(1)}, f32[128,128]{1,0:T(8,128)S(1)}, u32[]{:S(2)}, u32[]{:S(2)}) %collective-permute-start.8) | collective-permute-done | bytes 65568 | tf_op jit(solution)/shard_map/ppermute | solution.py:388
  55.8 1.6 %collective-permute-start.10 = (bf16[128,128]{1,0:T(8,128)(2,1)S(1)}, bf16[128,128]{1,0:T(8,128)(2,1)S(1)}, u32[]{:S(2)}, u32[]{:S(2)}) collective-permute-start(bf16[128,128]{1,0:T(8,128)(2,1)S(1)} %convert_element_type.28), channel_id=1, source_target_pairs={{0,16},{2,18},{4,20},{6,22},{8,24},{10,26},{12,28},{14,30},{16,0},... | collective-permute-start | bytes 98312 | tf_op jit(solution)/shard_map/ppermute | solution.py:316
  59.9 2.7 %collective-permute-done.10 = bf16[128,128]{1,0:T(8,128)(2,1)S(1)} collective-permute-done((bf16[128,128]{1,0:T(8,128)(2,1)S(1)}, bf16[128,128]{1,0:T(8,128)(2,1)S(1)}, u32[]{:S(2)}, u32[]{:S(2)}) %collective-permute-start.10) | collective-permute-done | bytes 32800 | tf_op jit(solution)/shard_map/ppermute | solution.py:316
  63.9 2.4 %collective-permute-done.11 = bf16[128,128]{1,0:T(8,128)(2,1)S(1)} collective-permute-done((bf16[128,128]{1,0:T(8,128)(2,1)S(1)}, bf16[128,128]{1,0:T(8,128)(2,1)S(1)}, u32[]{:S(2)}, u32[]{:S(2)}) %collective-permute-start.11) | collective-permute-done | bytes 32800 | tf_op jit(solution)/shard_map/ppermute | solution.py:316
  68.8 1.9 %collective-permute-done.12 = f32[128,128]{1,0:T(8,128)S(1)} collective-permute-done((f32[128,128]{1,0:T(8,128)S(1)}, f32[128,128]{1,0:T(8,128)S(1)}, u32[]{:S(2)}, u32[]{:S(2)}) %collective-permute-start.12) | collective-permute-done | bytes 65568 | tf_op jit(solution)/shard_map/ppermute | solution.py:316
  72.3 2.8 %collective-permute-done.13 = bf16[128,128]{1,0:T(8,128)(2,1)S(1)} collective-permute-done((bf16[128,128]{1,0:T(8,128)(2,1)S(1)}, bf16[128,128]{1,0:T(8,128)(2,1)S(1)}, u32[]{:S(2)}, u32[]{:S(2)}) %collective-permute-start.13) | collective-permute-done | bytes 32800 | tf_op jit(solution)/shard_map/ppermute | solution.py:316
  76.4 1.9 %collective-permute-done.14 = f32[128,128]{1,0:T(8,128)S(1)} collective-permute-done((f32[128,128]{1,0:T(8,128)S(1)}, f32[128,128]{1,0:T(8,128)S(1)}, u32[]{:S(2)}, u32[]{:S(2)}) %collective-permute-start.14) | collective-permute-done | bytes 65568 | tf_op jit(solution)/shard_map/ppermute | solution.py:316
  79.1 5.1 %collective-permute-start.16 = (f32[128,128]{1,0:T(8,128)S(1)}, f32[128,128]{1,0:T(8,128)S(1)}, u32[]{:S(2)}, u32[]{:S(2)}) collective-permute-start(f32[128,128]{1,0:T(8,128)S(1)} %add.29), channel_id=1, source_target_pairs={{0,2},{2,0},{4,6},{6,4},{8,10},{10,8},{12,14},{14,12},{16,18},{18,... | collective-permute-start | bytes 196616 | tf_op jit(solution)/shard_map/ppermute | solution.py:316
  84.3 2.4 %piece_tile.15 = f32[2048,128]{1,0:T(8,128)} custom-call(bf16[48,2048]{1,0:T(8,128)(2,1)S(1)} %get-tuple-element.60.refs_0_.refs_1_.home_ref, bf16[128,2176]{1,0:T(8,128)(2,1)S(1)} %collective-permute-done.3.message_ref, f32[128,2048]{1,0:T(8,128)S(1)} %piece_tile.14.total_ref), custom_call_target="tpu_custom_call" | custom-call | flops 67108864 | tf_op jit(solution)/shard_map/piece_tile/pallas_call | solution.py:223
  86.7 2.7 %collective-permute-done.17 = f32[128,128]{1,0:T(8,128)S(1)} collective-permute-done((f32[128,128]{1,0:T(8,128)S(1)}, f32[128,128]{1,0:T(8,128)S(1)}, u32[]{:S(2)}, u32[]{:S(2)}) %collective-permute-start.17) | collective-permute-done | bytes 65568 | tf_op jit(solution)/shard_map/ppermute | solution.py:316
  (37 shorter events, 14.3 us)
Async XLA Ops:
  2.0 18.9 %collective-permute-start = (bf16[128,2176]{1,0:T(8,128)(2,1)S(1)}, bf16[128,2176]{1,0:T(8,128)(2,1)S(1)}, u32[]{:S(2)}, u32[]{:S(2)}) collective-permute-start(bf16[128,2176]{1,0:T(8,128)(2,1)S(1)} %pack.1.message_ref), channel_id=1, source_target_pairs={{0,2},{2,0},{1,3},{3,1},{4,6},{6,4},{5,7},{7,5},{8,10},{10,8},{9,1... | collective-permute-start | bytes 1671176 | tf_op jit(solution)/shard_map/ppermute | solution.py:347
  5.3 19.7 %collective-permute-start.1 = (bf16[128,2176]{1,0:T(8,128)(2,1)S(1)}, bf16[128,2176]{1,0:T(8,128)(2,1)}, u32[]{:S(2)}, u32[]{:S(2)}) collective-permute-start(bf16[128,2176]{1,0:T(8,128)(2,1)S(1)} %pack.1.message_ref), channel_id=1, source_target_pairs={{0,6},{2,4},{4,0},{6,2},{8,14},{10,12},{12,8},{14,10},{16,22},{18,... | collective-permute-start | bytes 1671176 | tf_op jit(solution)/shard_map/ppermute | solution.py:327
  5.3 25.0 %collective-permute-start.2 = (bf16[128,2176]{1,0:T(8,128)(2,1)S(1)}, bf16[128,2176]{1,0:T(8,128)(2,1)}, u32[]{:S(2)}, u32[]{:S(2)}) collective-permute-start(bf16[128,2176]{1,0:T(8,128)(2,1)S(1)} %pack.1.message_ref), channel_id=1, source_target_pairs={{0,252},{2,254},{4,10},{6,8},{8,4},{10,6},{12,18},{14,16},{16,12},... | collective-permute-start | bytes 1671176 | tf_op jit(solution)/shard_map/ppermute | solution.py:327
  18.9 21.9 %collective-permute-start.5 = (bf16[128,2176]{1,0:T(8,128)(2,1)S(1)}, bf16[128,2176]{1,0:T(8,128)(2,1)}, u32[]{:S(2)}, u32[]{:S(2)}) collective-permute-start(bf16[128,2176]{1,0:T(8,128)(2,1)S(1)} %pack.1.message_ref), channel_id=1, source_target_pairs={{250,0},{8,2},{12,6},{2,8},{16,10},{6,12},{20,14},{10,16},{24,18},... | collective-permute-start | bytes 1671176 | tf_op jit(solution)/shard_map/ppermute | solution.py:361
  30.3 10.4 %collective-permute-start.6 = (bf16[128,2176]{1,0:T(8,128)(2,1)}, bf16[128,2176]{1,0:T(8,128)(2,1)}, u32[]{:S(2)}, u32[]{:S(2)}) collective-permute-start(bf16[128,2176]{1,0:T(8,128)(2,1)} %collective-permute-done.2.refs_1_), channel_id=1, source_target_pairs={{0,4},{28,26},{32,36},{60,58},{64,68},{92,90},{96,100},{124,122},{... | collective-permute-start | bytes 1671176 | tf_op jit(solution)/shard_map/ppermute | solution.py:368
  31.8 13.8 %collective-permute-start.4 = (bf16[2048,128]{1,0:T(8,128)(2,1)}, bf16[2048,128]{1,0:T(8,128)(2,1)}, u32[]{:S(2)}, u32[]{:S(2)}) collective-permute-start(bf16[2048,128]{1,0:T(8,128)(2,1)} %own_ref.1), channel_id=1, source_target_pairs={{0,1},{1,0},{2,3},{3,2},{4,5},{5,4},{6,7},{7,6},{8,9},{9,8},{10,11... | collective-permute-start | bytes 1572872 | tf_op jit(solution)/shard_map/ppermute | solution.py:364
  32.7 20.2 %collective-permute-start.9 = (bf16[128,2176]{1,0:T(8,128)(2,1)}, bf16[128,2176]{1,0:T(8,128)(2,1)S(1)}, u32[]{:S(2)}, u32[]{:S(2)}) collective-permute-start(bf16[128,2176]{1,0:T(8,128)(2,1)} %collective-permute-done.1.refs_1_), channel_id=1, source_target_pairs={{0,2},{2,0},{1,3},{3,1},{4,6},{6,4},{5,7},{7,5},{8,10},{10,8},{9,1... | collective-permute-start | bytes 1671176 | tf_op jit(solution)/shard_map/ppermute | solution.py:347
  47.3 3.4 %collective-permute-start.7 = (f32[128,128]{1,0:T(8,128)S(1)}, f32[128,128]{1,0:T(8,128)S(1)}, u32[]{:S(2)}, u32[]{:S(2)}) collective-permute-start(f32[128,128]{1,0:T(8,128)S(1)} %get-tuple-element.79), channel_id=1, source_target_pairs={{0,2},{2,0},{1,3},{3,1},{4,6},{6,4},{5,7},{7,5},{8,10},{10,8},{9,1... | collective-permute-start | bytes 196616 | tf_op jit(solution)/shard_map/ppermute | solution.py:347
  50.7 5.0 %collective-permute-start.8 = (f32[128,128]{1,0:T(8,128)S(1)}, f32[128,128]{1,0:T(8,128)S(1)}, u32[]{:S(2)}, u32[]{:S(2)}) collective-permute-start(f32[128,128]{1,0:T(8,128)S(1)} %add.24.value_ref), channel_id=1, source_target_pairs={{2,3},{3,2},{6,7},{7,6},{10,11},{11,10},{14,15},{15,14},{18,19},{1... | collective-permute-start | bytes 196616 | tf_op jit(solution)/shard_map/ppermute | solution.py:388
  55.8 6.8 %collective-permute-start.10 = (bf16[128,128]{1,0:T(8,128)(2,1)S(1)}, bf16[128,128]{1,0:T(8,128)(2,1)S(1)}, u32[]{:S(2)}, u32[]{:S(2)}) collective-permute-start(bf16[128,128]{1,0:T(8,128)(2,1)S(1)} %convert_element_type.28), channel_id=1, source_target_pairs={{0,16},{2,18},{4,20},{6,22},{8,24},{10,26},{12,28},{14,30},{16,0},... | collective-permute-start | bytes 98312 | tf_op jit(solution)/shard_map/ppermute | solution.py:316
  57.4 10.2 %collective-permute-start.3 = (bf16[128,2176]{1,0:T(8,128)(2,1)}, bf16[128,2176]{1,0:T(8,128)(2,1)S(1)}, u32[]{:S(2)}, u32[]{:S(2)}) collective-permute-start(bf16[128,2176]{1,0:T(8,128)(2,1)} %collective-permute-done.2.refs_1_), channel_id=1, source_target_pairs={{0,2},{2,0},{1,3},{3,1},{4,6},{6,4},{5,7},{7,5},{8,10},{10,8},{9,1... | collective-permute-start | bytes 1671176 | tf_op jit(solution)/shard_map/ppermute | solution.py:347
  62.6 3.8 %collective-permute-start.11 = (bf16[128,128]{1,0:T(8,128)(2,1)S(1)}, bf16[128,128]{1,0:T(8,128)(2,1)S(1)}, u32[]{:S(2)}, u32[]{:S(2)}) collective-permute-start(bf16[128,128]{1,0:T(8,128)(2,1)S(1)} %add_convert_fusion.1), channel_id=1, source_target_pairs={{0,8},{2,10},{4,12},{6,14},{8,0},{10,2},{12,4},{14,6},{16,24},{18,... | collective-permute-start | bytes 98312 | tf_op jit(solution)/shard_map/ppermute | solution.py:316
  66.4 4.4 %collective-permute-start.12 = (f32[128,128]{1,0:T(8,128)S(1)}, f32[128,128]{1,0:T(8,128)S(1)}, u32[]{:S(2)}, u32[]{:S(2)}) collective-permute-start(f32[128,128]{1,0:T(8,128)S(1)} %convert_add_fusion.1), channel_id=1, source_target_pairs={{0,4},{2,6},{4,0},{6,2},{8,12},{10,14},{12,8},{14,10},{16,20},{18,... | collective-permute-start | bytes 196616 | tf_op jit(solution)/shard_map/ppermute | solution.py:316
  70.7 4.4 %collective-permute-start.13 = (bf16[128,128]{1,0:T(8,128)(2,1)S(1)}, bf16[128,128]{1,0:T(8,128)(2,1)S(1)}, u32[]{:S(2)}, u32[]{:S(2)}) collective-permute-start(bf16[128,128]{1,0:T(8,128)(2,1)S(1)} %add_convert_fusion), channel_id=1, source_target_pairs={{0,128},{2,130},{4,132},{6,134},{8,136},{10,138},{12,140},{14,142}... | collective-permute-start | bytes 98312 | tf_op jit(solution)/shard_map/ppermute | solution.py:316
  75.1 3.2 %collective-permute-start.14 = (f32[128,128]{1,0:T(8,128)S(1)}, f32[128,128]{1,0:T(8,128)S(1)}, u32[]{:S(2)}, u32[]{:S(2)}) collective-permute-start(f32[128,128]{1,0:T(8,128)S(1)} %convert_add_fusion), channel_id=1, source_target_pairs={{0,64},{2,66},{4,68},{6,70},{8,72},{10,74},{12,76},{14,78},{16,80}... | collective-permute-start | bytes 196616 | tf_op jit(solution)/shard_map/ppermute | solution.py:316
  78.3 8.4 %collective-permute-start.15 = (f32[128,128]{1,0:T(8,128)S(1)}, f32[128,128]{1,0:T(8,128)S(1)}, u32[]{:S(2)}, u32[]{:S(2)}) collective-permute-start(f32[128,128]{1,0:T(8,128)S(1)} %add.29), channel_id=1, source_target_pairs={{0,32},{2,34},{4,36},{6,38},{8,40},{10,42},{12,44},{14,46},{16,48}... | collective-permute-start | bytes 196616 | tf_op jit(solution)/shard_map/ppermute | solution.py:316
  79.1 7.6 %collective-permute-start.16 = (f32[128,128]{1,0:T(8,128)S(1)}, f32[128,128]{1,0:T(8,128)S(1)}, u32[]{:S(2)}, u32[]{:S(2)}) collective-permute-start(f32[128,128]{1,0:T(8,128)S(1)} %add.29), channel_id=1, source_target_pairs={{0,2},{2,0},{4,6},{6,4},{8,10},{10,8},{12,14},{14,12},{16,18},{18,... | collective-permute-start | bytes 196616 | tf_op jit(solution)/shard_map/ppermute | solution.py:316
  84.2 5.2 %collective-permute-start.17 = (f32[128,128]{1,0:T(8,128)S(1)}, f32[128,128]{1,0:T(8,128)S(1)}, u32[]{:S(2)}, u32[]{:S(2)}) collective-permute-start(f32[128,128]{1,0:T(8,128)S(1)} %add.29), channel_id=1, source_target_pairs={{0,34},{2,32},{4,38},{6,36},{8,42},{10,40},{12,46},{14,44},{16,50}... | collective-permute-start | bytes 196616 | tf_op jit(solution)/shard_map/ppermute | solution.py:316

commit v6 on v5

--- a/solution.py
+++ b/solution.py
@@ -327,20 +327,11 @@
     return lax.ppermute(value, BLK, pairs)
 
 
-def from_far(length):
+def from_far(value):
     count = lax.axis_size(BLK)
-    direct, passed = [], []
-    for block in range(count):
-        place = block // 2 % length
-        if block % 2 == 0:
-            source, between, over = block - 3, block - 2, place == 1
-        else:
-            source, between, over = block + 3, block + 1, place == length - 2
-        if over:
-            passed.append((between % count, block))
-        else:
-            direct.append((source % count, block))
-    return tuple(functools.partial(lax.ppermute, axis_name=BLK, perm=pairs) for pairs in (direct, passed))
+    return lax.ppermute(
+        value, BLK, [((b - 3 if b % 2 == 0 else b + 3) % count, b) for b in range(count)]
+    )
 
 
 def core_swap(value):
@@ -357,22 +348,18 @@
 
     first, home = home_tile(message, count)
     first, late = lax.optimization_barrier((first, message))
-    direct, passed = from_far(sizes[2])
-    far = direct(late)
+    far = from_far(late)
     (first,) = guest_tile(home, (other,), first)
     first, even, later = lax.optimization_barrier((first, even, directions))
     pair = lax.ppermute(later, "rhs", [(0, 1), (1, 0)])
     even_other = core_swap(even)
     second, first = guest_tile(home, (even,), None, (first,))
     second, odd = lax.optimization_barrier((second, odd))
-    over = passed(odd)
     odd_other = core_swap(odd)
     second, first = guest_tile(home, (odd,), second, (first,))
-    second, far, over = lax.optimization_barrier((second, far, over))
+    second, far = lax.optimization_barrier((second, far))
     core = lax.axis_index("core").astype(jnp.int32)
-    place = lax.axis_index("z")
-    is_over = jnp.where(core == 0, place == 1, place == sizes[2] - 2).astype(jnp.int32).reshape(1)
-    first, second = guest_tile(home, (far, over), first, (second,), is_over)
+    first, second = guest_tile(home, (far,), first, (second,))
     keep, give, product = half_gram(core.reshape(1), directions, pair, first, second)
 
     work = [(guest, piece) for guest in (even_other, odd_other) for piece in range(PIECES)]

time: 90.3 us -> 86.3 us (0.956)
  starting transfers between devices: 34.3 us -> 29 us
  waiting for transfers between devices: 17.2 us -> 19.6 us
  Pallas kernels: 36.9 us -> 35.6 us
    ppermute x2 -> x1, starting transfers between devices: 3.39 us -> 0.09 us  [from_far(): lax.ppermute(value, BLK, [((b - 3 if b % 2 == 0 else b + 3) % count, b) f...]
    ppermute x2, waiting for transfers between devices: 0.4 us -> 2.23 us  [from_neighbour(): return lax.ppermute(value, BLK, pairs)]
    pallas_call x16, Pallas kernels: 36.9 us -> 35.6 us  [kernel_call(): pl.pallas_call(body, out_shape=outs, in_specs=[pl.BlockSpec(memory_space=...]
    ppermute x4, starting transfers between devices: 9 us -> 8.1 us  [core_swap(): return lax.ppermute(value, 'core', [(0, 1), (1, 0)])]
  transfers between devices with their start and end apart: 18 -> 17, of which waited for: 9 -> 10; matrix products, arithmetic and copies ran while one was open for 0% -> 0% of each run, Pallas kernels for 39% -> 40%
where the time goes in v6:
time: 86.3 us; the launch traced here: 85.9 us
  Pallas kernels  35.6 us (41%)
  starting transfers between devices  29 us (34%)
  waiting for transfers between devices  19.6 us (23%)
  between operations  0.9 us (1%)
    pallas_call x16, Pallas kernels, kernel_call(): pl.pallas_call(body, out_shape=outs, in_specs=[pl.BlockSpec(memory_space=...  35.6 us
    ppermute x8, waiting for transfers between devices, along_blk(): return lax.ppermute(value, BLK, pairs)  14.1 us
    ppermute x2, starting transfers between devices, from_neighbour(): return lax.ppermute(value, BLK, pairs)  9.49 us
    ppermute x8, starting transfers between devices, along_blk(): return lax.ppermute(value, BLK, pairs)  8.79 us
    ppermute x4, starting transfers between devices, core_swap(): return lax.ppermute(value, 'core', [(0, 1), (1, 0)])  8.1 us
    ppermute x2, waiting for transfers between devices, from_neighbour(): return lax.ppermute(value, BLK, pairs)  2.23 us
    ppermute x1, starting transfers between devices, shards(): crossed = lax.ppermute(value, ('core', 'rhs'), [(2, 3), (3, 2)])  2.21 us
  transfers between devices with their start and end apart: 17, of which 10 were waited for; matrix products, arithmetic and copies ran while one was open for 0% of the time, Pallas kernels for 40%

profile of v6, /device:TPU:1, one launch (start us, length us, event | category | flops | bytes accessed | tf_op | source)
XLA Modules:
  0.0 85.9 jit_solution(16879313945063796831)
XLA Ops:
  0.6 1.3 %pack.1.message_ref = bf16[128,2176]{1,0:T(8,128)(2,1)S(1)} custom-call(bf16[2048,128]{1,0:T(8,128)(2,1)} %own_ref.1, bf16[16,128]{1,0:T(8,128)(2,1)} %bitcast.4, bf16[16,128]{1,0:T(8,128)(2,1)} %bitcast.5, bf16[16,128]{1,0:T(8,128)(2,1)} %bitcast.6), custom_call_target="tpu_custom_call" | custom-call | bytes 1048576 | tf_op jit(solution)/shard_map/pack/pallas_call | solution.py:223
  2.0 3.3 %collective-permute-start = (bf16[128,2176]{1,0:T(8,128)(2,1)S(1)}, bf16[128,2176]{1,0:T(8,128)(2,1)S(1)}, u32[]{:S(2)}, u32[]{:S(2)}) collective-permute-start(bf16[128,2176]{1,0:T(8,128)(2,1)S(1)} %pack.1.message_ref), channel_id=1, source_target_pairs={{0,2},{2,0},{1,3},{3,1},{4,6},{6,4},{5,7},{7,5},{8,10},{10,8},{9,1... | collective-permute-start | bytes 1671176 | tf_op jit(solution)/shard_map/ppermute | solution.py:338
  5.3 9.5 %collective-permute-start.2 = (bf16[128,2176]{1,0:T(8,128)(2,1)S(1)}, bf16[128,2176]{1,0:T(8,128)(2,1)S(1)}, u32[]{:S(2)}, u32[]{:S(2)}) collective-permute-start(bf16[128,2176]{1,0:T(8,128)(2,1)S(1)} %pack.1.message_ref), channel_id=1, source_target_pairs={{0,252},{2,254},{4,10},{6,8},{8,4},{10,6},{12,18},{14,16},{16,12},... | collective-permute-start | bytes 1671176 | tf_op jit(solution)/shard_map/ppermute | solution.py:327
  14.8 4.1 %home_tile.1 = (f32[128,2048]{1,0:T(8,128)S(1)}, bf16[48,2048]{1,0:T(8,128)(2,1)S(1)}) custom-call(bf16[128,2176]{1,0:T(8,128)(2,1)S(1)} %pack.1.message_ref), custom_call_target="tpu_custom_call" | custom-call | flops 67108864 | tf_op jit(solution)/shard_map/home_tile/pallas_call | solution.py:223
  19.0 4.2 %guest_tile.4.refs_2_ = f32[128,2048]{1,0:T(8,128)S(1)} custom-call(bf16[48,2048]{1,0:T(8,128)(2,1)S(1)} %get-tuple-element.59.refs_0_.home_ref, bf16[128,2176]{1,0:T(8,128)(2,1)S(1)} %collective-permute-done.refs_1_, f32[128,2048]{1,0:T(8,128)S(1)} %get-tuple-element.61.refs_2_), custom_call_target="tpu_custom_call", output_to_operand_aliasing={{}: (2, {})} | custom-call | flops 67108864 | tf_op jit(solution)/shard_map/guest_tile/pallas_call | solution.py:223
  23.6 1.8 %collective-permute-start.8 = (bf16[128,2176]{1,0:T(8,128)(2,1)S(1)}, bf16[128,2176]{1,0:T(8,128)(2,1)S(1)}, u32[]{:S(2)}, u32[]{:S(2)}) collective-permute-start(bf16[128,2176]{1,0:T(8,128)(2,1)S(1)} %collective-permute-done.1.refs_1_), channel_id=1, source_target_pairs={{0,2},{2,0},{1,3},{3,1},{4,6},{6,4},{5,7},{7,5},{8,10},{10,8},{9,1... | collective-permute-start | bytes 1671176 | tf_op jit(solution)/shard_map/ppermute | solution.py:338
  25.4 4.2 %guest_tile.5 = (f32[128,2048]{1,0:T(8,128)S(1)}, f32[128,2048]{1,0:T(8,128)S(1)}) custom-call(bf16[48,2048]{1,0:T(8,128)(2,1)S(1)} %get-tuple-element.59.refs_0_.home_ref, bf16[128,2176]{1,0:T(8,128)(2,1)S(1)} %collective-permute-done.1.refs_1_, f32[128,2048]{1,0:T(8,128)S(1)} %guest_tile.4.refs_2_), custom_call_target="tpu_custom_call", output_to_operand_aliasing={{1}: (2, {})} | custom-call | flops 67108864 | tf_op jit(solution)/shard_map/guest_tile/pallas_call | solution.py:223
  29.6 2.2 %collective-permute-done.2.refs_1_ = bf16[128,2176]{1,0:T(8,128)(2,1)S(1)} collective-permute-done((bf16[128,2176]{1,0:T(8,128)(2,1)S(1)}, bf16[128,2176]{1,0:T(8,128)(2,1)S(1)}, u32[]{:S(2)}, u32[]{:S(2)}) %collective-permute-start.2) | collective-permute-done | bytes 557088 | tf_op jit(solution)/shard_map/ppermute | solution.py:327
  31.9 4.1 %guest_tile.6 = (f32[128,2048]{1,0:T(8,128)S(1)}, f32[128,2048]{1,0:T(8,128)S(1)}) custom-call(bf16[48,2048]{1,0:T(8,128)(2,1)S(1)} %get-tuple-element.59.refs_0_.home_ref, bf16[128,2176]{1,0:T(8,128)(2,1)S(1)} %collective-permute-done.2.refs_1_, f32[128,2048]{1,0:T(8,128)S(1)} %get-tuple-element.67.refs_2_, ...), custom_call_target="tpu_custom_call", output_to_operand_aliasing={{0}: (2, {}), {1}: (3, {})} | custom-call | flops 67108864 | tf_op jit(solution)/shard_map/guest_tile/pallas_call | solution.py:223
  36.0 4.8 %guest_tile.7 = (f32[128,2048]{1,0:T(8,128)S(1)}, f32[128,2048]{1,0:T(8,128)S(1)}) custom-call(bf16[48,2048]{1,0:T(8,128)(2,1)S(1)} %get-tuple-element.59.refs_0_.home_ref, bf16[128,2176]{1,0:T(8,128)(2,1)} %collective-permute-done.5.refs_1_, f32[128,2048]{1,0:T(8,128)S(1)} %get-tuple-element.72.refs_2_, ...), custom_call_target="tpu_custom_call", output_to_operand_aliasing={{0}: (2, {}), {1}: (3, {})} | custom-call | flops 67108864 | tf_op jit(solution)/shard_map/guest_tile/pallas_call | solution.py:223
  41.7 1.7 %half_gram.1 = (f32[128,128]{1,0:T(8,128)S(1)}, f32[128,128]{1,0:T(8,128)S(1)}, f32[128,2048]{1,0:T(8,128)S(1)}) custom-call(s32[1]{0:T(128)} %bitcast.3.core_ref, bf16[2048,128]{1,0:T(8,128)(2,1)} %own_ref.1, bf16[2048,128]{1,0:T(8,128)(2,1)} %collective-permute-done.4.pair_ref, ...), custom_call_target="tpu_custom_call", output_to_operand_aliasing={{2}: (3, {})} | custom-call | flops 67108864 | tf_op jit(solution)/shard_map/half_gram/pallas_call | solution.py:223
  43.4 2.8 %collective-permute-start.6 = (f32[128,128]{1,0:T(8,128)S(1)}, f32[128,128]{1,0:T(8,128)S(1)}, u32[]{:S(2)}, u32[]{:S(2)}) collective-permute-start(f32[128,128]{1,0:T(8,128)S(1)} %get-tuple-element.77), channel_id=1, source_target_pairs={{0,2},{2,0},{1,3},{3,1},{4,6},{6,4},{5,7},{7,5},{8,10},{10,8},{9,1... | collective-permute-start | bytes 196616 | tf_op jit(solution)/shard_map/ppermute | solution.py:338
  47.1 2.2 %collective-permute-start.7 = (f32[128,128]{1,0:T(8,128)S(1)}, f32[128,128]{1,0:T(8,128)S(1)}, u32[]{:S(2)}, u32[]{:S(2)}) collective-permute-start(f32[128,128]{1,0:T(8,128)S(1)} %add.24.value_ref), channel_id=1, source_target_pairs={{2,3},{3,2},{6,7},{7,6},{10,11},{11,10},{14,15},{15,14},{18,19},{1... | collective-permute-start | bytes 196616 | tf_op jit(solution)/shard_map/ppermute | solution.py:375
  50.6 1.5 %collective-permute-done.7.crossed_ref = f32[128,128]{1,0:T(8,128)S(1)} collective-permute-done((f32[128,128]{1,0:T(8,128)S(1)}, f32[128,128]{1,0:T(8,128)S(1)}, u32[]{:S(2)}, u32[]{:S(2)}) %collective-permute-start.7) | collective-permute-done | bytes 65568 | tf_op jit(solution)/shard_map/ppermute | solution.py:375
  54.9 4.1 %collective-permute-done.9 = bf16[128,128]{1,0:T(8,128)(2,1)S(1)} collective-permute-done((bf16[128,128]{1,0:T(8,128)(2,1)S(1)}, bf16[128,128]{1,0:T(8,128)(2,1)S(1)}, u32[]{:S(2)}, u32[]{:S(2)}) %collective-permute-start.9) | collective-permute-done | bytes 32800 | tf_op jit(solution)/shard_map/ppermute | solution.py:316
  60.6 2.4 %collective-permute-done.10 = bf16[128,128]{1,0:T(8,128)(2,1)S(1)} collective-permute-done((bf16[128,128]{1,0:T(8,128)(2,1)S(1)}, bf16[128,128]{1,0:T(8,128)(2,1)S(1)}, u32[]{:S(2)}, u32[]{:S(2)}) %collective-permute-start.10) | collective-permute-done | bytes 32800 | tf_op jit(solution)/shard_map/ppermute | solution.py:316
  63.0 2.2 %collective-permute-start.11 = (f32[128,128]{1,0:T(8,128)S(1)}, f32[128,128]{1,0:T(8,128)S(1)}, u32[]{:S(2)}, u32[]{:S(2)}) collective-permute-start(f32[128,128]{1,0:T(8,128)S(1)} %convert_add_fusion.1), channel_id=1, source_target_pairs={{0,4},{2,6},{4,0},{6,2},{8,12},{10,14},{12,8},{14,10},{16,20},{18,... | collective-permute-start | bytes 196616 | tf_op jit(solution)/shard_map/ppermute | solution.py:316
  66.5 1.4 %collective-permute-done.11 = f32[128,128]{1,0:T(8,128)S(1)} collective-permute-done((f32[128,128]{1,0:T(8,128)S(1)}, f32[128,128]{1,0:T(8,128)S(1)}, u32[]{:S(2)}, u32[]{:S(2)}) %collective-permute-start.11) | collective-permute-done | bytes 65568 | tf_op jit(solution)/shard_map/ppermute | solution.py:316
  69.2 3.0 %collective-permute-done.12 = bf16[128,128]{1,0:T(8,128)(2,1)S(1)} collective-permute-done((bf16[128,128]{1,0:T(8,128)(2,1)S(1)}, bf16[128,128]{1,0:T(8,128)(2,1)S(1)}, u32[]{:S(2)}, u32[]{:S(2)}) %collective-permute-start.12) | collective-permute-done | bytes 32800 | tf_op jit(solution)/shard_map/ppermute | solution.py:316
  73.6 1.9 %collective-permute-done.13 = f32[128,128]{1,0:T(8,128)S(1)} collective-permute-done((f32[128,128]{1,0:T(8,128)S(1)}, f32[128,128]{1,0:T(8,128)S(1)}, u32[]{:S(2)}, u32[]{:S(2)}) %collective-permute-start.13) | collective-permute-done | bytes 65568 | tf_op jit(solution)/shard_map/ppermute | solution.py:316
  75.7 4.3 %collective-permute-start.15 = (f32[128,128]{1,0:T(8,128)S(1)}, f32[128,128]{1,0:T(8,128)S(1)}, u32[]{:S(2)}, u32[]{:S(2)}) collective-permute-start(f32[128,128]{1,0:T(8,128)S(1)} %add.29), channel_id=1, source_target_pairs={{0,2},{2,0},{4,6},{6,4},{8,10},{10,8},{12,14},{14,12},{16,18},{18,... | collective-permute-start | bytes 196616 | tf_op jit(solution)/shard_map/ppermute | solution.py:316
  80.0 1.4 %collective-permute-start.16 = (f32[128,128]{1,0:T(8,128)S(1)}, f32[128,128]{1,0:T(8,128)S(1)}, u32[]{:S(2)}, u32[]{:S(2)}) collective-permute-start(f32[128,128]{1,0:T(8,128)S(1)} %add.29), channel_id=1, source_target_pairs={{0,34},{2,32},{4,38},{6,36},{8,42},{10,40},{12,46},{14,44},{16,50}... | collective-permute-start | bytes 196616 | tf_op jit(solution)/shard_map/ppermute | solution.py:316
  81.4 2.4 %piece_tile.15 = f32[2048,128]{1,0:T(8,128)} custom-call(bf16[48,2048]{1,0:T(8,128)(2,1)S(1)} %get-tuple-element.59.refs_0_.home_ref, bf16[128,2176]{1,0:T(8,128)(2,1)S(1)} %collective-permute-done.3.message_ref, f32[128,2048]{1,0:T(8,128)S(1)} %piece_tile.14.total_ref), custom_call_target="tpu_custom_call" | custom-call | flops 67108864 | tf_op jit(solution)/shard_map/piece_tile/pallas_call | solution.py:223
  83.8 1.4 %collective-permute-done.16 = f32[128,128]{1,0:T(8,128)S(1)} collective-permute-done((f32[128,128]{1,0:T(8,128)S(1)}, f32[128,128]{1,0:T(8,128)S(1)}, u32[]{:S(2)}, u32[]{:S(2)}) %collective-permute-start.16) | collective-permute-done | bytes 65568 | tf_op jit(solution)/shard_map/ppermute | solution.py:316
  (35 shorter events, 12.6 us)
Async XLA Ops:
  2.0 17.0 %collective-permute-start = (bf16[128,2176]{1,0:T(8,128)(2,1)S(1)}, bf16[128,2176]{1,0:T(8,128)(2,1)S(1)}, u32[]{:S(2)}, u32[]{:S(2)}) collective-permute-start(bf16[128,2176]{1,0:T(8,128)(2,1)S(1)} %pack.1.message_ref), channel_id=1, source_target_pairs={{0,2},{2,0},{1,3},{3,1},{4,6},{6,4},{5,7},{7,5},{8,10},{10,8},{9,1... | collective-permute-start | bytes 1671176 | tf_op jit(solution)/shard_map/ppermute | solution.py:338
  5.3 17.9 %collective-permute-start.1 = (bf16[128,2176]{1,0:T(8,128)(2,1)S(1)}, bf16[128,2176]{1,0:T(8,128)(2,1)S(1)}, u32[]{:S(2)}, u32[]{:S(2)}) collective-permute-start(bf16[128,2176]{1,0:T(8,128)(2,1)S(1)} %pack.1.message_ref), channel_id=1, source_target_pairs={{0,6},{2,4},{4,0},{6,2},{8,14},{10,12},{12,8},{14,10},{16,22},{18,... | collective-permute-start | bytes 1671176 | tf_op jit(solution)/shard_map/ppermute | solution.py:327
  5.3 26.6 %collective-permute-start.2 = (bf16[128,2176]{1,0:T(8,128)(2,1)S(1)}, bf16[128,2176]{1,0:T(8,128)(2,1)S(1)}, u32[]{:S(2)}, u32[]{:S(2)}) collective-permute-start(bf16[128,2176]{1,0:T(8,128)(2,1)S(1)} %pack.1.message_ref), channel_id=1, source_target_pairs={{0,252},{2,254},{4,10},{6,8},{8,4},{10,6},{12,18},{14,16},{16,12},... | collective-permute-start | bytes 1671176 | tf_op jit(solution)/shard_map/ppermute | solution.py:327
  18.9 17.1 %collective-permute-start.5 = (bf16[128,2176]{1,0:T(8,128)(2,1)S(1)}, bf16[128,2176]{1,0:T(8,128)(2,1)}, u32[]{:S(2)}, u32[]{:S(2)}) collective-permute-start(bf16[128,2176]{1,0:T(8,128)(2,1)S(1)} %pack.1.message_ref), channel_id=1, source_target_pairs={{250,0},{8,2},{254,4},{12,6},{2,8},{16,10},{6,12},{20,14},{10,16},... | collective-permute-start | bytes 1671176 | tf_op jit(solution)/shard_map/ppermute | solution.py:332
  23.2 18.5 %collective-permute-start.4 = (bf16[2048,128]{1,0:T(8,128)(2,1)}, bf16[2048,128]{1,0:T(8,128)(2,1)}, u32[]{:S(2)}, u32[]{:S(2)}) collective-permute-start(bf16[2048,128]{1,0:T(8,128)(2,1)} %own_ref.1), channel_id=1, source_target_pairs={{0,1},{1,0},{2,3},{3,2},{4,5},{5,4},{6,7},{7,6},{8,9},{9,8},{10,11... | collective-permute-start | bytes 1572872 | tf_op jit(solution)/shard_map/ppermute | solution.py:354
  23.6 25.8 %collective-permute-start.8 = (bf16[128,2176]{1,0:T(8,128)(2,1)S(1)}, bf16[128,2176]{1,0:T(8,128)(2,1)S(1)}, u32[]{:S(2)}, u32[]{:S(2)}) collective-permute-start(bf16[128,2176]{1,0:T(8,128)(2,1)S(1)} %collective-permute-done.1.refs_1_), channel_id=1, source_target_pairs={{0,2},{2,0},{1,3},{3,1},{4,6},{6,4},{5,7},{7,5},{8,10},{10,8},{9,1... | collective-permute-start | bytes 1671176 | tf_op jit(solution)/shard_map/ppermute | solution.py:338
  43.4 3.7 %collective-permute-start.6 = (f32[128,128]{1,0:T(8,128)S(1)}, f32[128,128]{1,0:T(8,128)S(1)}, u32[]{:S(2)}, u32[]{:S(2)}) collective-permute-start(f32[128,128]{1,0:T(8,128)S(1)} %get-tuple-element.77), channel_id=1, source_target_pairs={{0,2},{2,0},{1,3},{3,1},{4,6},{6,4},{5,7},{7,5},{8,10},{10,8},{9,1... | collective-permute-start | bytes 196616 | tf_op jit(solution)/shard_map/ppermute | solution.py:338
  47.1 5.0 %collective-permute-start.7 = (f32[128,128]{1,0:T(8,128)S(1)}, f32[128,128]{1,0:T(8,128)S(1)}, u32[]{:S(2)}, u32[]{:S(2)}) collective-permute-start(f32[128,128]{1,0:T(8,128)S(1)} %add.24.value_ref), channel_id=1, source_target_pairs={{2,3},{3,2},{6,7},{7,6},{10,11},{11,10},{14,15},{15,14},{18,19},{1... | collective-permute-start | bytes 196616 | tf_op jit(solution)/shard_map/ppermute | solution.py:375
  52.3 6.8 %collective-permute-start.9 = (bf16[128,128]{1,0:T(8,128)(2,1)S(1)}, bf16[128,128]{1,0:T(8,128)(2,1)S(1)}, u32[]{:S(2)}, u32[]{:S(2)}) collective-permute-start(bf16[128,128]{1,0:T(8,128)(2,1)S(1)} %convert_element_type.27), channel_id=1, source_target_pairs={{0,16},{2,18},{4,20},{6,22},{8,24},{10,26},{12,28},{14,30},{16,0},... | collective-permute-start | bytes 98312 | tf_op jit(solution)/shard_map/ppermute | solution.py:316
  52.4 12.9 %collective-permute-start.3 = (bf16[128,2176]{1,0:T(8,128)(2,1)S(1)}, bf16[128,2176]{1,0:T(8,128)(2,1)S(1)}, u32[]{:S(2)}, u32[]{:S(2)}) collective-permute-start(bf16[128,2176]{1,0:T(8,128)(2,1)S(1)} %collective-permute-done.2.refs_1_), channel_id=1, source_target_pairs={{0,2},{2,0},{1,3},{3,1},{4,6},{6,4},{5,7},{7,5},{8,10},{10,8},{9,1... | collective-permute-start | bytes 1671176 | tf_op jit(solution)/shard_map/ppermute | solution.py:338
  59.0 4.0 %collective-permute-start.10 = (bf16[128,128]{1,0:T(8,128)(2,1)S(1)}, bf16[128,128]{1,0:T(8,128)(2,1)S(1)}, u32[]{:S(2)}, u32[]{:S(2)}) collective-permute-start(bf16[128,128]{1,0:T(8,128)(2,1)S(1)} %add_convert_fusion.1), channel_id=1, source_target_pairs={{0,8},{2,10},{4,12},{6,14},{8,0},{10,2},{12,4},{14,6},{16,24},{18,... | collective-permute-start | bytes 98312 | tf_op jit(solution)/shard_map/ppermute | solution.py:316
  63.0 4.8 %collective-permute-start.11 = (f32[128,128]{1,0:T(8,128)S(1)}, f32[128,128]{1,0:T(8,128)S(1)}, u32[]{:S(2)}, u32[]{:S(2)}) collective-permute-start(f32[128,128]{1,0:T(8,128)S(1)} %convert_add_fusion.1), channel_id=1, source_target_pairs={{0,4},{2,6},{4,0},{6,2},{8,12},{10,14},{12,8},{14,10},{16,20},{18,... | collective-permute-start | bytes 196616 | tf_op jit(solution)/shard_map/ppermute | solution.py:316
  67.9 4.4 %collective-permute-start.12 = (bf16[128,128]{1,0:T(8,128)(2,1)S(1)}, bf16[128,128]{1,0:T(8,128)(2,1)S(1)}, u32[]{:S(2)}, u32[]{:S(2)}) collective-permute-start(bf16[128,128]{1,0:T(8,128)(2,1)S(1)} %add_convert_fusion), channel_id=1, source_target_pairs={{0,128},{2,130},{4,132},{6,134},{8,136},{10,138},{12,140},{14,142}... | collective-permute-start | bytes 98312 | tf_op jit(solution)/shard_map/ppermute | solution.py:316
  72.2 3.2 %collective-permute-start.13 = (f32[128,128]{1,0:T(8,128)S(1)}, f32[128,128]{1,0:T(8,128)S(1)}, u32[]{:S(2)}, u32[]{:S(2)}) collective-permute-start(f32[128,128]{1,0:T(8,128)S(1)} %convert_add_fusion), channel_id=1, source_target_pairs={{0,64},{2,66},{4,68},{6,70},{8,72},{10,74},{12,76},{14,78},{16,80}... | collective-permute-start | bytes 196616 | tf_op jit(solution)/shard_map/ppermute | solution.py:316
  75.4 8.4 %collective-permute-start.14 = (f32[128,128]{1,0:T(8,128)S(1)}, f32[128,128]{1,0:T(8,128)S(1)}, u32[]{:S(2)}, u32[]{:S(2)}) collective-permute-start(f32[128,128]{1,0:T(8,128)S(1)} %add.29), channel_id=1, source_target_pairs={{0,32},{2,34},{4,36},{6,38},{8,40},{10,42},{12,44},{14,46},{16,48}... | collective-permute-start | bytes 196616 | tf_op jit(solution)/shard_map/ppermute | solution.py:316
  75.7 8.1 %collective-permute-start.15 = (f32[128,128]{1,0:T(8,128)S(1)}, f32[128,128]{1,0:T(8,128)S(1)}, u32[]{:S(2)}, u32[]{:S(2)}) collective-permute-start(f32[128,128]{1,0:T(8,128)S(1)} %add.29), channel_id=1, source_target_pairs={{0,2},{2,0},{4,6},{6,4},{8,10},{10,8},{12,14},{14,12},{16,18},{18,... | collective-permute-start | bytes 196616 | tf_op jit(solution)/shard_map/ppermute | solution.py:316
  80.0 5.2 %collective-permute-start.16 = (f32[128,128]{1,0:T(8,128)S(1)}, f32[128,128]{1,0:T(8,128)S(1)}, u32[]{:S(2)}, u32[]{:S(2)}) collective-permute-start(f32[128,128]{1,0:T(8,128)S(1)} %add.29), channel_id=1, source_target_pairs={{0,34},{2,32},{4,38},{6,36},{8,42},{10,40},{12,46},{14,44},{16,50}... | collective-permute-start | bytes 196616 | tf_op jit(solution)/shard_map/ppermute | solution.py:316

commit v7 on v6

--- a/solution.py
+++ b/solution.py
@@ -383,16 +383,20 @@
         )
 
     stages = (
-        ((0, 0, 4, 0), 2, True), ((0, 0, 2, 0), 1, True), ((0, 0, 1, 0), 1, False),
-        ((2, 0, 0, 0), 1, True), ((1, 0, 0, 0), 1, False),
-    )
-    for move, pieces, rounded in stages:
-        sent = value.astype(jnp.bfloat16) if rounded else value
+        (((0, 0, 4, 0),), 2),
+        (((0, 0, 1, 0), (0, 0, 2, 0), (0, 0, 3, 0)), 2),
+        (((1, 0, 0, 0), (2, 0, 0, 0), (3, 0, 0, 0)), 2),
+    )
+    for moves, pieces in stages:
+        sent = value.astype(jnp.bfloat16)
         product, sent = lax.optimization_barrier((product, sent))
-        moved = moved_by(sent, move)
+        moved = [moved_by(sent, move) for move in moves]
         product = advance(product, pieces)
-        sent, product, moved = lax.optimization_barrier((sent, product, moved))
-        value = sent.astype(jnp.float32) + moved.astype(jnp.float32)
+        sent, product, *moved = lax.optimization_barrier((sent, product, *moved))
+        value, *moved = [term.astype(jnp.float32) for term in (sent, *moved)]
+        value = value + moved[0]
+        if len(moved) > 1:
+            value = value + (moved[1] + moved[2])
 
     product, value = lax.optimization_barrier((product, value))
     moved = [moved_by(value, move) for move in ((0, 1, 0, 0), (0, 0, 0, 1), (0, 1, 0, 1))]

time: 86.3 us -> 84.8 us (0.983)
  waiting for transfers between devices: 19.6 us -> 8.94 us
  starting transfers between devices: 29 us -> 35.1 us
  Pallas kernels: 35.6 us -> 38.9 us
    ppermute x8 -> x10, waiting for transfers between devices: 14.1 us -> 6.5 us  [along_blk(): return lax.ppermute(value, BLK, pairs)]
    ppermute x4, starting transfers between devices: 8.1 us -> 11.7 us  [core_swap(): return lax.ppermute(value, 'core', [(0, 1), (1, 0)])]
    pallas_call x16, Pallas kernels: 35.6 us -> 38.9 us  [kernel_call(): pl.pallas_call(body, out_shape=outs, in_specs=[pl.BlockSpec(memory_space=...]
    ppermute x8 -> x10, starting transfers between devices: 8.79 us -> 11.1 us  [along_blk(): return lax.ppermute(value, BLK, pairs)]
    ppermute x2, waiting for transfers between devices: 2.23 us -> 0.01 us  [from_neighbour(): return lax.ppermute(value, BLK, pairs)]
  transfers between devices with their start and end apart: 17 -> 19, of which waited for: 10 -> 4; matrix products, arithmetic and copies ran while one was open for 0% -> 0% of each run, Pallas kernels for 40% -> 43%
where the time goes in v7:
time: 84.8 us; the launch traced here: 84.6 us
  Pallas kernels  38.9 us (46%)
  starting transfers between devices  35.1 us (41%)
  waiting for transfers between devices  8.94 us (11%)
  between operations  0.96 us (1%)
    pallas_call x16, Pallas kernels, kernel_call(): pl.pallas_call(body, out_shape=outs, in_specs=[pl.BlockSpec(memory_space=...  38.9 us
    ppermute x4, starting transfers between devices, core_swap(): return lax.ppermute(value, 'core', [(0, 1), (1, 0)])  11.7 us
    ppermute x10, starting transfers between devices, along_blk(): return lax.ppermute(value, BLK, pairs)  11.1 us
    ppermute x2, starting transfers between devices, from_neighbour(): return lax.ppermute(value, BLK, pairs)  9.49 us
    ppermute x10, waiting for transfers between devices, along_blk(): return lax.ppermute(value, BLK, pairs)  6.5 us
    ppermute x1, starting transfers between devices, shards(): crossed = lax.ppermute(value, ('core', 'rhs'), [(2, 3), (3, 2)])  2.23 us
  transfers between devices with their start and end apart: 19, of which 4 were waited for; matrix products, arithmetic and copies ran while one was open for 0% of the time, Pallas kernels for 43%

profile of v7, /device:TPU:1, one launch (start us, length us, event | category | flops | bytes accessed | tf_op | source)
XLA Modules:
  0.0 84.6 jit_solution(17585573316626926645)
XLA Ops:
  0.6 2.1 %pack.1.message_ref = bf16[128,2176]{1,0:T(8,128)(2,1)} custom-call(bf16[2048,128]{1,0:T(8,128)(2,1)} %own_ref.1, bf16[16,128]{1,0:T(8,128)(2,1)} %bitcast.4, bf16[16,128]{1,0:T(8,128)(2,1)} %bitcast.5, bf16[16,128]{1,0:T(8,128)(2,1)} %bitcast.6), custom_call_target="tpu_custom_call" | custom-call | bytes 1048576 | tf_op jit(solution)/shard_map/pack/pallas_call | solution.py:223
  2.8 3.3 %collective-permute-start = (bf16[128,2176]{1,0:T(8,128)(2,1)}, bf16[128,2176]{1,0:T(8,128)(2,1)S(1)}, u32[]{:S(2)}, u32[]{:S(2)}) collective-permute-start(bf16[128,2176]{1,0:T(8,128)(2,1)} %pack.1.message_ref), channel_id=1, source_target_pairs={{0,2},{2,0},{1,3},{3,1},{4,6},{6,4},{5,7},{7,5},{8,10},{10,8},{9,1... | collective-permute-start | bytes 1671176 | tf_op jit(solution)/shard_map/ppermute | solution.py:338
  6.1 9.5 %collective-permute-start.2 = (bf16[128,2176]{1,0:T(8,128)(2,1)}, bf16[128,2176]{1,0:T(8,128)(2,1)}, u32[]{:S(2)}, u32[]{:S(2)}) collective-permute-start(bf16[128,2176]{1,0:T(8,128)(2,1)} %pack.1.message_ref), channel_id=1, source_target_pairs={{0,252},{2,254},{4,10},{6,8},{8,4},{10,6},{12,18},{14,16},{16,12},... | collective-permute-start | bytes 1671176 | tf_op jit(solution)/shard_map/ppermute | solution.py:327
  15.6 5.2 %home_tile.1 = (f32[128,2048]{1,0:T(8,128)S(1)}, bf16[48,2048]{1,0:T(8,128)(2,1)S(1)}) custom-call(bf16[128,2176]{1,0:T(8,128)(2,1)} %pack.1.message_ref), custom_call_target="tpu_custom_call" | custom-call | flops 67108864 | tf_op jit(solution)/shard_map/home_tile/pallas_call | solution.py:223
  21.0 4.1 %guest_tile.4.refs_2_ = f32[128,2048]{1,0:T(8,128)S(1)} custom-call(bf16[48,2048]{1,0:T(8,128)(2,1)S(1)} %get-tuple-element.53.refs_0_.home_ref, bf16[128,2176]{1,0:T(8,128)(2,1)S(1)} %collective-permute-done.refs_1_, f32[128,2048]{1,0:T(8,128)S(1)} %get-tuple-element.55.refs_2_), custom_call_target="tpu_custom_call", output_to_operand_aliasing={{}: (2, {})} | custom-call | flops 67108864 | tf_op jit(solution)/shard_map/guest_tile/pallas_call | solution.py:223
  25.5 1.8 %collective-permute-start.8 = (bf16[128,2176]{1,0:T(8,128)(2,1)}, bf16[128,2176]{1,0:T(8,128)(2,1)S(1)}, u32[]{:S(2)}, u32[]{:S(2)}) collective-permute-start(bf16[128,2176]{1,0:T(8,128)(2,1)} %collective-permute-done.1.refs_1_), channel_id=1, source_target_pairs={{0,2},{2,0},{1,3},{3,1},{4,6},{6,4},{5,7},{7,5},{8,10},{10,8},{9,1... | collective-permute-start | bytes 1671176 | tf_op jit(solution)/shard_map/ppermute | solution.py:338
  27.4 4.9 %guest_tile.5 = (f32[128,2048]{1,0:T(8,128)S(1)}, f32[128,2048]{1,0:T(8,128)S(1)}) custom-call(bf16[48,2048]{1,0:T(8,128)(2,1)S(1)} %get-tuple-element.53.refs_0_.home_ref, bf16[128,2176]{1,0:T(8,128)(2,1)} %collective-permute-done.1.refs_1_, f32[128,2048]{1,0:T(8,128)S(1)} %guest_tile.4.refs_2_), custom_call_target="tpu_custom_call", output_to_operand_aliasing={{1}: (2, {})} | custom-call | flops 67108864 | tf_op jit(solution)/shard_map/guest_tile/pallas_call | solution.py:223
  33.0 4.8 %guest_tile.6 = (f32[128,2048]{1,0:T(8,128)S(1)}, f32[128,2048]{1,0:T(8,128)S(1)}) custom-call(bf16[48,2048]{1,0:T(8,128)(2,1)S(1)} %get-tuple-element.53.refs_0_.home_ref, bf16[128,2176]{1,0:T(8,128)(2,1)} %collective-permute-done.2.refs_1_, f32[128,2048]{1,0:T(8,128)S(1)} %get-tuple-element.61.refs_2_, ...), custom_call_target="tpu_custom_call", output_to_operand_aliasing={{0}: (2, {}), {1}: (3, {})} | custom-call | flops 67108864 | tf_op jit(solution)/shard_map/guest_tile/pallas_call | solution.py:223
  37.9 4.8 %guest_tile.7 = (f32[128,2048]{1,0:T(8,128)S(1)}, f32[128,2048]{1,0:T(8,128)S(1)}) custom-call(bf16[48,2048]{1,0:T(8,128)(2,1)S(1)} %get-tuple-element.53.refs_0_.home_ref, bf16[128,2176]{1,0:T(8,128)(2,1)} %collective-permute-done.5.refs_1_, f32[128,2048]{1,0:T(8,128)S(1)} %get-tuple-element.66.refs_2_, ...), custom_call_target="tpu_custom_call", output_to_operand_aliasing={{0}: (2, {}), {1}: (3, {})} | custom-call | flops 67108864 | tf_op jit(solution)/shard_map/guest_tile/pallas_call | solution.py:223
  42.7 1.7 %half_gram.1 = (f32[128,128]{1,0:T(8,128)S(1)}, f32[128,128]{1,0:T(8,128)S(1)}, f32[128,2048]{1,0:T(8,128)S(1)}) custom-call(s32[1]{0:T(128)} %bitcast.3.core_ref, bf16[2048,128]{1,0:T(8,128)(2,1)} %own_ref.1, bf16[2048,128]{1,0:T(8,128)(2,1)} %collective-permute-done.4.pair_ref, ...), custom_call_target="tpu_custom_call", output_to_operand_aliasing={{2}: (3, {})} | custom-call | flops 67108864 | tf_op jit(solution)/shard_map/half_gram/pallas_call | solution.py:223
  44.4 5.8 %collective-permute-start.6 = (f32[128,128]{1,0:T(8,128)S(1)}, f32[128,128]{1,0:T(8,128)S(1)}, u32[]{:S(2)}, u32[]{:S(2)}) collective-permute-start(f32[128,128]{1,0:T(8,128)S(1)} %get-tuple-element.71), channel_id=1, source_target_pairs={{0,2},{2,0},{1,3},{3,1},{4,6},{6,4},{5,7},{7,5},{8,10},{10,8},{9,1... | collective-permute-start | bytes 196616 | tf_op jit(solution)/shard_map/ppermute | solution.py:338
  51.1 2.2 %collective-permute-start.7 = (f32[128,128]{1,0:T(8,128)S(1)}, f32[128,128]{1,0:T(8,128)S(1)}, u32[]{:S(2)}, u32[]{:S(2)}) collective-permute-start(f32[128,128]{1,0:T(8,128)S(1)} %add.30.value_ref), channel_id=1, source_target_pairs={{2,3},{3,2},{6,7},{7,6},{10,11},{11,10},{14,15},{15,14},{18,19},{1... | collective-permute-start | bytes 196616 | tf_op jit(solution)/shard_map/ppermute | solution.py:375
  54.6 1.5 %collective-permute-done.7.crossed_ref = f32[128,128]{1,0:T(8,128)S(1)} collective-permute-done((f32[128,128]{1,0:T(8,128)S(1)}, f32[128,128]{1,0:T(8,128)S(1)}, u32[]{:S(2)}, u32[]{:S(2)}) %collective-permute-start.7) | collective-permute-done | bytes 65568 | tf_op jit(solution)/shard_map/ppermute | solution.py:375
  56.3 1.2 %piece_tile.9.total_ref = f32[128,2048]{1,0:T(8,128)S(1)} custom-call(bf16[48,2048]{1,0:T(8,128)(2,1)S(1)} %get-tuple-element.53.refs_0_.home_ref, bf16[128,2176]{1,0:T(8,128)(2,1)S(1)} %collective-permute-done.8.message_ref, f32[128,2048]{1,0:T(8,128)S(1)} %piece_tile.8.total_ref), custom_call_target="tpu_custom_call", output_to_operand_aliasing={{}: (2, {})} | custom-call | flops 67108864 | tf_op jit(solution)/shard_map/piece_tile/pallas_call | solution.py:223
  57.6 1.2 %piece_tile.10.total_ref = f32[128,2048]{1,0:T(8,128)S(1)} custom-call(bf16[48,2048]{1,0:T(8,128)(2,1)S(1)} %get-tuple-element.53.refs_0_.home_ref, bf16[128,2176]{1,0:T(8,128)(2,1)S(1)} %collective-permute-done.8.message_ref, f32[128,2048]{1,0:T(8,128)S(1)} %piece_tile.9.total_ref), custom_call_target="tpu_custom_call", output_to_operand_aliasing={{}: (2, {})} | custom-call | flops 67108864 | tf_op jit(solution)/shard_map/piece_tile/pallas_call | solution.py:223
  58.8 4.2 %collective-permute-done.9 = bf16[128,128]{1,0:T(8,128)(2,1)S(1)} collective-permute-done((bf16[128,128]{1,0:T(8,128)(2,1)S(1)}, bf16[128,128]{1,0:T(8,128)(2,1)S(1)}, u32[]{:S(2)}, u32[]{:S(2)}) %collective-permute-start.9) | collective-permute-done | bytes 32800 | tf_op jit(solution)/shard_map/ppermute | solution.py:316
  63.2 3.4 %collective-permute-start.12 = (bf16[128,128]{1,0:T(8,128)(2,1)S(1)}, bf16[128,128]{1,0:T(8,128)(2,1)S(1)}, u32[]{:S(2)}, u32[]{:S(2)}) collective-permute-start(bf16[128,128]{1,0:T(8,128)(2,1)S(1)} %add_convert_fusion.1), channel_id=1, source_target_pairs={{0,12},{2,14},{4,8},{6,10},{8,4},{10,6},{12,0},{14,2},{16,28},{18,... | collective-permute-start | bytes 98312 | tf_op jit(solution)/shard_map/ppermute | solution.py:316
  66.6 1.2 %piece_tile.11.total_ref = f32[128,2048]{1,0:T(8,128)S(1)} custom-call(bf16[48,2048]{1,0:T(8,128)(2,1)S(1)} %get-tuple-element.53.refs_0_.home_ref, bf16[128,2176]{1,0:T(8,128)(2,1)S(1)} %collective-permute-done.8.message_ref, f32[128,2048]{1,0:T(8,128)S(1)} %piece_tile.10.total_ref), custom_call_target="tpu_custom_call", output_to_operand_aliasing={{}: (2, {})} | custom-call | flops 67108864 | tf_op jit(solution)/shard_map/piece_tile/pallas_call | solution.py:223
  69.4 3.7 %collective-permute-start.15 = (bf16[128,128]{1,0:T(8,128)(2,1)S(1)}, bf16[128,128]{1,0:T(8,128)(2,1)S(1)}, u32[]{:S(2)}, u32[]{:S(2)}) collective-permute-start(bf16[128,128]{1,0:T(8,128)(2,1)S(1)} %add_convert_fusion), channel_id=1, source_target_pairs={{0,192},{2,194},{4,196},{6,198},{8,200},{10,202},{12,204},{14,206}... | collective-permute-start | bytes 98312 | tf_op jit(solution)/shard_map/ppermute | solution.py:316
  73.1 1.2 %piece_tile.13.total_ref = f32[128,2048]{1,0:T(8,128)S(1)} custom-call(bf16[48,2048]{1,0:T(8,128)(2,1)S(1)} %get-tuple-element.53.refs_0_.home_ref, bf16[128,2176]{1,0:T(8,128)(2,1)S(1)} %collective-permute-done.3.message_ref, f32[128,2048]{1,0:T(8,128)S(1)} %piece_tile.12.total_ref), custom_call_target="tpu_custom_call", output_to_operand_aliasing={{}: (2, {})} | custom-call | flops 67108864 | tf_op jit(solution)/shard_map/piece_tile/pallas_call | solution.py:223
  74.4 1.2 %piece_tile.14.total_ref = f32[128,2048]{1,0:T(8,128)S(1)} custom-call(bf16[48,2048]{1,0:T(8,128)(2,1)S(1)} %get-tuple-element.53.refs_0_.home_ref, bf16[128,2176]{1,0:T(8,128)(2,1)S(1)} %collective-permute-done.3.message_ref, f32[128,2048]{1,0:T(8,128)S(1)} %piece_tile.13.total_ref), custom_call_target="tpu_custom_call", output_to_operand_aliasing={{}: (2, {})} | custom-call | flops 67108864 | tf_op jit(solution)/shard_map/piece_tile/pallas_call | solution.py:223
  75.7 2.2 %collective-permute-start.16 = (f32[128,128]{1,0:T(8,128)S(1)}, f32[128,128]{1,0:T(8,128)S(1)}, u32[]{:S(2)}, u32[]{:S(2)}) collective-permute-start(f32[128,128]{1,0:T(8,128)S(1)} %add_add_fusion), channel_id=1, source_target_pairs={{0,32},{2,34},{4,36},{6,38},{8,40},{10,42},{12,44},{14,46},{16,48}... | collective-permute-start | bytes 196616 | tf_op jit(solution)/shard_map/ppermute | solution.py:316
  79.2 2.4 %piece_tile.15 = f32[2048,128]{1,0:T(8,128)} custom-call(bf16[48,2048]{1,0:T(8,128)(2,1)S(1)} %get-tuple-element.53.refs_0_.home_ref, bf16[128,2176]{1,0:T(8,128)(2,1)S(1)} %collective-permute-done.3.message_ref, f32[128,2048]{1,0:T(8,128)S(1)} %piece_tile.14.total_ref), custom_call_target="tpu_custom_call" | custom-call | flops 67108864 | tf_op jit(solution)/shard_map/piece_tile/pallas_call | solution.py:223
  81.6 2.3 %collective-permute-done.18 = f32[128,128]{1,0:T(8,128)S(1)} collective-permute-done((f32[128,128]{1,0:T(8,128)S(1)}, f32[128,128]{1,0:T(8,128)S(1)}, u32[]{:S(2)}, u32[]{:S(2)}) %collective-permute-start.18) | collective-permute-done | bytes 65568 | tf_op jit(solution)/shard_map/ppermute | solution.py:316
  (37 shorter events, 7.4 us)
Async XLA Ops:
  2.8 18.2 %collective-permute-start = (bf16[128,2176]{1,0:T(8,128)(2,1)}, bf16[128,2176]{1,0:T(8,128)(2,1)S(1)}, u32[]{:S(2)}, u32[]{:S(2)}) collective-permute-start(bf16[128,2176]{1,0:T(8,128)(2,1)} %pack.1.message_ref), channel_id=1, source_target_pairs={{0,2},{2,0},{1,3},{3,1},{4,6},{6,4},{5,7},{7,5},{8,10},{10,8},{9,1... | collective-permute-start | bytes 1671176 | tf_op jit(solution)/shard_map/ppermute | solution.py:338
  6.1 19.0 %collective-permute-start.1 = (bf16[128,2176]{1,0:T(8,128)(2,1)}, bf16[128,2176]{1,0:T(8,128)(2,1)}, u32[]{:S(2)}, u32[]{:S(2)}) collective-permute-start(bf16[128,2176]{1,0:T(8,128)(2,1)} %pack.1.message_ref), channel_id=1, source_target_pairs={{0,6},{2,4},{4,0},{6,2},{8,14},{10,12},{12,8},{14,10},{16,22},{18,... | collective-permute-start | bytes 1671176 | tf_op jit(solution)/shard_map/ppermute | solution.py:327
  6.1 26.2 %collective-permute-start.2 = (bf16[128,2176]{1,0:T(8,128)(2,1)}, bf16[128,2176]{1,0:T(8,128)(2,1)}, u32[]{:S(2)}, u32[]{:S(2)}) collective-permute-start(bf16[128,2176]{1,0:T(8,128)(2,1)} %pack.1.message_ref), channel_id=1, source_target_pairs={{0,252},{2,254},{4,10},{6,8},{8,4},{10,6},{12,18},{14,16},{16,12},... | collective-permute-start | bytes 1671176 | tf_op jit(solution)/shard_map/ppermute | solution.py:327
  20.8 17.0 %collective-permute-start.5 = (bf16[128,2176]{1,0:T(8,128)(2,1)}, bf16[128,2176]{1,0:T(8,128)(2,1)}, u32[]{:S(2)}, u32[]{:S(2)}) collective-permute-start(bf16[128,2176]{1,0:T(8,128)(2,1)} %pack.1.message_ref), channel_id=1, source_target_pairs={{250,0},{8,2},{254,4},{12,6},{2,8},{16,10},{6,12},{20,14},{10,16},... | collective-permute-start | bytes 1671176 | tf_op jit(solution)/shard_map/ppermute | solution.py:332
  25.1 17.6 %collective-permute-start.4 = (bf16[2048,128]{1,0:T(8,128)(2,1)}, bf16[2048,128]{1,0:T(8,128)(2,1)}, u32[]{:S(2)}, u32[]{:S(2)}) collective-permute-start(bf16[2048,128]{1,0:T(8,128)(2,1)} %own_ref.1), channel_id=1, source_target_pairs={{0,1},{1,0},{2,3},{3,2},{4,5},{5,4},{6,7},{7,6},{8,9},{9,8},{10,11... | collective-permute-start | bytes 1572872 | tf_op jit(solution)/shard_map/ppermute | solution.py:354
  25.5 27.8 %collective-permute-start.8 = (bf16[128,2176]{1,0:T(8,128)(2,1)}, bf16[128,2176]{1,0:T(8,128)(2,1)S(1)}, u32[]{:S(2)}, u32[]{:S(2)}) collective-permute-start(bf16[128,2176]{1,0:T(8,128)(2,1)} %collective-permute-done.1.refs_1_), channel_id=1, source_target_pairs={{0,2},{2,0},{1,3},{3,1},{4,6},{6,4},{5,7},{7,5},{8,10},{10,8},{9,1... | collective-permute-start | bytes 1671176 | tf_op jit(solution)/shard_map/ppermute | solution.py:338
  32.3 35.6 %collective-permute-start.3 = (bf16[128,2176]{1,0:T(8,128)(2,1)}, bf16[128,2176]{1,0:T(8,128)(2,1)S(1)}, u32[]{:S(2)}, u32[]{:S(2)}) collective-permute-start(bf16[128,2176]{1,0:T(8,128)(2,1)} %collective-permute-done.2.refs_1_), channel_id=1, source_target_pairs={{0,2},{2,0},{1,3},{3,1},{4,6},{6,4},{5,7},{7,5},{8,10},{10,8},{9,1... | collective-permute-start | bytes 1671176 | tf_op jit(solution)/shard_map/ppermute | solution.py:338
  44.4 6.7 %collective-permute-start.6 = (f32[128,128]{1,0:T(8,128)S(1)}, f32[128,128]{1,0:T(8,128)S(1)}, u32[]{:S(2)}, u32[]{:S(2)}) collective-permute-start(f32[128,128]{1,0:T(8,128)S(1)} %get-tuple-element.71), channel_id=1, source_target_pairs={{0,2},{2,0},{1,3},{3,1},{4,6},{6,4},{5,7},{7,5},{8,10},{10,8},{9,1... | collective-permute-start | bytes 196616 | tf_op jit(solution)/shard_map/ppermute | solution.py:338
  51.1 5.0 %collective-permute-start.7 = (f32[128,128]{1,0:T(8,128)S(1)}, f32[128,128]{1,0:T(8,128)S(1)}, u32[]{:S(2)}, u32[]{:S(2)}) collective-permute-start(f32[128,128]{1,0:T(8,128)S(1)} %add.30.value_ref), channel_id=1, source_target_pairs={{2,3},{3,2},{6,7},{7,6},{10,11},{11,10},{14,15},{15,14},{18,19},{1... | collective-permute-start | bytes 196616 | tf_op jit(solution)/shard_map/ppermute | solution.py:375
  56.2 6.8 %collective-permute-start.9 = (bf16[128,128]{1,0:T(8,128)(2,1)S(1)}, bf16[128,128]{1,0:T(8,128)(2,1)S(1)}, u32[]{:S(2)}, u32[]{:S(2)}) collective-permute-start(bf16[128,128]{1,0:T(8,128)(2,1)S(1)} %convert_element_type.39), channel_id=1, source_target_pairs={{0,16},{2,18},{4,20},{6,22},{8,24},{10,26},{12,28},{14,30},{16,0},... | collective-permute-start | bytes 98312 | tf_op jit(solution)/shard_map/ppermute | solution.py:316
  63.0 6.1 %collective-permute-start.10 = (bf16[128,128]{1,0:T(8,128)(2,1)S(1)}, bf16[128,128]{1,0:T(8,128)(2,1)S(1)}, u32[]{:S(2)}, u32[]{:S(2)}) collective-permute-start(bf16[128,128]{1,0:T(8,128)(2,1)S(1)} %add_convert_fusion.1), channel_id=1, source_target_pairs={{0,4},{2,6},{4,0},{6,2},{8,12},{10,14},{12,8},{14,10},{16,20},{18,... | collective-permute-start | bytes 98312 | tf_op jit(solution)/shard_map/ppermute | solution.py:316
  63.1 6.0 %collective-permute-start.11 = (bf16[128,128]{1,0:T(8,128)(2,1)S(1)}, bf16[128,128]{1,0:T(8,128)(2,1)S(1)}, u32[]{:S(2)}, u32[]{:S(2)}) collective-permute-start(bf16[128,128]{1,0:T(8,128)(2,1)S(1)} %add_convert_fusion.1), channel_id=1, source_target_pairs={{0,8},{2,10},{4,12},{6,14},{8,0},{10,2},{12,4},{14,6},{16,24},{18,... | collective-permute-start | bytes 98312 | tf_op jit(solution)/shard_map/ppermute | solution.py:316
  63.2 6.0 %collective-permute-start.12 = (bf16[128,128]{1,0:T(8,128)(2,1)S(1)}, bf16[128,128]{1,0:T(8,128)(2,1)S(1)}, u32[]{:S(2)}, u32[]{:S(2)}) collective-permute-start(bf16[128,128]{1,0:T(8,128)(2,1)S(1)} %add_convert_fusion.1), channel_id=1, source_target_pairs={{0,12},{2,14},{4,8},{6,10},{8,4},{10,6},{12,0},{14,2},{16,28},{18,... | collective-permute-start | bytes 98312 | tf_op jit(solution)/shard_map/ppermute | solution.py:316
  69.2 6.4 %collective-permute-start.13 = (bf16[128,128]{1,0:T(8,128)(2,1)S(1)}, bf16[128,128]{1,0:T(8,128)(2,1)S(1)}, u32[]{:S(2)}, u32[]{:S(2)}) collective-permute-start(bf16[128,128]{1,0:T(8,128)(2,1)S(1)} %add_convert_fusion), channel_id=1, source_target_pairs={{0,64},{2,66},{4,68},{6,70},{8,72},{10,74},{12,76},{14,78},{16,80}... | collective-permute-start | bytes 98312 | tf_op jit(solution)/shard_map/ppermute | solution.py:316
  69.3 6.3 %collective-permute-start.14 = (bf16[128,128]{1,0:T(8,128)(2,1)S(1)}, bf16[128,128]{1,0:T(8,128)(2,1)S(1)}, u32[]{:S(2)}, u32[]{:S(2)}) collective-permute-start(bf16[128,128]{1,0:T(8,128)(2,1)S(1)} %add_convert_fusion), channel_id=1, source_target_pairs={{0,128},{2,130},{4,132},{6,134},{8,136},{10,138},{12,140},{14,142}... | collective-permute-start | bytes 98312 | tf_op jit(solution)/shard_map/ppermute | solution.py:316
  69.4 6.2 %collective-permute-start.15 = (bf16[128,128]{1,0:T(8,128)(2,1)S(1)}, bf16[128,128]{1,0:T(8,128)(2,1)S(1)}, u32[]{:S(2)}, u32[]{:S(2)}) collective-permute-start(bf16[128,128]{1,0:T(8,128)(2,1)S(1)} %add_convert_fusion), channel_id=1, source_target_pairs={{0,192},{2,194},{4,196},{6,198},{8,200},{10,202},{12,204},{14,206}... | collective-permute-start | bytes 98312 | tf_op jit(solution)/shard_map/ppermute | solution.py:316
  75.7 5.9 %collective-permute-start.16 = (f32[128,128]{1,0:T(8,128)S(1)}, f32[128,128]{1,0:T(8,128)S(1)}, u32[]{:S(2)}, u32[]{:S(2)}) collective-permute-start(f32[128,128]{1,0:T(8,128)S(1)} %add_add_fusion), channel_id=1, source_target_pairs={{0,32},{2,34},{4,36},{6,38},{8,40},{10,42},{12,44},{14,46},{16,48}... | collective-permute-start | bytes 196616 | tf_op jit(solution)/shard_map/ppermute | solution.py:316
  77.8 3.7 %collective-permute-start.17 = (f32[128,128]{1,0:T(8,128)S(1)}, f32[128,128]{1,0:T(8,128)S(1)}, u32[]{:S(2)}, u32[]{:S(2)}) collective-permute-start(f32[128,128]{1,0:T(8,128)S(1)} %add_add_fusion), channel_id=1, source_target_pairs={{0,2},{2,0},{4,6},{6,4},{8,10},{10,8},{12,14},{14,12},{16,18},{18,... | collective-permute-start | bytes 196616 | tf_op jit(solution)/shard_map/ppermute | solution.py:316
  78.7 5.2 %collective-permute-start.18 = (f32[128,128]{1,0:T(8,128)S(1)}, f32[128,128]{1,0:T(8,128)S(1)}, u32[]{:S(2)}, u32[]{:S(2)}) collective-permute-start(f32[128,128]{1,0:T(8,128)S(1)} %add_add_fusion), channel_id=1, source_target_pairs={{0,34},{2,32},{4,38},{6,36},{8,42},{10,40},{12,46},{14,44},{16,50}... | collective-permute-start | bytes 196616 | tf_op jit(solution)/shard_map/ppermute | solution.py:316

commit v8 on v7

--- a/solution.py
+++ b/solution.py
@@ -280,7 +280,7 @@
     width = count // PIECES
     out = jax.ShapeDtypeStruct((count, LANES), jnp.float32) if last else pltpu.VMEM((LANES, count), jnp.float32)
     return kernel_call(
-        functools.partial(piece_body, piece * width, last), "piece_tile", [home, message, total], "vav", [out],
+        functools.partial(piece_body, piece * width, last), "piece_tile", [home, message, total], "vhv", [out],
         fetch_scratch(width, 3 * count // LANES, 2), tile_cost(count), None if last else {2: 0},
     )[0]
 
@@ -383,9 +383,9 @@
         )
 
     stages = (
-        (((0, 0, 4, 0),), 2),
+        (((0, 0, 4, 0),), 3),
         (((0, 0, 1, 0), (0, 0, 2, 0), (0, 0, 3, 0)), 2),
-        (((1, 0, 0, 0), (2, 0, 0, 0), (3, 0, 0, 0)), 2),
+        (((1, 0, 0, 0), (2, 0, 0, 0), (3, 0, 0, 0)), 1),
     )
     for moves, pieces in stages:
         sent = value.astype(jnp.bfloat16)

time: 84.8 us -> 87.9 us (1.037)
  Pallas kernels: 38.9 us -> 42.2 us
  waiting for transfers between devices: 8.94 us -> 6.7 us
  starting transfers between devices: 35.1 us -> 37 us
    ppermute x10, starting transfers between devices: 11.1 us -> 16 us  [along_blk(): return lax.ppermute(value, BLK, pairs)]
    pallas_call x16, Pallas kernels: 38.9 us -> 42.2 us  [kernel_call(): pl.pallas_call(body, out_shape=outs, in_specs=[pl.BlockSpec(memory_space=...]
    ppermute x10, waiting for transfers between devices: 6.5 us -> 3.42 us  [along_blk(): return lax.ppermute(value, BLK, pairs)]
    ppermute x4, starting transfers between devices: 11.7 us -> 8.81 us  [core_swap(): return lax.ppermute(value, 'core', [(0, 1), (1, 0)])]
    ppermute x2, waiting for transfers between devices: 0.01 us -> 1.57 us  [from_neighbour(): return lax.ppermute(value, BLK, pairs)]
  transfers between devices with their start and end apart: 19 -> 19, of which waited for: 4 -> 6; matrix products, arithmetic and copies ran while one was open for 0% -> 0% of each run, Pallas kernels for 43% -> 47%
where the time goes in v8:
time: 87.9 us; the launch traced here: 87.6 us
  Pallas kernels  42.2 us (48%)
  starting transfers between devices  37 us (42%)
  waiting for transfers between devices  6.7 us (8%)
  between operations  0.92 us (1%)
    pallas_call x16, Pallas kernels, kernel_call(): pl.pallas_call(body, out_shape=outs, in_specs=[pl.BlockSpec(memory_space=...  42.2 us
    ppermute x10, starting transfers between devices, along_blk(): return lax.ppermute(value, BLK, pairs)  16 us
    ppermute x2, starting transfers between devices, from_neighbour(): return lax.ppermute(value, BLK, pairs)  9.49 us
    ppermute x4, starting transfers between devices, core_swap(): return lax.ppermute(value, 'core', [(0, 1), (1, 0)])  8.81 us
    ppermute x10, waiting for transfers between devices, along_blk(): return lax.ppermute(value, BLK, pairs)  3.42 us
    ppermute x1, starting transfers between devices, shards(): crossed = lax.ppermute(value, ('core', 'rhs'), [(2, 3), (3, 2)])  2.21 us
  transfers between devices with their start and end apart: 19, of which 6 were waited for; matrix products, arithmetic and copies ran while one was open for 0% of the time, Pallas kernels for 47%

profile of v8, /device:TPU:1, one launch (start us, length us, event | category | flops | bytes accessed | tf_op | source)
XLA Modules:
  0.0 87.6 jit_solution(5752176755352198974)
XLA Ops:
  2.0 3.3 %collective-permute-start = (bf16[128,2176]{1,0:T(8,128)(2,1)S(1)}, bf16[128,2176]{1,0:T(8,128)(2,1)S(1)}, u32[]{:S(2)}, u32[]{:S(2)}) collective-permute-start(bf16[128,2176]{1,0:T(8,128)(2,1)S(1)} %pack.1.message_ref), channel_id=1, source_target_pairs={{0,2},{2,0},{1,3},{3,1},{4,6},{6,4},{5,7},{7,5},{8,10},{10,8},{9,1... | collective-permute-start | bytes 1671176 | tf_op jit(solution)/shard_map/ppermute | solution.py:338
  5.3 9.5 %collective-permute-start.2 = (bf16[128,2176]{1,0:T(8,128)(2,1)S(1)}, bf16[128,2176]{1,0:T(8,128)(2,1)S(1)}, u32[]{:S(2)}, u32[]{:S(2)}) collective-permute-start(bf16[128,2176]{1,0:T(8,128)(2,1)S(1)} %pack.1.message_ref), channel_id=1, source_target_pairs={{0,252},{2,254},{4,10},{6,8},{8,4},{10,6},{12,18},{14,16},{16,12},... | collective-permute-start | bytes 1671176 | tf_op jit(solution)/shard_map/ppermute | solution.py:327
  14.8 4.1 %home_tile.1 = (f32[128,2048]{1,0:T(8,128)S(1)}, bf16[48,2048]{1,0:T(8,128)(2,1)S(1)}) custom-call(bf16[128,2176]{1,0:T(8,128)(2,1)S(1)} %pack.1.message_ref), custom_call_target="tpu_custom_call" | custom-call | flops 67108864 | tf_op jit(solution)/shard_map/home_tile/pallas_call | solution.py:223
  19.0 4.2 %guest_tile.4.refs_2_ = f32[128,2048]{1,0:T(8,128)S(1)} custom-call(bf16[48,2048]{1,0:T(8,128)(2,1)S(1)} %get-tuple-element.53.refs_0_.home_ref, bf16[128,2176]{1,0:T(8,128)(2,1)S(1)} %collective-permute-done.refs_1_, f32[128,2048]{1,0:T(8,128)S(1)} %get-tuple-element.55.refs_2_), custom_call_target="tpu_custom_call", output_to_operand_aliasing={{}: (2, {})} | custom-call | flops 67108864 | tf_op jit(solution)/shard_map/guest_tile/pallas_call | solution.py:223
  23.6 1.8 %collective-permute-start.8 = (bf16[128,2176]{1,0:T(8,128)(2,1)}, bf16[128,2176]{1,0:T(8,128)(2,1)}, u32[]{:S(2)}, u32[]{:S(2)}) collective-permute-start(bf16[128,2176]{1,0:T(8,128)(2,1)} %collective-permute-done.1.refs_1_), channel_id=1, source_target_pairs={{0,2},{2,0},{1,3},{3,1},{4,6},{6,4},{5,7},{7,5},{8,10},{10,8},{9,1... | collective-permute-start | bytes 1671176 | tf_op jit(solution)/shard_map/ppermute | solution.py:338
  25.4 4.9 %guest_tile.5 = (f32[128,2048]{1,0:T(8,128)S(1)}, f32[128,2048]{1,0:T(8,128)S(1)}) custom-call(bf16[48,2048]{1,0:T(8,128)(2,1)S(1)} %get-tuple-element.53.refs_0_.home_ref, bf16[128,2176]{1,0:T(8,128)(2,1)} %collective-permute-done.1.refs_1_, f32[128,2048]{1,0:T(8,128)S(1)} %guest_tile.4.refs_2_), custom_call_target="tpu_custom_call", output_to_operand_aliasing={{1}: (2, {})} | custom-call | flops 67108864 | tf_op jit(solution)/shard_map/guest_tile/pallas_call | solution.py:223
  31.9 1.8 %collective-permute-start.3 = (bf16[128,2176]{1,0:T(8,128)(2,1)S(1)}, bf16[128,2176]{1,0:T(8,128)(2,1)}, u32[]{:S(2)}, u32[]{:S(2)}) collective-permute-start(bf16[128,2176]{1,0:T(8,128)(2,1)S(1)} %collective-permute-done.2.refs_1_), channel_id=1, source_target_pairs={{0,2},{2,0},{1,3},{3,1},{4,6},{6,4},{5,7},{7,5},{8,10},{10,8},{9,1... | collective-permute-start | bytes 1671176 | tf_op jit(solution)/shard_map/ppermute | solution.py:338
  33.7 4.2 %guest_tile.6 = (f32[128,2048]{1,0:T(8,128)S(1)}, f32[128,2048]{1,0:T(8,128)S(1)}) custom-call(bf16[48,2048]{1,0:T(8,128)(2,1)S(1)} %get-tuple-element.53.refs_0_.home_ref, bf16[128,2176]{1,0:T(8,128)(2,1)S(1)} %collective-permute-done.2.refs_1_, f32[128,2048]{1,0:T(8,128)S(1)} %get-tuple-element.61.refs_2_, ...), custom_call_target="tpu_custom_call", output_to_operand_aliasing={{0}: (2, {}), {1}: (3, {})} | custom-call | flops 67108864 | tf_op jit(solution)/shard_map/guest_tile/pallas_call | solution.py:223
  37.9 4.8 %guest_tile.7 = (f32[128,2048]{1,0:T(8,128)S(1)}, f32[128,2048]{1,0:T(8,128)S(1)}) custom-call(bf16[48,2048]{1,0:T(8,128)(2,1)S(1)} %get-tuple-element.53.refs_0_.home_ref, bf16[128,2176]{1,0:T(8,128)(2,1)} %collective-permute-done.5.refs_1_, f32[128,2048]{1,0:T(8,128)S(1)} %get-tuple-element.66.refs_2_, ...), custom_call_target="tpu_custom_call", output_to_operand_aliasing={{0}: (2, {}), {1}: (3, {})} | custom-call | flops 67108864 | tf_op jit(solution)/shard_map/guest_tile/pallas_call | solution.py:223
  44.4 1.8 %collective-permute-start.6 = (f32[128,128]{1,0:T(8,128)S(1)}, f32[128,128]{1,0:T(8,128)S(1)}, u32[]{:S(2)}, u32[]{:S(2)}) collective-permute-start(f32[128,128]{1,0:T(8,128)S(1)} %get-tuple-element.71), channel_id=1, source_target_pairs={{0,2},{2,0},{1,3},{3,1},{4,6},{6,4},{5,7},{7,5},{8,10},{10,8},{9,1... | collective-permute-start | bytes 196616 | tf_op jit(solution)/shard_map/ppermute | solution.py:338
  47.1 2.2 %collective-permute-start.7 = (f32[128,128]{1,0:T(8,128)S(1)}, f32[128,128]{1,0:T(8,128)S(1)}, u32[]{:S(2)}, u32[]{:S(2)}) collective-permute-start(f32[128,128]{1,0:T(8,128)S(1)} %add.30.value_ref), channel_id=1, source_target_pairs={{2,3},{3,2},{6,7},{7,6},{10,11},{11,10},{14,15},{15,14},{18,19},{1... | collective-permute-start | bytes 196616 | tf_op jit(solution)/shard_map/ppermute | solution.py:375
  49.4 2.0 %piece_tile.8.total_ref = f32[128,2048]{1,0:T(8,128)S(1)} custom-call(bf16[48,2048]{1,0:T(8,128)(2,1)S(1)} %get-tuple-element.53.refs_0_.home_ref, bf16[128,2176]{1,0:T(8,128)(2,1)} %collective-permute-done.8.message_ref, f32[128,2048]{1,0:T(8,128)S(1)} %get-tuple-element.74.total_ref), custom_call_target="tpu_custom_call", output_to_operand_aliasing={{}: (2, {})} | custom-call | flops 67108864 | tf_op jit(solution)/shard_map/piece_tile/pallas_call | solution.py:223
  52.4 2.0 %piece_tile.9.total_ref = f32[128,2048]{1,0:T(8,128)S(1)} custom-call(bf16[48,2048]{1,0:T(8,128)(2,1)S(1)} %get-tuple-element.53.refs_0_.home_ref, bf16[128,2176]{1,0:T(8,128)(2,1)} %collective-permute-done.8.message_ref, f32[128,2048]{1,0:T(8,128)S(1)} %piece_tile.8.total_ref), custom_call_target="tpu_custom_call", output_to_operand_aliasing={{}: (2, {})} | custom-call | flops 67108864 | tf_op jit(solution)/shard_map/piece_tile/pallas_call | solution.py:223
  54.3 2.0 %piece_tile.10.total_ref = f32[128,2048]{1,0:T(8,128)S(1)} custom-call(bf16[48,2048]{1,0:T(8,128)(2,1)S(1)} %get-tuple-element.53.refs_0_.home_ref, bf16[128,2176]{1,0:T(8,128)(2,1)} %collective-permute-done.8.message_ref, f32[128,2048]{1,0:T(8,128)S(1)} %piece_tile.9.total_ref), custom_call_target="tpu_custom_call", output_to_operand_aliasing={{}: (2, {})} | custom-call | flops 67108864 | tf_op jit(solution)/shard_map/piece_tile/pallas_call | solution.py:223
  56.3 2.0 %piece_tile.11.total_ref = f32[128,2048]{1,0:T(8,128)S(1)} custom-call(bf16[48,2048]{1,0:T(8,128)(2,1)S(1)} %get-tuple-element.53.refs_0_.home_ref, bf16[128,2176]{1,0:T(8,128)(2,1)} %collective-permute-done.8.message_ref, f32[128,2048]{1,0:T(8,128)S(1)} %piece_tile.10.total_ref), custom_call_target="tpu_custom_call", output_to_operand_aliasing={{}: (2, {})} | custom-call | flops 67108864 | tf_op jit(solution)/shard_map/piece_tile/pallas_call | solution.py:223
  59.2 2.1 %collective-permute-start.10 = (bf16[128,128]{1,0:T(8,128)(2,1)S(1)}, bf16[128,128]{1,0:T(8,128)(2,1)S(1)}, u32[]{:S(2)}, u32[]{:S(2)}) collective-permute-start(bf16[128,128]{1,0:T(8,128)(2,1)S(1)} %add_convert_fusion.1), channel_id=1, source_target_pairs={{0,4},{2,6},{4,0},{6,2},{8,12},{10,14},{12,8},{14,10},{16,20},{18,... | collective-permute-start | bytes 98312 | tf_op jit(solution)/shard_map/ppermute | solution.py:316
  61.3 4.4 %collective-permute-start.11 = (bf16[128,128]{1,0:T(8,128)(2,1)S(1)}, bf16[128,128]{1,0:T(8,128)(2,1)S(1)}, u32[]{:S(2)}, u32[]{:S(2)}) collective-permute-start(bf16[128,128]{1,0:T(8,128)(2,1)S(1)} %add_convert_fusion.1), channel_id=1, source_target_pairs={{0,8},{2,10},{4,12},{6,14},{8,0},{10,2},{12,4},{14,6},{16,24},{18,... | collective-permute-start | bytes 98312 | tf_op jit(solution)/shard_map/ppermute | solution.py:316
  65.8 2.0 %piece_tile.12.total_ref = f32[128,2048]{1,0:T(8,128)S(1)} custom-call(bf16[48,2048]{1,0:T(8,128)(2,1)S(1)} %get-tuple-element.53.refs_0_.home_ref, bf16[128,2176]{1,0:T(8,128)(2,1)} %collective-permute-done.3.message_ref, f32[128,2048]{1,0:T(8,128)S(1)} %piece_tile.11.total_ref), custom_call_target="tpu_custom_call", output_to_operand_aliasing={{}: (2, {})} | custom-call | flops 67108864 | tf_op jit(solution)/shard_map/piece_tile/pallas_call | solution.py:223
  67.8 2.0 %piece_tile.13.total_ref = f32[128,2048]{1,0:T(8,128)S(1)} custom-call(bf16[48,2048]{1,0:T(8,128)(2,1)S(1)} %get-tuple-element.53.refs_0_.home_ref, bf16[128,2176]{1,0:T(8,128)(2,1)} %collective-permute-done.3.message_ref, f32[128,2048]{1,0:T(8,128)S(1)} %piece_tile.12.total_ref), custom_call_target="tpu_custom_call", output_to_operand_aliasing={{}: (2, {})} | custom-call | flops 67108864 | tf_op jit(solution)/shard_map/piece_tile/pallas_call | solution.py:223
  72.0 2.2 %collective-permute-start.15 = (bf16[128,128]{1,0:T(8,128)(2,1)S(1)}, bf16[128,128]{1,0:T(8,128)(2,1)S(1)}, u32[]{:S(2)}, u32[]{:S(2)}) collective-permute-start(bf16[128,128]{1,0:T(8,128)(2,1)S(1)} %add_convert_fusion), channel_id=1, source_target_pairs={{0,192},{2,194},{4,196},{6,198},{8,200},{10,202},{12,204},{14,206}... | collective-permute-start | bytes 98312 | tf_op jit(solution)/shard_map/ppermute | solution.py:316
  74.2 2.0 %piece_tile.14.total_ref = f32[128,2048]{1,0:T(8,128)S(1)} custom-call(bf16[48,2048]{1,0:T(8,128)(2,1)S(1)} %get-tuple-element.53.refs_0_.home_ref, bf16[128,2176]{1,0:T(8,128)(2,1)} %collective-permute-done.3.message_ref, f32[128,2048]{1,0:T(8,128)S(1)} %piece_tile.13.total_ref), custom_call_target="tpu_custom_call", output_to_operand_aliasing={{}: (2, {})} | custom-call | flops 67108864 | tf_op jit(solution)/shard_map/piece_tile/pallas_call | solution.py:223
  76.2 4.7 %collective-permute-start.16 = (f32[128,128]{1,0:T(8,128)S(1)}, f32[128,128]{1,0:T(8,128)S(1)}, u32[]{:S(2)}, u32[]{:S(2)}) collective-permute-start(f32[128,128]{1,0:T(8,128)S(1)} %add_add_fusion), channel_id=1, source_target_pairs={{0,32},{2,34},{4,36},{6,38},{8,40},{10,42},{12,44},{14,46},{16,48}... | collective-permute-start | bytes 196616 | tf_op jit(solution)/shard_map/ppermute | solution.py:316
  81.7 3.1 %piece_tile.15 = f32[2048,128]{1,0:T(8,128)} custom-call(bf16[48,2048]{1,0:T(8,128)(2,1)S(1)} %get-tuple-element.53.refs_0_.home_ref, bf16[128,2176]{1,0:T(8,128)(2,1)} %collective-permute-done.3.message_ref, f32[128,2048]{1,0:T(8,128)S(1)} %piece_tile.14.total_ref), custom_call_target="tpu_custom_call" | custom-call | flops 67108864 | tf_op jit(solution)/shard_map/piece_tile/pallas_call | solution.py:223
  84.8 2.1 %collective-permute-done.18 = f32[128,128]{1,0:T(8,128)S(1)} collective-permute-done((f32[128,128]{1,0:T(8,128)S(1)}, f32[128,128]{1,0:T(8,128)S(1)}, u32[]{:S(2)}, u32[]{:S(2)}) %collective-permute-start.18) | collective-permute-done | bytes 65568 | tf_op jit(solution)/shard_map/ppermute | solution.py:316
  (37 shorter events, 11.6 us)
Async XLA Ops:
  2.0 17.0 %collective-permute-start = (bf16[128,2176]{1,0:T(8,128)(2,1)S(1)}, bf16[128,2176]{1,0:T(8,128)(2,1)S(1)}, u32[]{:S(2)}, u32[]{:S(2)}) collective-permute-start(bf16[128,2176]{1,0:T(8,128)(2,1)S(1)} %pack.1.message_ref), channel_id=1, source_target_pairs={{0,2},{2,0},{1,3},{3,1},{4,6},{6,4},{5,7},{7,5},{8,10},{10,8},{9,1... | collective-permute-start | bytes 1671176 | tf_op jit(solution)/shard_map/ppermute | solution.py:338
  5.3 17.9 %collective-permute-start.1 = (bf16[128,2176]{1,0:T(8,128)(2,1)S(1)}, bf16[128,2176]{1,0:T(8,128)(2,1)}, u32[]{:S(2)}, u32[]{:S(2)}) collective-permute-start(bf16[128,2176]{1,0:T(8,128)(2,1)S(1)} %pack.1.message_ref), channel_id=1, source_target_pairs={{0,6},{2,4},{4,0},{6,2},{8,14},{10,12},{12,8},{14,10},{16,22},{18,... | collective-permute-start | bytes 1671176 | tf_op jit(solution)/shard_map/ppermute | solution.py:327
  5.3 26.6 %collective-permute-start.2 = (bf16[128,2176]{1,0:T(8,128)(2,1)S(1)}, bf16[128,2176]{1,0:T(8,128)(2,1)S(1)}, u32[]{:S(2)}, u32[]{:S(2)}) collective-permute-start(bf16[128,2176]{1,0:T(8,128)(2,1)S(1)} %pack.1.message_ref), channel_id=1, source_target_pairs={{0,252},{2,254},{4,10},{6,8},{8,4},{10,6},{12,18},{14,16},{16,12},... | collective-permute-start | bytes 1671176 | tf_op jit(solution)/shard_map/ppermute | solution.py:327
  18.9 18.9 %collective-permute-start.5 = (bf16[128,2176]{1,0:T(8,128)(2,1)S(1)}, bf16[128,2176]{1,0:T(8,128)(2,1)}, u32[]{:S(2)}, u32[]{:S(2)}) collective-permute-start(bf16[128,2176]{1,0:T(8,128)(2,1)S(1)} %pack.1.message_ref), channel_id=1, source_target_pairs={{250,0},{8,2},{254,4},{12,6},{2,8},{16,10},{6,12},{20,14},{10,16},... | collective-permute-start | bytes 1671176 | tf_op jit(solution)/shard_map/ppermute | solution.py:332
  23.2 19.5 %collective-permute-start.4 = (bf16[2048,128]{1,0:T(8,128)(2,1)}, bf16[2048,128]{1,0:T(8,128)(2,1)}, u32[]{:S(2)}, u32[]{:S(2)}) collective-permute-start(bf16[2048,128]{1,0:T(8,128)(2,1)} %own_ref.1), channel_id=1, source_target_pairs={{0,1},{1,0},{2,3},{3,2},{4,5},{5,4},{6,7},{7,6},{8,9},{9,8},{10,11... | collective-permute-start | bytes 1572872 | tf_op jit(solution)/shard_map/ppermute | solution.py:354
  23.6 25.8 %collective-permute-start.8 = (bf16[128,2176]{1,0:T(8,128)(2,1)}, bf16[128,2176]{1,0:T(8,128)(2,1)}, u32[]{:S(2)}, u32[]{:S(2)}) collective-permute-start(bf16[128,2176]{1,0:T(8,128)(2,1)} %collective-permute-done.1.refs_1_), channel_id=1, source_target_pairs={{0,2},{2,0},{1,3},{3,1},{4,6},{6,4},{5,7},{7,5},{8,10},{10,8},{9,1... | collective-permute-start | bytes 1671176 | tf_op jit(solution)/shard_map/ppermute | solution.py:338
  31.9 33.9 %collective-permute-start.3 = (bf16[128,2176]{1,0:T(8,128)(2,1)S(1)}, bf16[128,2176]{1,0:T(8,128)(2,1)}, u32[]{:S(2)}, u32[]{:S(2)}) collective-permute-start(bf16[128,2176]{1,0:T(8,128)(2,1)S(1)} %collective-permute-done.2.refs_1_), channel_id=1, source_target_pairs={{0,2},{2,0},{1,3},{3,1},{4,6},{6,4},{5,7},{7,5},{8,10},{10,8},{9,1... | collective-permute-start | bytes 1671176 | tf_op jit(solution)/shard_map/ppermute | solution.py:338
  44.4 2.7 %collective-permute-start.6 = (f32[128,128]{1,0:T(8,128)S(1)}, f32[128,128]{1,0:T(8,128)S(1)}, u32[]{:S(2)}, u32[]{:S(2)}) collective-permute-start(f32[128,128]{1,0:T(8,128)S(1)} %get-tuple-element.71), channel_id=1, source_target_pairs={{0,2},{2,0},{1,3},{3,1},{4,6},{6,4},{5,7},{7,5},{8,10},{10,8},{9,1... | collective-permute-start | bytes 196616 | tf_op jit(solution)/shard_map/ppermute | solution.py:338
  47.1 5.0 %collective-permute-start.7 = (f32[128,128]{1,0:T(8,128)S(1)}, f32[128,128]{1,0:T(8,128)S(1)}, u32[]{:S(2)}, u32[]{:S(2)}) collective-permute-start(f32[128,128]{1,0:T(8,128)S(1)} %add.30.value_ref), channel_id=1, source_target_pairs={{2,3},{3,2},{6,7},{7,6},{10,11},{11,10},{14,15},{15,14},{18,19},{1... | collective-permute-start | bytes 196616 | tf_op jit(solution)/shard_map/ppermute | solution.py:375
  52.3 7.0 %collective-permute-start.9 = (bf16[128,128]{1,0:T(8,128)(2,1)S(1)}, bf16[128,128]{1,0:T(8,128)(2,1)S(1)}, u32[]{:S(2)}, u32[]{:S(2)}) collective-permute-start(bf16[128,128]{1,0:T(8,128)(2,1)S(1)} %convert_element_type.39), channel_id=1, source_target_pairs={{0,16},{2,18},{4,20},{6,22},{8,24},{10,26},{12,28},{14,30},{16,0},... | collective-permute-start | bytes 98312 | tf_op jit(solution)/shard_map/ppermute | solution.py:316
  59.2 10.5 %collective-permute-start.10 = (bf16[128,128]{1,0:T(8,128)(2,1)S(1)}, bf16[128,128]{1,0:T(8,128)(2,1)S(1)}, u32[]{:S(2)}, u32[]{:S(2)}) collective-permute-start(bf16[128,128]{1,0:T(8,128)(2,1)S(1)} %add_convert_fusion.1), channel_id=1, source_target_pairs={{0,4},{2,6},{4,0},{6,2},{8,12},{10,14},{12,8},{14,10},{16,20},{18,... | collective-permute-start | bytes 98312 | tf_op jit(solution)/shard_map/ppermute | solution.py:316
  61.3 8.5 %collective-permute-start.11 = (bf16[128,128]{1,0:T(8,128)(2,1)S(1)}, bf16[128,128]{1,0:T(8,128)(2,1)S(1)}, u32[]{:S(2)}, u32[]{:S(2)}) collective-permute-start(bf16[128,128]{1,0:T(8,128)(2,1)S(1)} %add_convert_fusion.1), channel_id=1, source_target_pairs={{0,8},{2,10},{4,12},{6,14},{8,0},{10,2},{12,4},{14,6},{16,24},{18,... | collective-permute-start | bytes 98312 | tf_op jit(solution)/shard_map/ppermute | solution.py:316
  65.7 4.6 %collective-permute-start.12 = (bf16[128,128]{1,0:T(8,128)(2,1)S(1)}, bf16[128,128]{1,0:T(8,128)(2,1)S(1)}, u32[]{:S(2)}, u32[]{:S(2)}) collective-permute-start(bf16[128,128]{1,0:T(8,128)(2,1)S(1)} %add_convert_fusion.1), channel_id=1, source_target_pairs={{0,12},{2,14},{4,8},{6,10},{8,4},{10,6},{12,0},{14,2},{16,28},{18,... | collective-permute-start | bytes 98312 | tf_op jit(solution)/shard_map/ppermute | solution.py:316
  70.3 5.9 %collective-permute-start.13 = (bf16[128,128]{1,0:T(8,128)(2,1)S(1)}, bf16[128,128]{1,0:T(8,128)(2,1)S(1)}, u32[]{:S(2)}, u32[]{:S(2)}) collective-permute-start(bf16[128,128]{1,0:T(8,128)(2,1)S(1)} %add_convert_fusion), channel_id=1, source_target_pairs={{0,64},{2,66},{4,68},{6,70},{8,72},{10,74},{12,76},{14,78},{16,80}... | collective-permute-start | bytes 98312 | tf_op jit(solution)/shard_map/ppermute | solution.py:316
  70.4 5.8 %collective-permute-start.14 = (bf16[128,128]{1,0:T(8,128)(2,1)S(1)}, bf16[128,128]{1,0:T(8,128)(2,1)S(1)}, u32[]{:S(2)}, u32[]{:S(2)}) collective-permute-start(bf16[128,128]{1,0:T(8,128)(2,1)S(1)} %add_convert_fusion), channel_id=1, source_target_pairs={{0,128},{2,130},{4,132},{6,134},{8,136},{10,138},{12,140},{14,142}... | collective-permute-start | bytes 98312 | tf_op jit(solution)/shard_map/ppermute | solution.py:316
  72.0 4.2 %collective-permute-start.15 = (bf16[128,128]{1,0:T(8,128)(2,1)S(1)}, bf16[128,128]{1,0:T(8,128)(2,1)S(1)}, u32[]{:S(2)}, u32[]{:S(2)}) collective-permute-start(bf16[128,128]{1,0:T(8,128)(2,1)S(1)} %add_convert_fusion), channel_id=1, source_target_pairs={{0,192},{2,194},{4,196},{6,198},{8,200},{10,202},{12,204},{14,206}... | collective-permute-start | bytes 98312 | tf_op jit(solution)/shard_map/ppermute | solution.py:316
  76.2 8.6 %collective-permute-start.16 = (f32[128,128]{1,0:T(8,128)S(1)}, f32[128,128]{1,0:T(8,128)S(1)}, u32[]{:S(2)}, u32[]{:S(2)}) collective-permute-start(f32[128,128]{1,0:T(8,128)S(1)} %add_add_fusion), channel_id=1, source_target_pairs={{0,32},{2,34},{4,36},{6,38},{8,40},{10,42},{12,44},{14,46},{16,48}... | collective-permute-start | bytes 196616 | tf_op jit(solution)/shard_map/ppermute | solution.py:316
  80.9 3.9 %collective-permute-start.17 = (f32[128,128]{1,0:T(8,128)S(1)}, f32[128,128]{1,0:T(8,128)S(1)}, u32[]{:S(2)}, u32[]{:S(2)}) collective-permute-start(f32[128,128]{1,0:T(8,128)S(1)} %add_add_fusion), channel_id=1, source_target_pairs={{0,2},{2,0},{4,6},{6,4},{8,10},{10,8},{12,14},{14,12},{16,18},{18,... | collective-permute-start | bytes 196616 | tf_op jit(solution)/shard_map/ppermute | solution.py:316
  81.7 5.2 %collective-permute-start.18 = (f32[128,128]{1,0:T(8,128)S(1)}, f32[128,128]{1,0:T(8,128)S(1)}, u32[]{:S(2)}, u32[]{:S(2)}) collective-permute-start(f32[128,128]{1,0:T(8,128)S(1)} %add_add_fusion), channel_id=1, source_target_pairs={{0,34},{2,32},{4,38},{6,36},{8,42},{10,40},{12,46},{14,44},{16,50}... | collective-permute-start | bytes 196616 | tf_op jit(solution)/shard_map/ppermute | solution.py:316

commit v9 on v8

--- a/solution.py
+++ b/solution.py
@@ -280,7 +280,7 @@
     width = count // PIECES
     out = jax.ShapeDtypeStruct((count, LANES), jnp.float32) if last else pltpu.VMEM((LANES, count), jnp.float32)
     return kernel_call(
-        functools.partial(piece_body, piece * width, last), "piece_tile", [home, message, total], "vhv", [out],
+        functools.partial(piece_body, piece * width, last), "piece_tile", [home, message, total], "vav", [out],
         fetch_scratch(width, 3 * count // LANES, 2), tile_cost(count), None if last else {2: 0},
     )[0]
 

time: 87.9 us -> 86.1 us (0.980)
  Pallas kernels: 42.2 us -> 38.8 us
  waiting for transfers between devices: 6.7 us -> 8.79 us
    ppermute x10, starting transfers between devices: 16 us -> 12.6 us  [along_blk(): return lax.ppermute(value, BLK, pairs)]
    pallas_call x16, Pallas kernels: 42.2 us -> 38.8 us  [kernel_call(): pl.pallas_call(body, out_shape=outs, in_specs=[pl.BlockSpec(memory_space=...]
    ppermute x10, waiting for transfers between devices: 3.42 us -> 6.35 us  [along_blk(): return lax.ppermute(value, BLK, pairs)]
    ppermute x4, starting transfers between devices: 8.81 us -> 11.7 us  [core_swap(): return lax.ppermute(value, 'core', [(0, 1), (1, 0)])]
    ppermute x2, waiting for transfers between devices: 1.57 us -> 0.01 us  [from_neighbour(): return lax.ppermute(value, BLK, pairs)]
  transfers between devices with their start and end apart: 19 -> 19, of which waited for: 6 -> 5; matrix products, arithmetic and copies ran while one was open for 0% -> 0% of each run, Pallas kernels for 47% -> 43%
where the time goes in v9:
time: 86.1 us; the launch traced here: 85.8 us
  Pallas kernels  38.8 us (45%)
  starting transfers between devices  36.5 us (42%)
  waiting for transfers between devices  8.79 us (10%)
  between operations  0.94 us (1%)
    pallas_call x16, Pallas kernels, kernel_call(): pl.pallas_call(body, out_shape=outs, in_specs=[pl.BlockSpec(memory_space=...  38.8 us
    ppermute x10, starting transfers between devices, along_blk(): return lax.ppermute(value, BLK, pairs)  12.6 us
    ppermute x4, starting transfers between devices, core_swap(): return lax.ppermute(value, 'core', [(0, 1), (1, 0)])  11.7 us
    ppermute x2, starting transfers between devices, from_neighbour(): return lax.ppermute(value, BLK, pairs)  9.49 us
    ppermute x10, waiting for transfers between devices, along_blk(): return lax.ppermute(value, BLK, pairs)  6.35 us
    ppermute x1, starting transfers between devices, shards(): crossed = lax.ppermute(value, ('core', 'rhs'), [(2, 3), (3, 2)])  2.23 us
  transfers between devices with their start and end apart: 19, of which 5 were waited for; matrix products, arithmetic and copies ran while one was open for 0% of the time, Pallas kernels for 43%

profile of v9, /device:TPU:1, one launch (start us, length us, event | category | flops | bytes accessed | tf_op | source)
XLA Modules:
  0.0 85.8 jit_solution(9861173497345337655)
XLA Ops:
  0.6 2.1 %pack.1.message_ref = bf16[128,2176]{1,0:T(8,128)(2,1)} custom-call(bf16[2048,128]{1,0:T(8,128)(2,1)} %own_ref.1, bf16[16,128]{1,0:T(8,128)(2,1)} %bitcast.4, bf16[16,128]{1,0:T(8,128)(2,1)} %bitcast.5, bf16[16,128]{1,0:T(8,128)(2,1)} %bitcast.6), custom_call_target="tpu_custom_call" | custom-call | bytes 1048576 | tf_op jit(solution)/shard_map/pack/pallas_call | solution.py:223
  2.8 3.3 %collective-permute-start = (bf16[128,2176]{1,0:T(8,128)(2,1)}, bf16[128,2176]{1,0:T(8,128)(2,1)S(1)}, u32[]{:S(2)}, u32[]{:S(2)}) collective-permute-start(bf16[128,2176]{1,0:T(8,128)(2,1)} %pack.1.message_ref), channel_id=1, source_target_pairs={{0,2},{2,0},{1,3},{3,1},{4,6},{6,4},{5,7},{7,5},{8,10},{10,8},{9,1... | collective-permute-start | bytes 1671176 | tf_op jit(solution)/shard_map/ppermute | solution.py:338
  6.1 9.5 %collective-permute-start.2 = (bf16[128,2176]{1,0:T(8,128)(2,1)}, bf16[128,2176]{1,0:T(8,128)(2,1)}, u32[]{:S(2)}, u32[]{:S(2)}) collective-permute-start(bf16[128,2176]{1,0:T(8,128)(2,1)} %pack.1.message_ref), channel_id=1, source_target_pairs={{0,252},{2,254},{4,10},{6,8},{8,4},{10,6},{12,18},{14,16},{16,12},... | collective-permute-start | bytes 1671176 | tf_op jit(solution)/shard_map/ppermute | solution.py:327
  15.6 5.2 %home_tile.1 = (f32[128,2048]{1,0:T(8,128)S(1)}, bf16[48,2048]{1,0:T(8,128)(2,1)S(1)}) custom-call(bf16[128,2176]{1,0:T(8,128)(2,1)} %pack.1.message_ref), custom_call_target="tpu_custom_call" | custom-call | flops 67108864 | tf_op jit(solution)/shard_map/home_tile/pallas_call | solution.py:223
  21.0 4.1 %guest_tile.4.refs_2_ = f32[128,2048]{1,0:T(8,128)S(1)} custom-call(bf16[48,2048]{1,0:T(8,128)(2,1)S(1)} %get-tuple-element.53.refs_0_.home_ref, bf16[128,2176]{1,0:T(8,128)(2,1)S(1)} %collective-permute-done.refs_1_, f32[128,2048]{1,0:T(8,128)S(1)} %get-tuple-element.55.refs_2_), custom_call_target="tpu_custom_call", output_to_operand_aliasing={{}: (2, {})} | custom-call | flops 67108864 | tf_op jit(solution)/shard_map/guest_tile/pallas_call | solution.py:223
  25.5 1.8 %collective-permute-start.8 = (bf16[128,2176]{1,0:T(8,128)(2,1)}, bf16[128,2176]{1,0:T(8,128)(2,1)S(1)}, u32[]{:S(2)}, u32[]{:S(2)}) collective-permute-start(bf16[128,2176]{1,0:T(8,128)(2,1)} %collective-permute-done.1.refs_1_), channel_id=1, source_target_pairs={{0,2},{2,0},{1,3},{3,1},{4,6},{6,4},{5,7},{7,5},{8,10},{10,8},{9,1... | collective-permute-start | bytes 1671176 | tf_op jit(solution)/shard_map/ppermute | solution.py:338
  27.4 4.9 %guest_tile.5 = (f32[128,2048]{1,0:T(8,128)S(1)}, f32[128,2048]{1,0:T(8,128)S(1)}) custom-call(bf16[48,2048]{1,0:T(8,128)(2,1)S(1)} %get-tuple-element.53.refs_0_.home_ref, bf16[128,2176]{1,0:T(8,128)(2,1)} %collective-permute-done.1.refs_1_, f32[128,2048]{1,0:T(8,128)S(1)} %guest_tile.4.refs_2_), custom_call_target="tpu_custom_call", output_to_operand_aliasing={{1}: (2, {})} | custom-call | flops 67108864 | tf_op jit(solution)/shard_map/guest_tile/pallas_call | solution.py:223
  33.0 4.8 %guest_tile.6 = (f32[128,2048]{1,0:T(8,128)S(1)}, f32[128,2048]{1,0:T(8,128)S(1)}) custom-call(bf16[48,2048]{1,0:T(8,128)(2,1)S(1)} %get-tuple-element.53.refs_0_.home_ref, bf16[128,2176]{1,0:T(8,128)(2,1)} %collective-permute-done.2.refs_1_, f32[128,2048]{1,0:T(8,128)S(1)} %get-tuple-element.61.refs_2_, ...), custom_call_target="tpu_custom_call", output_to_operand_aliasing={{0}: (2, {}), {1}: (3, {})} | custom-call | flops 67108864 | tf_op jit(solution)/shard_map/guest_tile/pallas_call | solution.py:223
  37.9 4.8 %guest_tile.7 = (f32[128,2048]{1,0:T(8,128)S(1)}, f32[128,2048]{1,0:T(8,128)S(1)}) custom-call(bf16[48,2048]{1,0:T(8,128)(2,1)S(1)} %get-tuple-element.53.refs_0_.home_ref, bf16[128,2176]{1,0:T(8,128)(2,1)} %collective-permute-done.5.refs_1_, f32[128,2048]{1,0:T(8,128)S(1)} %get-tuple-element.66.refs_2_, ...), custom_call_target="tpu_custom_call", output_to_operand_aliasing={{0}: (2, {}), {1}: (3, {})} | custom-call | flops 67108864 | tf_op jit(solution)/shard_map/guest_tile/pallas_call | solution.py:223
  42.7 1.7 %half_gram.1 = (f32[128,128]{1,0:T(8,128)S(1)}, f32[128,128]{1,0:T(8,128)S(1)}, f32[128,2048]{1,0:T(8,128)S(1)}) custom-call(s32[1]{0:T(128)} %bitcast.3.core_ref, bf16[2048,128]{1,0:T(8,128)(2,1)} %own_ref.1, bf16[2048,128]{1,0:T(8,128)(2,1)} %collective-permute-done.4.pair_ref, ...), custom_call_target="tpu_custom_call", output_to_operand_aliasing={{2}: (3, {})} | custom-call | flops 67108864 | tf_op jit(solution)/shard_map/half_gram/pallas_call | solution.py:223
  44.4 5.8 %collective-permute-start.6 = (f32[128,128]{1,0:T(8,128)S(1)}, f32[128,128]{1,0:T(8,128)S(1)}, u32[]{:S(2)}, u32[]{:S(2)}) collective-permute-start(f32[128,128]{1,0:T(8,128)S(1)} %get-tuple-element.71), channel_id=1, source_target_pairs={{0,2},{2,0},{1,3},{3,1},{4,6},{6,4},{5,7},{7,5},{8,10},{10,8},{9,1... | collective-permute-start | bytes 196616 | tf_op jit(solution)/shard_map/ppermute | solution.py:338
  51.1 2.2 %collective-permute-start.7 = (f32[128,128]{1,0:T(8,128)S(1)}, f32[128,128]{1,0:T(8,128)S(1)}, u32[]{:S(2)}, u32[]{:S(2)}) collective-permute-start(f32[128,128]{1,0:T(8,128)S(1)} %add.30.value_ref), channel_id=1, source_target_pairs={{2,3},{3,2},{6,7},{7,6},{10,11},{11,10},{14,15},{15,14},{18,19},{1... | collective-permute-start | bytes 196616 | tf_op jit(solution)/shard_map/ppermute | solution.py:375
  54.6 1.5 %collective-permute-done.7.crossed_ref = f32[128,128]{1,0:T(8,128)S(1)} collective-permute-done((f32[128,128]{1,0:T(8,128)S(1)}, f32[128,128]{1,0:T(8,128)S(1)}, u32[]{:S(2)}, u32[]{:S(2)}) %collective-permute-start.7) | collective-permute-done | bytes 65568 | tf_op jit(solution)/shard_map/ppermute | solution.py:375
  56.3 1.2 %piece_tile.9.total_ref = f32[128,2048]{1,0:T(8,128)S(1)} custom-call(bf16[48,2048]{1,0:T(8,128)(2,1)S(1)} %get-tuple-element.53.refs_0_.home_ref, bf16[128,2176]{1,0:T(8,128)(2,1)S(1)} %collective-permute-done.8.message_ref, f32[128,2048]{1,0:T(8,128)S(1)} %piece_tile.8.total_ref), custom_call_target="tpu_custom_call", output_to_operand_aliasing={{}: (2, {})} | custom-call | flops 67108864 | tf_op jit(solution)/shard_map/piece_tile/pallas_call | solution.py:223
  57.6 1.2 %piece_tile.10.total_ref = f32[128,2048]{1,0:T(8,128)S(1)} custom-call(bf16[48,2048]{1,0:T(8,128)(2,1)S(1)} %get-tuple-element.53.refs_0_.home_ref, bf16[128,2176]{1,0:T(8,128)(2,1)S(1)} %collective-permute-done.8.message_ref, f32[128,2048]{1,0:T(8,128)S(1)} %piece_tile.9.total_ref), custom_call_target="tpu_custom_call", output_to_operand_aliasing={{}: (2, {})} | custom-call | flops 67108864 | tf_op jit(solution)/shard_map/piece_tile/pallas_call | solution.py:223
  60.0 2.9 %collective-permute-done.9 = bf16[128,128]{1,0:T(8,128)(2,1)S(1)} collective-permute-done((bf16[128,128]{1,0:T(8,128)(2,1)S(1)}, bf16[128,128]{1,0:T(8,128)(2,1)S(1)}, u32[]{:S(2)}, u32[]{:S(2)}) %collective-permute-start.9) | collective-permute-done | bytes 32800 | tf_op jit(solution)/shard_map/ppermute | solution.py:316
  63.1 1.3 %collective-permute-start.11 = (bf16[128,128]{1,0:T(8,128)(2,1)S(1)}, bf16[128,128]{1,0:T(8,128)(2,1)S(1)}, u32[]{:S(2)}, u32[]{:S(2)}) collective-permute-start(bf16[128,128]{1,0:T(8,128)(2,1)S(1)} %add_convert_fusion.1), channel_id=1, source_target_pairs={{0,8},{2,10},{4,12},{6,14},{8,0},{10,2},{12,4},{14,6},{16,24},{18,... | collective-permute-start | bytes 98312 | tf_op jit(solution)/shard_map/ppermute | solution.py:316
  64.4 2.3 %collective-permute-start.12 = (bf16[128,128]{1,0:T(8,128)(2,1)S(1)}, bf16[128,128]{1,0:T(8,128)(2,1)S(1)}, u32[]{:S(2)}, u32[]{:S(2)}) collective-permute-start(bf16[128,128]{1,0:T(8,128)(2,1)S(1)} %add_convert_fusion.1), channel_id=1, source_target_pairs={{0,12},{2,14},{4,8},{6,10},{8,4},{10,6},{12,0},{14,2},{16,28},{18,... | collective-permute-start | bytes 98312 | tf_op jit(solution)/shard_map/ppermute | solution.py:316
  69.3 1.4 %collective-permute-start.14 = (bf16[128,128]{1,0:T(8,128)(2,1)S(1)}, bf16[128,128]{1,0:T(8,128)(2,1)S(1)}, u32[]{:S(2)}, u32[]{:S(2)}) collective-permute-start(bf16[128,128]{1,0:T(8,128)(2,1)S(1)} %add_convert_fusion), channel_id=1, source_target_pairs={{0,128},{2,130},{4,132},{6,134},{8,136},{10,138},{12,140},{14,142}... | collective-permute-start | bytes 98312 | tf_op jit(solution)/shard_map/ppermute | solution.py:316
  70.7 2.4 %collective-permute-start.15 = (bf16[128,128]{1,0:T(8,128)(2,1)S(1)}, bf16[128,128]{1,0:T(8,128)(2,1)S(1)}, u32[]{:S(2)}, u32[]{:S(2)}) collective-permute-start(bf16[128,128]{1,0:T(8,128)(2,1)S(1)} %add_convert_fusion), channel_id=1, source_target_pairs={{0,192},{2,194},{4,196},{6,198},{8,200},{10,202},{12,204},{14,206}... | collective-permute-start | bytes 98312 | tf_op jit(solution)/shard_map/ppermute | solution.py:316
  73.1 1.2 %piece_tile.14.total_ref = f32[128,2048]{1,0:T(8,128)S(1)} custom-call(bf16[48,2048]{1,0:T(8,128)(2,1)S(1)} %get-tuple-element.53.refs_0_.home_ref, bf16[128,2176]{1,0:T(8,128)(2,1)S(1)} %collective-permute-done.3.message_ref, f32[128,2048]{1,0:T(8,128)S(1)} %piece_tile.13.total_ref), custom_call_target="tpu_custom_call", output_to_operand_aliasing={{}: (2, {})} | custom-call | flops 67108864 | tf_op jit(solution)/shard_map/piece_tile/pallas_call | solution.py:223
  75.0 4.1 %collective-permute-start.16 = (f32[128,128]{1,0:T(8,128)S(1)}, f32[128,128]{1,0:T(8,128)S(1)}, u32[]{:S(2)}, u32[]{:S(2)}) collective-permute-start(f32[128,128]{1,0:T(8,128)S(1)} %add_add_fusion), channel_id=1, source_target_pairs={{0,32},{2,34},{4,36},{6,38},{8,40},{10,42},{12,44},{14,46},{16,48}... | collective-permute-start | bytes 196616 | tf_op jit(solution)/shard_map/ppermute | solution.py:316
  79.9 2.4 %piece_tile.15 = f32[2048,128]{1,0:T(8,128)} custom-call(bf16[48,2048]{1,0:T(8,128)(2,1)S(1)} %get-tuple-element.53.refs_0_.home_ref, bf16[128,2176]{1,0:T(8,128)(2,1)S(1)} %collective-permute-done.3.message_ref, f32[128,2048]{1,0:T(8,128)S(1)} %piece_tile.14.total_ref), custom_call_target="tpu_custom_call" | custom-call | flops 67108864 | tf_op jit(solution)/shard_map/piece_tile/pallas_call | solution.py:223
  82.3 2.8 %collective-permute-done.18 = f32[128,128]{1,0:T(8,128)S(1)} collective-permute-done((f32[128,128]{1,0:T(8,128)S(1)}, f32[128,128]{1,0:T(8,128)S(1)}, u32[]{:S(2)}, u32[]{:S(2)}) %collective-permute-start.18) | collective-permute-done | bytes 65568 | tf_op jit(solution)/shard_map/ppermute | solution.py:316
  (37 shorter events, 9.7 us)
Async XLA Ops:
  2.8 18.2 %collective-permute-start = (bf16[128,2176]{1,0:T(8,128)(2,1)}, bf16[128,2176]{1,0:T(8,128)(2,1)S(1)}, u32[]{:S(2)}, u32[]{:S(2)}) collective-permute-start(bf16[128,2176]{1,0:T(8,128)(2,1)} %pack.1.message_ref), channel_id=1, source_target_pairs={{0,2},{2,0},{1,3},{3,1},{4,6},{6,4},{5,7},{7,5},{8,10},{10,8},{9,1... | collective-permute-start | bytes 1671176 | tf_op jit(solution)/shard_map/ppermute | solution.py:338
  6.1 19.0 %collective-permute-start.1 = (bf16[128,2176]{1,0:T(8,128)(2,1)}, bf16[128,2176]{1,0:T(8,128)(2,1)}, u32[]{:S(2)}, u32[]{:S(2)}) collective-permute-start(bf16[128,2176]{1,0:T(8,128)(2,1)} %pack.1.message_ref), channel_id=1, source_target_pairs={{0,6},{2,4},{4,0},{6,2},{8,14},{10,12},{12,8},{14,10},{16,22},{18,... | collective-permute-start | bytes 1671176 | tf_op jit(solution)/shard_map/ppermute | solution.py:327
  6.1 26.2 %collective-permute-start.2 = (bf16[128,2176]{1,0:T(8,128)(2,1)}, bf16[128,2176]{1,0:T(8,128)(2,1)}, u32[]{:S(2)}, u32[]{:S(2)}) collective-permute-start(bf16[128,2176]{1,0:T(8,128)(2,1)} %pack.1.message_ref), channel_id=1, source_target_pairs={{0,252},{2,254},{4,10},{6,8},{8,4},{10,6},{12,18},{14,16},{16,12},... | collective-permute-start | bytes 1671176 | tf_op jit(solution)/shard_map/ppermute | solution.py:327
  20.8 17.0 %collective-permute-start.5 = (bf16[128,2176]{1,0:T(8,128)(2,1)}, bf16[128,2176]{1,0:T(8,128)(2,1)}, u32[]{:S(2)}, u32[]{:S(2)}) collective-permute-start(bf16[128,2176]{1,0:T(8,128)(2,1)} %pack.1.message_ref), channel_id=1, source_target_pairs={{250,0},{8,2},{254,4},{12,6},{2,8},{16,10},{6,12},{20,14},{10,16},... | collective-permute-start | bytes 1671176 | tf_op jit(solution)/shard_map/ppermute | solution.py:332
  25.1 17.6 %collective-permute-start.4 = (bf16[2048,128]{1,0:T(8,128)(2,1)}, bf16[2048,128]{1,0:T(8,128)(2,1)}, u32[]{:S(2)}, u32[]{:S(2)}) collective-permute-start(bf16[2048,128]{1,0:T(8,128)(2,1)} %own_ref.1), channel_id=1, source_target_pairs={{0,1},{1,0},{2,3},{3,2},{4,5},{5,4},{6,7},{7,6},{8,9},{9,8},{10,11... | collective-permute-start | bytes 1572872 | tf_op jit(solution)/shard_map/ppermute | solution.py:354
  25.5 27.8 %collective-permute-start.8 = (bf16[128,2176]{1,0:T(8,128)(2,1)}, bf16[128,2176]{1,0:T(8,128)(2,1)S(1)}, u32[]{:S(2)}, u32[]{:S(2)}) collective-permute-start(bf16[128,2176]{1,0:T(8,128)(2,1)} %collective-permute-done.1.refs_1_), channel_id=1, source_target_pairs={{0,2},{2,0},{1,3},{3,1},{4,6},{6,4},{5,7},{7,5},{8,10},{10,8},{9,1... | collective-permute-start | bytes 1671176 | tf_op jit(solution)/shard_map/ppermute | solution.py:338
  32.3 34.3 %collective-permute-start.3 = (bf16[128,2176]{1,0:T(8,128)(2,1)}, bf16[128,2176]{1,0:T(8,128)(2,1)S(1)}, u32[]{:S(2)}, u32[]{:S(2)}) collective-permute-start(bf16[128,2176]{1,0:T(8,128)(2,1)} %collective-permute-done.2.refs_1_), channel_id=1, source_target_pairs={{0,2},{2,0},{1,3},{3,1},{4,6},{6,4},{5,7},{7,5},{8,10},{10,8},{9,1... | collective-permute-start | bytes 1671176 | tf_op jit(solution)/shard_map/ppermute | solution.py:338
  44.4 6.7 %collective-permute-start.6 = (f32[128,128]{1,0:T(8,128)S(1)}, f32[128,128]{1,0:T(8,128)S(1)}, u32[]{:S(2)}, u32[]{:S(2)}) collective-permute-start(f32[128,128]{1,0:T(8,128)S(1)} %get-tuple-element.71), channel_id=1, source_target_pairs={{0,2},{2,0},{1,3},{3,1},{4,6},{6,4},{5,7},{7,5},{8,10},{10,8},{9,1... | collective-permute-start | bytes 196616 | tf_op jit(solution)/shard_map/ppermute | solution.py:338
  51.1 5.0 %collective-permute-start.7 = (f32[128,128]{1,0:T(8,128)S(1)}, f32[128,128]{1,0:T(8,128)S(1)}, u32[]{:S(2)}, u32[]{:S(2)}) collective-permute-start(f32[128,128]{1,0:T(8,128)S(1)} %add.30.value_ref), channel_id=1, source_target_pairs={{2,3},{3,2},{6,7},{7,6},{10,11},{11,10},{14,15},{15,14},{18,19},{1... | collective-permute-start | bytes 196616 | tf_op jit(solution)/shard_map/ppermute | solution.py:375
  56.2 6.8 %collective-permute-start.9 = (bf16[128,128]{1,0:T(8,128)(2,1)S(1)}, bf16[128,128]{1,0:T(8,128)(2,1)S(1)}, u32[]{:S(2)}, u32[]{:S(2)}) collective-permute-start(bf16[128,128]{1,0:T(8,128)(2,1)S(1)} %convert_element_type.39), channel_id=1, source_target_pairs={{0,16},{2,18},{4,20},{6,22},{8,24},{10,26},{12,28},{14,30},{16,0},... | collective-permute-start | bytes 98312 | tf_op jit(solution)/shard_map/ppermute | solution.py:316
  63.0 6.1 %collective-permute-start.10 = (bf16[128,128]{1,0:T(8,128)(2,1)S(1)}, bf16[128,128]{1,0:T(8,128)(2,1)S(1)}, u32[]{:S(2)}, u32[]{:S(2)}) collective-permute-start(bf16[128,128]{1,0:T(8,128)(2,1)S(1)} %add_convert_fusion.1), channel_id=1, source_target_pairs={{0,4},{2,6},{4,0},{6,2},{8,12},{10,14},{12,8},{14,10},{16,20},{18,... | collective-permute-start | bytes 98312 | tf_op jit(solution)/shard_map/ppermute | solution.py:316
  63.1 6.0 %collective-permute-start.11 = (bf16[128,128]{1,0:T(8,128)(2,1)S(1)}, bf16[128,128]{1,0:T(8,128)(2,1)S(1)}, u32[]{:S(2)}, u32[]{:S(2)}) collective-permute-start(bf16[128,128]{1,0:T(8,128)(2,1)S(1)} %add_convert_fusion.1), channel_id=1, source_target_pairs={{0,8},{2,10},{4,12},{6,14},{8,0},{10,2},{12,4},{14,6},{16,24},{18,... | collective-permute-start | bytes 98312 | tf_op jit(solution)/shard_map/ppermute | solution.py:316
  64.4 4.8 %collective-permute-start.12 = (bf16[128,128]{1,0:T(8,128)(2,1)S(1)}, bf16[128,128]{1,0:T(8,128)(2,1)S(1)}, u32[]{:S(2)}, u32[]{:S(2)}) collective-permute-start(bf16[128,128]{1,0:T(8,128)(2,1)S(1)} %add_convert_fusion.1), channel_id=1, source_target_pairs={{0,12},{2,14},{4,8},{6,10},{8,4},{10,6},{12,0},{14,2},{16,28},{18,... | collective-permute-start | bytes 98312 | tf_op jit(solution)/shard_map/ppermute | solution.py:316
  69.2 5.2 %collective-permute-start.13 = (bf16[128,128]{1,0:T(8,128)(2,1)S(1)}, bf16[128,128]{1,0:T(8,128)(2,1)S(1)}, u32[]{:S(2)}, u32[]{:S(2)}) collective-permute-start(bf16[128,128]{1,0:T(8,128)(2,1)S(1)} %add_convert_fusion), channel_id=1, source_target_pairs={{0,64},{2,66},{4,68},{6,70},{8,72},{10,74},{12,76},{14,78},{16,80}... | collective-permute-start | bytes 98312 | tf_op jit(solution)/shard_map/ppermute | solution.py:316
  69.3 5.1 %collective-permute-start.14 = (bf16[128,128]{1,0:T(8,128)(2,1)S(1)}, bf16[128,128]{1,0:T(8,128)(2,1)S(1)}, u32[]{:S(2)}, u32[]{:S(2)}) collective-permute-start(bf16[128,128]{1,0:T(8,128)(2,1)S(1)} %add_convert_fusion), channel_id=1, source_target_pairs={{0,128},{2,130},{4,132},{6,134},{8,136},{10,138},{12,140},{14,142}... | collective-permute-start | bytes 98312 | tf_op jit(solution)/shard_map/ppermute | solution.py:316
  70.7 4.3 %collective-permute-start.15 = (bf16[128,128]{1,0:T(8,128)(2,1)S(1)}, bf16[128,128]{1,0:T(8,128)(2,1)S(1)}, u32[]{:S(2)}, u32[]{:S(2)}) collective-permute-start(bf16[128,128]{1,0:T(8,128)(2,1)S(1)} %add_convert_fusion), channel_id=1, source_target_pairs={{0,192},{2,194},{4,196},{6,198},{8,200},{10,202},{12,204},{14,206}... | collective-permute-start | bytes 98312 | tf_op jit(solution)/shard_map/ppermute | solution.py:316
  75.0 7.3 %collective-permute-start.16 = (f32[128,128]{1,0:T(8,128)S(1)}, f32[128,128]{1,0:T(8,128)S(1)}, u32[]{:S(2)}, u32[]{:S(2)}) collective-permute-start(f32[128,128]{1,0:T(8,128)S(1)} %add_add_fusion), channel_id=1, source_target_pairs={{0,32},{2,34},{4,36},{6,38},{8,40},{10,42},{12,44},{14,46},{16,48}... | collective-permute-start | bytes 196616 | tf_op jit(solution)/shard_map/ppermute | solution.py:316
  79.1 3.2 %collective-permute-start.17 = (f32[128,128]{1,0:T(8,128)S(1)}, f32[128,128]{1,0:T(8,128)S(1)}, u32[]{:S(2)}, u32[]{:S(2)}) collective-permute-start(f32[128,128]{1,0:T(8,128)S(1)} %add_add_fusion), channel_id=1, source_target_pairs={{0,2},{2,0},{4,6},{6,4},{8,10},{10,8},{12,14},{14,12},{16,18},{18,... | collective-permute-start | bytes 196616 | tf_op jit(solution)/shard_map/ppermute | solution.py:316
  79.9 5.2 %collective-permute-start.18 = (f32[128,128]{1,0:T(8,128)S(1)}, f32[128,128]{1,0:T(8,128)S(1)}, u32[]{:S(2)}, u32[]{:S(2)}) collective-permute-start(f32[128,128]{1,0:T(8,128)S(1)} %add_add_fusion), channel_id=1, source_target_pairs={{0,34},{2,32},{4,38},{6,36},{8,42},{10,40},{12,46},{14,44},{16,50}... | collective-permute-start | bytes 196616 | tf_op jit(solution)/shard_map/ppermute | solution.py:316

commit v10 on v9

--- a/solution.py
+++ b/solution.py
@@ -383,9 +383,9 @@
         )
 
     stages = (
-        (((0, 0, 4, 0),), 3),
+        (((1, 0, 0, 0), (2, 0, 0, 0), (3, 0, 0, 0)), 2),
         (((0, 0, 1, 0), (0, 0, 2, 0), (0, 0, 3, 0)), 2),
-        (((1, 0, 0, 0), (2, 0, 0, 0), (3, 0, 0, 0)), 1),
+        (((0, 0, 4, 0),), 2),
     )
     for moves, pieces in stages:
         sent = value.astype(jnp.bfloat16)

time: 86.1 us -> 82.8 us (0.962)
  waiting for transfers between devices: 8.79 us -> 5.3 us
    ppermute x10, waiting for transfers between devices: 6.35 us -> 2.86 us  [along_blk(): return lax.ppermute(value, BLK, pairs)]
  transfers between devices with their start and end apart: 19 -> 19, of which waited for: 5 -> 4; matrix products, arithmetic and copies ran while one was open for 0% -> 0% of each run, Pallas kernels for 43% -> 44%
where the time goes in v10:
time: 82.8 us; the launch traced here: 82.5 us
  Pallas kernels  38.8 us (47%)
  starting transfers between devices  36.7 us (44%)
  waiting for transfers between devices  5.3 us (6%)
  between operations  0.96 us (1%)
    pallas_call x16, Pallas kernels, kernel_call(): pl.pallas_call(body, out_shape=outs, in_specs=[pl.BlockSpec(memory_space=...  38.8 us
    ppermute x10, starting transfers between devices, along_blk(): return lax.ppermute(value, BLK, pairs)  12.8 us
    ppermute x4, starting transfers between devices, core_swap(): return lax.ppermute(value, 'core', [(0, 1), (1, 0)])  11.7 us
    ppermute x2, starting transfers between devices, from_neighbour(): return lax.ppermute(value, BLK, pairs)  9.49 us
    ppermute x10, waiting for transfers between devices, along_blk(): return lax.ppermute(value, BLK, pairs)  2.86 us
    ppermute x1, starting transfers between devices, shards(): crossed = lax.ppermute(value, ('core', 'rhs'), [(2, 3), (3, 2)])  2.23 us
  transfers between devices with their start and end apart: 19, of which 4 were waited for; matrix products, arithmetic and copies ran while one was open for 0% of the time, Pallas kernels for 44%

profile of v10, /device:TPU:1, one launch (start us, length us, event | category | flops | bytes accessed | tf_op | source)
XLA Modules:
  0.0 82.5 jit_solution(10787728797423156025)
XLA Ops:
  0.6 2.1 %pack.1.message_ref = bf16[128,2176]{1,0:T(8,128)(2,1)} custom-call(bf16[2048,128]{1,0:T(8,128)(2,1)} %own_ref.1, bf16[16,128]{1,0:T(8,128)(2,1)} %bitcast.4, bf16[16,128]{1,0:T(8,128)(2,1)} %bitcast.5, bf16[16,128]{1,0:T(8,128)(2,1)} %bitcast.6), custom_call_target="tpu_custom_call" | custom-call | bytes 1048576 | tf_op jit(solution)/shard_map/pack/pallas_call | solution.py:223
  2.8 3.3 %collective-permute-start = (bf16[128,2176]{1,0:T(8,128)(2,1)}, bf16[128,2176]{1,0:T(8,128)(2,1)S(1)}, u32[]{:S(2)}, u32[]{:S(2)}) collective-permute-start(bf16[128,2176]{1,0:T(8,128)(2,1)} %pack.1.message_ref), channel_id=1, source_target_pairs={{0,2},{2,0},{1,3},{3,1},{4,6},{6,4},{5,7},{7,5},{8,10},{10,8},{9,1... | collective-permute-start | bytes 1671176 | tf_op jit(solution)/shard_map/ppermute | solution.py:338
  6.1 9.5 %collective-permute-start.2 = (bf16[128,2176]{1,0:T(8,128)(2,1)}, bf16[128,2176]{1,0:T(8,128)(2,1)}, u32[]{:S(2)}, u32[]{:S(2)}) collective-permute-start(bf16[128,2176]{1,0:T(8,128)(2,1)} %pack.1.message_ref), channel_id=1, source_target_pairs={{0,252},{2,254},{4,10},{6,8},{8,4},{10,6},{12,18},{14,16},{16,12},... | collective-permute-start | bytes 1671176 | tf_op jit(solution)/shard_map/ppermute | solution.py:327
  15.6 5.2 %home_tile.1 = (f32[128,2048]{1,0:T(8,128)S(1)}, bf16[48,2048]{1,0:T(8,128)(2,1)S(1)}) custom-call(bf16[128,2176]{1,0:T(8,128)(2,1)} %pack.1.message_ref), custom_call_target="tpu_custom_call" | custom-call | flops 67108864 | tf_op jit(solution)/shard_map/home_tile/pallas_call | solution.py:223
  21.0 4.1 %guest_tile.4.refs_2_ = f32[128,2048]{1,0:T(8,128)S(1)} custom-call(bf16[48,2048]{1,0:T(8,128)(2,1)S(1)} %get-tuple-element.53.refs_0_.home_ref, bf16[128,2176]{1,0:T(8,128)(2,1)S(1)} %collective-permute-done.refs_1_, f32[128,2048]{1,0:T(8,128)S(1)} %get-tuple-element.55.refs_2_), custom_call_target="tpu_custom_call", output_to_operand_aliasing={{}: (2, {})} | custom-call | flops 67108864 | tf_op jit(solution)/shard_map/guest_tile/pallas_call | solution.py:223
  25.5 1.8 %collective-permute-start.8 = (bf16[128,2176]{1,0:T(8,128)(2,1)}, bf16[128,2176]{1,0:T(8,128)(2,1)S(1)}, u32[]{:S(2)}, u32[]{:S(2)}) collective-permute-start(bf16[128,2176]{1,0:T(8,128)(2,1)} %collective-permute-done.1.refs_1_), channel_id=1, source_target_pairs={{0,2},{2,0},{1,3},{3,1},{4,6},{6,4},{5,7},{7,5},{8,10},{10,8},{9,1... | collective-permute-start | bytes 1671176 | tf_op jit(solution)/shard_map/ppermute | solution.py:338
  27.4 4.9 %guest_tile.5 = (f32[128,2048]{1,0:T(8,128)S(1)}, f32[128,2048]{1,0:T(8,128)S(1)}) custom-call(bf16[48,2048]{1,0:T(8,128)(2,1)S(1)} %get-tuple-element.53.refs_0_.home_ref, bf16[128,2176]{1,0:T(8,128)(2,1)} %collective-permute-done.1.refs_1_, f32[128,2048]{1,0:T(8,128)S(1)} %guest_tile.4.refs_2_), custom_call_target="tpu_custom_call", output_to_operand_aliasing={{1}: (2, {})} | custom-call | flops 67108864 | tf_op jit(solution)/shard_map/guest_tile/pallas_call | solution.py:223
  33.0 4.8 %guest_tile.6 = (f32[128,2048]{1,0:T(8,128)S(1)}, f32[128,2048]{1,0:T(8,128)S(1)}) custom-call(bf16[48,2048]{1,0:T(8,128)(2,1)S(1)} %get-tuple-element.53.refs_0_.home_ref, bf16[128,2176]{1,0:T(8,128)(2,1)} %collective-permute-done.2.refs_1_, f32[128,2048]{1,0:T(8,128)S(1)} %get-tuple-element.61.refs_2_, ...), custom_call_target="tpu_custom_call", output_to_operand_aliasing={{0}: (2, {}), {1}: (3, {})} | custom-call | flops 67108864 | tf_op jit(solution)/shard_map/guest_tile/pallas_call | solution.py:223
  37.9 4.8 %guest_tile.7 = (f32[128,2048]{1,0:T(8,128)S(1)}, f32[128,2048]{1,0:T(8,128)S(1)}) custom-call(bf16[48,2048]{1,0:T(8,128)(2,1)S(1)} %get-tuple-element.53.refs_0_.home_ref, bf16[128,2176]{1,0:T(8,128)(2,1)} %collective-permute-done.5.refs_1_, f32[128,2048]{1,0:T(8,128)S(1)} %get-tuple-element.66.refs_2_, ...), custom_call_target="tpu_custom_call", output_to_operand_aliasing={{0}: (2, {}), {1}: (3, {})} | custom-call | flops 67108864 | tf_op jit(solution)/shard_map/guest_tile/pallas_call | solution.py:223
  42.7 1.7 %half_gram.1 = (f32[128,128]{1,0:T(8,128)S(1)}, f32[128,128]{1,0:T(8,128)S(1)}, f32[128,2048]{1,0:T(8,128)S(1)}) custom-call(s32[1]{0:T(128)} %bitcast.3.core_ref, bf16[2048,128]{1,0:T(8,128)(2,1)} %own_ref.1, bf16[2048,128]{1,0:T(8,128)(2,1)} %collective-permute-done.4.pair_ref, ...), custom_call_target="tpu_custom_call", output_to_operand_aliasing={{2}: (3, {})} | custom-call | flops 67108864 | tf_op jit(solution)/shard_map/half_gram/pallas_call | solution.py:223
  44.4 5.8 %collective-permute-start.6 = (f32[128,128]{1,0:T(8,128)S(1)}, f32[128,128]{1,0:T(8,128)S(1)}, u32[]{:S(2)}, u32[]{:S(2)}) collective-permute-start(f32[128,128]{1,0:T(8,128)S(1)} %get-tuple-element.71), channel_id=1, source_target_pairs={{0,2},{2,0},{1,3},{3,1},{4,6},{6,4},{5,7},{7,5},{8,10},{10,8},{9,1... | collective-permute-start | bytes 196616 | tf_op jit(solution)/shard_map/ppermute | solution.py:338
  51.1 2.2 %collective-permute-start.7 = (f32[128,128]{1,0:T(8,128)S(1)}, f32[128,128]{1,0:T(8,128)S(1)}, u32[]{:S(2)}, u32[]{:S(2)}) collective-permute-start(f32[128,128]{1,0:T(8,128)S(1)} %add.30.value_ref), channel_id=1, source_target_pairs={{2,3},{3,2},{6,7},{7,6},{10,11},{11,10},{14,15},{15,14},{18,19},{1... | collective-permute-start | bytes 196616 | tf_op jit(solution)/shard_map/ppermute | solution.py:375
  53.3 1.2 %piece_tile.8.total_ref = f32[128,2048]{1,0:T(8,128)S(1)} custom-call(bf16[48,2048]{1,0:T(8,128)(2,1)S(1)} %get-tuple-element.53.refs_0_.home_ref, bf16[128,2176]{1,0:T(8,128)(2,1)S(1)} %collective-permute-done.8.message_ref, f32[128,2048]{1,0:T(8,128)S(1)} %get-tuple-element.74.total_ref), custom_call_target="tpu_custom_call", output_to_operand_aliasing={{}: (2, {})} | custom-call | flops 67108864 | tf_op jit(solution)/shard_map/piece_tile/pallas_call | solution.py:223
  54.6 1.5 %collective-permute-done.7.crossed_ref = f32[128,128]{1,0:T(8,128)S(1)} collective-permute-done((f32[128,128]{1,0:T(8,128)S(1)}, f32[128,128]{1,0:T(8,128)S(1)}, u32[]{:S(2)}, u32[]{:S(2)}) %collective-permute-start.7) | collective-permute-done | bytes 65568 | tf_op jit(solution)/shard_map/ppermute | solution.py:375
  56.4 2.5 %collective-permute-start.9 = (bf16[128,128]{1,0:T(8,128)(2,1)S(1)}, bf16[128,128]{1,0:T(8,128)(2,1)S(1)}, u32[]{:S(2)}, u32[]{:S(2)}) collective-permute-start(bf16[128,128]{1,0:T(8,128)(2,1)S(1)} %convert_element_type.39), channel_id=1, source_target_pairs={{0,64},{2,66},{4,68},{6,70},{8,72},{10,74},{12,76},{14,78},{16,80}... | collective-permute-start | bytes 98312 | tf_op jit(solution)/shard_map/ppermute | solution.py:316
  60.2 1.2 %piece_tile.10.total_ref = f32[128,2048]{1,0:T(8,128)S(1)} custom-call(bf16[48,2048]{1,0:T(8,128)(2,1)S(1)} %get-tuple-element.53.refs_0_.home_ref, bf16[128,2176]{1,0:T(8,128)(2,1)S(1)} %collective-permute-done.8.message_ref, f32[128,2048]{1,0:T(8,128)S(1)} %piece_tile.9.total_ref), custom_call_target="tpu_custom_call", output_to_operand_aliasing={{}: (2, {})} | custom-call | flops 67108864 | tf_op jit(solution)/shard_map/piece_tile/pallas_call | solution.py:223
  61.7 3.4 %collective-permute-start.14 = (bf16[128,128]{1,0:T(8,128)(2,1)S(1)}, bf16[128,128]{1,0:T(8,128)(2,1)S(1)}, u32[]{:S(2)}, u32[]{:S(2)}) collective-permute-start(bf16[128,128]{1,0:T(8,128)(2,1)S(1)} %add_convert_fusion.1), channel_id=1, source_target_pairs={{0,12},{2,14},{4,8},{6,10},{8,4},{10,6},{12,0},{14,2},{16,28},{18,... | collective-permute-start | bytes 98312 | tf_op jit(solution)/shard_map/ppermute | solution.py:316
  65.1 1.2 %piece_tile.11.total_ref = f32[128,2048]{1,0:T(8,128)S(1)} custom-call(bf16[48,2048]{1,0:T(8,128)(2,1)S(1)} %get-tuple-element.53.refs_0_.home_ref, bf16[128,2176]{1,0:T(8,128)(2,1)S(1)} %collective-permute-done.8.message_ref, f32[128,2048]{1,0:T(8,128)S(1)} %piece_tile.10.total_ref), custom_call_target="tpu_custom_call", output_to_operand_aliasing={{}: (2, {})} | custom-call | flops 67108864 | tf_op jit(solution)/shard_map/piece_tile/pallas_call | solution.py:223
  66.4 1.2 %piece_tile.12.total_ref = f32[128,2048]{1,0:T(8,128)S(1)} custom-call(bf16[48,2048]{1,0:T(8,128)(2,1)S(1)} %get-tuple-element.53.refs_0_.home_ref, bf16[128,2176]{1,0:T(8,128)(2,1)S(1)} %collective-permute-done.3.message_ref, f32[128,2048]{1,0:T(8,128)S(1)} %piece_tile.11.total_ref), custom_call_target="tpu_custom_call", output_to_operand_aliasing={{}: (2, {})} | custom-call | flops 67108864 | tf_op jit(solution)/shard_map/piece_tile/pallas_call | solution.py:223
  67.7 2.8 %collective-permute-start.15 = (bf16[128,128]{1,0:T(8,128)(2,1)S(1)}, bf16[128,128]{1,0:T(8,128)(2,1)S(1)}, u32[]{:S(2)}, u32[]{:S(2)}) collective-permute-start(bf16[128,128]{1,0:T(8,128)(2,1)S(1)} %add_convert_fusion), channel_id=1, source_target_pairs={{0,16},{2,18},{4,20},{6,22},{8,24},{10,26},{12,28},{14,30},{16,0},... | collective-permute-start | bytes 98312 | tf_op jit(solution)/shard_map/ppermute | solution.py:316
  71.7 1.2 %piece_tile.14.total_ref = f32[128,2048]{1,0:T(8,128)S(1)} custom-call(bf16[48,2048]{1,0:T(8,128)(2,1)S(1)} %get-tuple-element.53.refs_0_.home_ref, bf16[128,2176]{1,0:T(8,128)(2,1)S(1)} %collective-permute-done.3.message_ref, f32[128,2048]{1,0:T(8,128)S(1)} %piece_tile.13.total_ref), custom_call_target="tpu_custom_call", output_to_operand_aliasing={{}: (2, {})} | custom-call | flops 67108864 | tf_op jit(solution)/shard_map/piece_tile/pallas_call | solution.py:223
  73.0 2.0 %collective-permute-done.15 = bf16[128,128]{1,0:T(8,128)(2,1)S(1)} collective-permute-done((bf16[128,128]{1,0:T(8,128)(2,1)S(1)}, bf16[128,128]{1,0:T(8,128)(2,1)S(1)}, u32[]{:S(2)}, u32[]{:S(2)}) %collective-permute-start.15) | collective-permute-done | bytes 32800 | tf_op jit(solution)/shard_map/ppermute | solution.py:316
  75.7 2.9 %collective-permute-start.18 = (f32[128,128]{1,0:T(8,128)S(1)}, f32[128,128]{1,0:T(8,128)S(1)}, u32[]{:S(2)}, u32[]{:S(2)}) collective-permute-start(f32[128,128]{1,0:T(8,128)S(1)} %convert_add_fusion), channel_id=1, source_target_pairs={{0,34},{2,32},{4,38},{6,36},{8,42},{10,40},{12,46},{14,44},{16,50}... | collective-permute-start | bytes 196616 | tf_op jit(solution)/shard_map/ppermute | solution.py:316
  78.6 2.4 %piece_tile.15 = f32[2048,128]{1,0:T(8,128)} custom-call(bf16[48,2048]{1,0:T(8,128)(2,1)S(1)} %get-tuple-element.53.refs_0_.home_ref, bf16[128,2176]{1,0:T(8,128)(2,1)S(1)} %collective-permute-done.3.message_ref, f32[128,2048]{1,0:T(8,128)S(1)} %piece_tile.14.total_ref), custom_call_target="tpu_custom_call" | custom-call | flops 67108864 | tf_op jit(solution)/shard_map/piece_tile/pallas_call | solution.py:223
  (37 shorter events, 7.4 us)
Async XLA Ops:
  2.8 18.2 %collective-permute-start = (bf16[128,2176]{1,0:T(8,128)(2,1)}, bf16[128,2176]{1,0:T(8,128)(2,1)S(1)}, u32[]{:S(2)}, u32[]{:S(2)}) collective-permute-start(bf16[128,2176]{1,0:T(8,128)(2,1)} %pack.1.message_ref), channel_id=1, source_target_pairs={{0,2},{2,0},{1,3},{3,1},{4,6},{6,4},{5,7},{7,5},{8,10},{10,8},{9,1... | collective-permute-start | bytes 1671176 | tf_op jit(solution)/shard_map/ppermute | solution.py:338
  6.1 19.0 %collective-permute-start.1 = (bf16[128,2176]{1,0:T(8,128)(2,1)}, bf16[128,2176]{1,0:T(8,128)(2,1)}, u32[]{:S(2)}, u32[]{:S(2)}) collective-permute-start(bf16[128,2176]{1,0:T(8,128)(2,1)} %pack.1.message_ref), channel_id=1, source_target_pairs={{0,6},{2,4},{4,0},{6,2},{8,14},{10,12},{12,8},{14,10},{16,22},{18,... | collective-permute-start | bytes 1671176 | tf_op jit(solution)/shard_map/ppermute | solution.py:327
  6.1 26.2 %collective-permute-start.2 = (bf16[128,2176]{1,0:T(8,128)(2,1)}, bf16[128,2176]{1,0:T(8,128)(2,1)}, u32[]{:S(2)}, u32[]{:S(2)}) collective-permute-start(bf16[128,2176]{1,0:T(8,128)(2,1)} %pack.1.message_ref), channel_id=1, source_target_pairs={{0,252},{2,254},{4,10},{6,8},{8,4},{10,6},{12,18},{14,16},{16,12},... | collective-permute-start | bytes 1671176 | tf_op jit(solution)/shard_map/ppermute | solution.py:327
  20.8 17.0 %collective-permute-start.5 = (bf16[128,2176]{1,0:T(8,128)(2,1)}, bf16[128,2176]{1,0:T(8,128)(2,1)}, u32[]{:S(2)}, u32[]{:S(2)}) collective-permute-start(bf16[128,2176]{1,0:T(8,128)(2,1)} %pack.1.message_ref), channel_id=1, source_target_pairs={{250,0},{8,2},{254,4},{12,6},{2,8},{16,10},{6,12},{20,14},{10,16},... | collective-permute-start | bytes 1671176 | tf_op jit(solution)/shard_map/ppermute | solution.py:332
  25.1 17.6 %collective-permute-start.4 = (bf16[2048,128]{1,0:T(8,128)(2,1)}, bf16[2048,128]{1,0:T(8,128)(2,1)}, u32[]{:S(2)}, u32[]{:S(2)}) collective-permute-start(bf16[2048,128]{1,0:T(8,128)(2,1)} %own_ref.1), channel_id=1, source_target_pairs={{0,1},{1,0},{2,3},{3,2},{4,5},{5,4},{6,7},{7,6},{8,9},{9,8},{10,11... | collective-permute-start | bytes 1572872 | tf_op jit(solution)/shard_map/ppermute | solution.py:354
  25.5 27.8 %collective-permute-start.8 = (bf16[128,2176]{1,0:T(8,128)(2,1)}, bf16[128,2176]{1,0:T(8,128)(2,1)S(1)}, u32[]{:S(2)}, u32[]{:S(2)}) collective-permute-start(bf16[128,2176]{1,0:T(8,128)(2,1)} %collective-permute-done.1.refs_1_), channel_id=1, source_target_pairs={{0,2},{2,0},{1,3},{3,1},{4,6},{6,4},{5,7},{7,5},{8,10},{10,8},{9,1... | collective-permute-start | bytes 1671176 | tf_op jit(solution)/shard_map/ppermute | solution.py:338
  32.3 34.1 %collective-permute-start.3 = (bf16[128,2176]{1,0:T(8,128)(2,1)}, bf16[128,2176]{1,0:T(8,128)(2,1)S(1)}, u32[]{:S(2)}, u32[]{:S(2)}) collective-permute-start(bf16[128,2176]{1,0:T(8,128)(2,1)} %collective-permute-done.2.refs_1_), channel_id=1, source_target_pairs={{0,2},{2,0},{1,3},{3,1},{4,6},{6,4},{5,7},{7,5},{8,10},{10,8},{9,1... | collective-permute-start | bytes 1671176 | tf_op jit(solution)/shard_map/ppermute | solution.py:338
  44.4 6.7 %collective-permute-start.6 = (f32[128,128]{1,0:T(8,128)S(1)}, f32[128,128]{1,0:T(8,128)S(1)}, u32[]{:S(2)}, u32[]{:S(2)}) collective-permute-start(f32[128,128]{1,0:T(8,128)S(1)} %get-tuple-element.71), channel_id=1, source_target_pairs={{0,2},{2,0},{1,3},{3,1},{4,6},{6,4},{5,7},{7,5},{8,10},{10,8},{9,1... | collective-permute-start | bytes 196616 | tf_op jit(solution)/shard_map/ppermute | solution.py:338
  51.1 5.0 %collective-permute-start.7 = (f32[128,128]{1,0:T(8,128)S(1)}, f32[128,128]{1,0:T(8,128)S(1)}, u32[]{:S(2)}, u32[]{:S(2)}) collective-permute-start(f32[128,128]{1,0:T(8,128)S(1)} %add.30.value_ref), channel_id=1, source_target_pairs={{2,3},{3,2},{6,7},{7,6},{10,11},{11,10},{14,15},{15,14},{18,19},{1... | collective-permute-start | bytes 196616 | tf_op jit(solution)/shard_map/ppermute | solution.py:375
  56.2 5.2 %collective-permute-start.10 = (bf16[128,128]{1,0:T(8,128)(2,1)S(1)}, bf16[128,128]{1,0:T(8,128)(2,1)S(1)}, u32[]{:S(2)}, u32[]{:S(2)}) collective-permute-start(bf16[128,128]{1,0:T(8,128)(2,1)S(1)} %convert_element_type.39), channel_id=1, source_target_pairs={{0,128},{2,130},{4,132},{6,134},{8,136},{10,138},{12,140},{14,142}... | collective-permute-start | bytes 98312 | tf_op jit(solution)/shard_map/ppermute | solution.py:316
  56.3 5.1 %collective-permute-start.11 = (bf16[128,128]{1,0:T(8,128)(2,1)S(1)}, bf16[128,128]{1,0:T(8,128)(2,1)S(1)}, u32[]{:S(2)}, u32[]{:S(2)}) collective-permute-start(bf16[128,128]{1,0:T(8,128)(2,1)S(1)} %convert_element_type.39), channel_id=1, source_target_pairs={{0,192},{2,194},{4,196},{6,198},{8,200},{10,202},{12,204},{14,206}... | collective-permute-start | bytes 98312 | tf_op jit(solution)/shard_map/ppermute | solution.py:316
  56.4 5.0 %collective-permute-start.9 = (bf16[128,128]{1,0:T(8,128)(2,1)S(1)}, bf16[128,128]{1,0:T(8,128)(2,1)S(1)}, u32[]{:S(2)}, u32[]{:S(2)}) collective-permute-start(bf16[128,128]{1,0:T(8,128)(2,1)S(1)} %convert_element_type.39), channel_id=1, source_target_pairs={{0,64},{2,66},{4,68},{6,70},{8,72},{10,74},{12,76},{14,78},{16,80}... | collective-permute-start | bytes 98312 | tf_op jit(solution)/shard_map/ppermute | solution.py:316
  61.5 6.1 %collective-permute-start.12 = (bf16[128,128]{1,0:T(8,128)(2,1)S(1)}, bf16[128,128]{1,0:T(8,128)(2,1)S(1)}, u32[]{:S(2)}, u32[]{:S(2)}) collective-permute-start(bf16[128,128]{1,0:T(8,128)(2,1)S(1)} %add_convert_fusion.1), channel_id=1, source_target_pairs={{0,4},{2,6},{4,0},{6,2},{8,12},{10,14},{12,8},{14,10},{16,20},{18,... | collective-permute-start | bytes 98312 | tf_op jit(solution)/shard_map/ppermute | solution.py:316
  61.6 6.0 %collective-permute-start.13 = (bf16[128,128]{1,0:T(8,128)(2,1)S(1)}, bf16[128,128]{1,0:T(8,128)(2,1)S(1)}, u32[]{:S(2)}, u32[]{:S(2)}) collective-permute-start(bf16[128,128]{1,0:T(8,128)(2,1)S(1)} %add_convert_fusion.1), channel_id=1, source_target_pairs={{0,8},{2,10},{4,12},{6,14},{8,0},{10,2},{12,4},{14,6},{16,24},{18,... | collective-permute-start | bytes 98312 | tf_op jit(solution)/shard_map/ppermute | solution.py:316
  61.7 5.9 %collective-permute-start.14 = (bf16[128,128]{1,0:T(8,128)(2,1)S(1)}, bf16[128,128]{1,0:T(8,128)(2,1)S(1)}, u32[]{:S(2)}, u32[]{:S(2)}) collective-permute-start(bf16[128,128]{1,0:T(8,128)(2,1)S(1)} %add_convert_fusion.1), channel_id=1, source_target_pairs={{0,12},{2,14},{4,8},{6,10},{8,4},{10,6},{12,0},{14,2},{16,28},{18,... | collective-permute-start | bytes 98312 | tf_op jit(solution)/shard_map/ppermute | solution.py:316
  67.7 7.3 %collective-permute-start.15 = (bf16[128,128]{1,0:T(8,128)(2,1)S(1)}, bf16[128,128]{1,0:T(8,128)(2,1)S(1)}, u32[]{:S(2)}, u32[]{:S(2)}) collective-permute-start(bf16[128,128]{1,0:T(8,128)(2,1)S(1)} %add_convert_fusion), channel_id=1, source_target_pairs={{0,16},{2,18},{4,20},{6,22},{8,24},{10,26},{12,28},{14,30},{16,0},... | collective-permute-start | bytes 98312 | tf_op jit(solution)/shard_map/ppermute | solution.py:316
  75.0 6.0 %collective-permute-start.16 = (f32[128,128]{1,0:T(8,128)S(1)}, f32[128,128]{1,0:T(8,128)S(1)}, u32[]{:S(2)}, u32[]{:S(2)}) collective-permute-start(f32[128,128]{1,0:T(8,128)S(1)} %convert_add_fusion), channel_id=1, source_target_pairs={{0,32},{2,34},{4,36},{6,38},{8,40},{10,42},{12,44},{14,46},{16,48}... | collective-permute-start | bytes 196616 | tf_op jit(solution)/shard_map/ppermute | solution.py:316
  75.3 5.8 %collective-permute-start.17 = (f32[128,128]{1,0:T(8,128)S(1)}, f32[128,128]{1,0:T(8,128)S(1)}, u32[]{:S(2)}, u32[]{:S(2)}) collective-permute-start(f32[128,128]{1,0:T(8,128)S(1)} %convert_add_fusion), channel_id=1, source_target_pairs={{0,2},{2,0},{4,6},{6,4},{8,10},{10,8},{12,14},{14,12},{16,18},{18,... | collective-permute-start | bytes 196616 | tf_op jit(solution)/shard_map/ppermute | solution.py:316
  75.7 6.1 %collective-permute-start.18 = (f32[128,128]{1,0:T(8,128)S(1)}, f32[128,128]{1,0:T(8,128)S(1)}, u32[]{:S(2)}, u32[]{:S(2)}) collective-permute-start(f32[128,128]{1,0:T(8,128)S(1)} %convert_add_fusion), channel_id=1, source_target_pairs={{0,34},{2,32},{4,38},{6,36},{8,42},{10,40},{12,46},{14,44},{16,50}... | collective-permute-start | bytes 196616 | tf_op jit(solution)/shard_map/ppermute | solution.py:316
